TPU v7x, 32 devices: a whole 2x2x4 slice. The times are simulated.
32 devices in a mesh: section: 4 (over y, x), expert: 8 (over z, core).
Axes of the slice: x: 2, y: 2, z: 4, core: 2. Of those that a mesh axis runs over, the one named last changes fastest.
Arguments:
- saved_input: bfloat16 [4, 1024, 2048], P('section', 'expert'), may hold values from -6 to 6
- upstream: bfloat16 [4, 1024, 2048], P('section', 'expert'), may hold values from -6 to 6
- norm_gain: float32 [4, 2048], P('section'), may hold values from 0.1 to 1.9
- gate_weight: bfloat16 [4, 8, 2048, 768], P('section', 'expert'), may hold values from -0.125 to 0.125
- up_weight: bfloat16 [4, 8, 2048, 768], P('section', 'expert'), may hold values from -0.125 to 0.125
- down_weight: bfloat16 [4, 8, 768, 2048], P('section', 'expert'), may hold values from -0.21875 to 0.21875
- expert_ids: int32 [4, 1024, 4], P('section', 'expert'), may hold values from 0 to 7, all different within a row; in each aligned block of 128 rows (0 to 127, 128 to 255, ..., all dimensions but the last counted through in order) at most 96 rows name the same one
- gate_share: float32 [4, 1024, 4], P('section', 'expert'), may hold values from 0.05 to 1
Outputs:
- passed_grad: bfloat16 [4, 1024, 2048], P('section', 'expert')
Inputs may be any that keep to these rules, and one draw needn't show every extreme that they name: `expert_ids`: among the 128 tokens of one index of expert in one layer, every expert is named by at most 96 of the pairs (token, k), a bound that some block reaches; a token names 4 different experts.
All inputs are finite; a program needn't handle non-finite values.
Results may differ from a plain program's by a relative error of at most 0.0063.
Values may be sent and summed in bfloat16 or wider, within the bound.
No kernel may reach another device: no remote copies, remote signals or barrier semaphores. Data moves between devices by JAX's collectives and lax.ppermute only.
A program may use at most 128 MiB of HBM per device.

v0:
```python
import jax
import jax.numpy as jnp
from jax import lax
from jax.sharding import PartitionSpec as P

epsilon = 1e-06


def shifted(value, axis, by):
    length = lax.axis_size(axis)
    return lax.ppermute(value, axis, [(i, (i + by) % length) for i in range(length)])


def slot_ranks(flat_ids, experts):
    pairs = flat_ids.shape[0]
    onehot = (flat_ids[:, None] == jnp.arange(experts, dtype=jnp.int32)[None, :]).astype(
        jnp.bfloat16
    )
    row_index = jnp.arange(pairs, dtype=jnp.int32)
    lower = (row_index[None, :] < row_index[:, None]).astype(jnp.bfloat16)
    before = jnp.dot(lower, onehot, preferred_element_type=jnp.float32)
    ranks = jnp.sum(before * onehot.astype(jnp.float32), axis=1)
    return ranks.astype(jnp.int32)


def expert_backward(inputs, grads, gate_w, up_w, down_w):
    pre_gate = jnp.dot(inputs, gate_w, preferred_element_type=jnp.float32)
    pre_up = jnp.dot(inputs, up_w, preferred_element_type=jnp.float32)
    sigmoid_gate = jax.nn.sigmoid(pre_gate)
    hidden_grad = lax.dot_general(
        grads, down_w, (((1,), (1,)), ((), ())), preferred_element_type=jnp.float32
    )
    d_gate = (hidden_grad * pre_up * sigmoid_gate * (1.0 + pre_gate * (1.0 - sigmoid_gate))).astype(
        jnp.bfloat16
    )
    d_up = (hidden_grad * pre_gate * sigmoid_gate).astype(jnp.bfloat16)
    summed = lax.dot_general(
        d_gate, gate_w, (((1,), (1,)), ((), ())), preferred_element_type=jnp.float32
    )
    summed = summed + lax.dot_general(
        d_up, up_w, (((1,), (1,)), ((), ())), preferred_element_type=jnp.float32
    )
    return summed.astype(jnp.bfloat16)


def per_device(
    saved_input, upstream, norm_gain, gate_weight, up_weight, down_weight, expert_ids, gate_share
):
    saved_rows = saved_input[0]
    upstream_rows = upstream[0]
    gain_row = norm_gain[0]
    gate_w = gate_weight[0, 0]
    up_w = up_weight[0, 0]
    down_w = down_weight[0, 0]
    routed = expert_ids[0]
    shares = gate_share[0]
    tok_rows, top_count = routed.shape
    model_width = saved_rows.shape[1]
    experts = lax.axis_size("expert")
    capacity = max(2, 3 * tok_rows * top_count // (2 * experts))
    inputs_f = saved_rows.astype(jnp.float32)
    inv_root = lax.rsqrt(jnp.mean(inputs_f * inputs_f, axis=1, keepdims=True) + epsilon)
    unit_rows = inputs_f * inv_root
    normed = (unit_rows * gain_row[None, :]).astype(jnp.bfloat16)
    flat_ids = routed.reshape(-1)
    slot_rank = slot_ranks(flat_ids, experts)
    slot_number = (flat_ids * capacity + slot_rank).reshape(tok_rows, top_count)
    slot_index = jnp.arange(experts * capacity, dtype=jnp.int32)
    matches = slot_number[None, :, :] == slot_index[:, None, None]
    select = jnp.any(matches, axis=2).astype(jnp.bfloat16)
    slot_share = jnp.sum(jnp.where(matches, shares[None, :, :], 0.0), axis=(1, 2))
    send_inputs = jnp.dot(select, normed, preferred_element_type=jnp.float32).astype(jnp.bfloat16)
    send_inputs = send_inputs.reshape(experts, capacity, model_width)
    copied_grads = jnp.dot(select, upstream_rows, preferred_element_type=jnp.float32)
    send_grads = (
        (copied_grads * slot_share[:, None])
        .astype(jnp.bfloat16)
        .reshape(experts, capacity, model_width)
    )
    got_inputs, got_grads = (
        lax.all_to_all(send_inputs, "expert", split_axis=0, concat_axis=0, tiled=True),
        lax.all_to_all(send_grads, "expert", split_axis=0, concat_axis=0, tiled=True),
    )
    slot_count = got_inputs.shape[1]
    result_rows = expert_backward(
        got_inputs.reshape(-1, model_width),
        got_grads.reshape(-1, model_width),
        gate_w,
        up_w,
        down_w,
    )
    returned = lax.all_to_all(
        result_rows.reshape(experts, slot_count, model_width),
        "expert",
        split_axis=0,
        concat_axis=0,
        tiled=True,
    )
    normed_grad = lax.dot_general(
        select,
        returned.reshape(experts * capacity, model_width),
        (((0,), (0,)), ((), ())),
        preferred_element_type=jnp.float32,
    )
    scaled = normed_grad * gain_row[None, :]
    layer_grad = upstream_rows.astype(jnp.float32) + inv_root * (
        scaled - unit_rows * jnp.mean(scaled * unit_rows, axis=1, keepdims=True)
    )
    layer_grad = layer_grad.astype(jnp.bfloat16)
    passed = shifted(layer_grad, "section", -1)
    return passed[None]


def solution(mesh):
    placed = (
        P("section", "expert", None),
        P("section", "expert", None),
        P("section", None),
        P("section", "expert", None, None),
        P("section", "expert", None, None),
        P("section", "expert", None, None),
        P("section", "expert", None),
        P("section", "expert", None),
    )
    return jax.shard_map(
        per_device,
        mesh=mesh,
        in_specs=placed,
        out_specs=P("section", "expert", None),
        check_vma=False,
    )
```

profile of v0, /device:TPU:8, one launch (start us, length us, event | category | flops | bytes accessed | tf_op | source)
XLA Modules:
  0.0 273.4 jit_solution(6050806517076637573)
XLA Ops:
  0.0 0.0 copy-start
  0.0 0.9 copy.19
  0.9 0.1 eq.30
  1.0 0.3 fusion.16
  1.3 0.1 convert_element_type.57
  1.4 0.1 copy.20
  1.5 0.7 add_bitcast_fusion
  2.2 0.2 fusion.11
  2.4 0.9 select_reduce_fusion
  3.4 3.7 %multiply_convert_fusion = bf16[768,2048]{1,0:T(8,128)(2,1)} fusion(pred[768,128]{1,0:T(8,128)(4,1)S(1)} %fusion.11, f32[768]{0:T(1024)S(1)} %select_reduce_fusion, bf16[1,128,2048]{2,1,0:T(8,128)(2,1)} %param.9), kind=kOutput, calls=%fused_computation.1 | convolution fusion | flops 405798912 | bytes 3771392 | tf_op jit(solution)/shard_map/dot_general | solution.py:74
  7.1 0.0 copy-start.3
  7.1 5.5 %all-to-all-start = ((bf16[8,96,2048]{2,1,0:T(8,128)(2,1)}), bf16[8,96,2048]{2,1,0:T(8,128)(2,1)}, u32[]{:S(2)}, u32[]{:S(2)}) async-start(bf16[8,96,2048]{2,1,0:T(8,128)(2,1)} %bitcast.49), calls=%async_computation | async-start | bytes 6291456 | tf_op jit(solution)/shard_map/all_to_all | solution.py:82
  12.5 1.2 fusion.23
  13.8 0.0 copy-done.3
  13.8 3.8 %convolution_convert_fusion = bf16[768,2048]{1,0:T(8,128)(2,1)} fusion(pred[768,128]{1,0:T(8,128)(4,1)S(1)} %fusion.11, bf16[1,128,2048]{2,1,0:T(8,128)(2,1)} %param.8, f32[2048]{0:T(1024)S(1)} %bitcast.53, f32[128]{0:T(128)S(1)} %add_rsqrt_fusion), kind=kOutput, calls=%fused_computation.2 | convolution fusion | flops 405274624 | bytes 3777024 | tf_op jit(solution)/shard_map/dot_general | solution.py:72
  17.6 63.0 %all-to-all-done = bf16[8,96,2048]{2,1,0:T(8,128)(2,1)} async-done(((bf16[8,96,2048]{2,1,0:T(8,128)(2,1)}), bf16[8,96,2048]{2,1,0:T(8,128)(2,1)}, u32[]{:S(2)}, u32[]{:S(2)}) %all-to-all-start) | async-done | bytes 3145760 | tf_op jit(solution)/shard_map/all_to_all | solution.py:82
  80.6 7.9 %all-to-all-start.1 = ((bf16[8,96,2048]{2,1,0:T(8,128)(2,1)}), bf16[8,96,2048]{2,1,0:T(8,128)(2,1)}, u32[]{:S(2)}, u32[]{:S(2)}) async-start(bf16[8,96,2048]{2,1,0:T(8,128)(2,1)} %bitcast.48), calls=%async_computation.1 | async-start | bytes 6291456 | tf_op jit(solution)/shard_map/all_to_all | solution.py:81
  88.5 6.9 %fusion.7 = f32[768,768]{1,0:T(8,128)} fusion(bf16[768,2048]{1,0:T(8,128)(2,1)} %bitcast.5, bf16[1,1,768,2048]{3,2,1,0:T(8,128)(2,1)} %param.13), kind=kOutput, calls=%fused_computation.10 | convolution fusion | flops 2415919104 | bytes 8650752 | tf_op jit(solution)/shard_map/dot_general | solution.py:30
  95.4 61.2 %all-to-all-done.1 = bf16[8,96,2048]{2,1,0:T(8,128)(2,1)} async-done(((bf16[8,96,2048]{2,1,0:T(8,128)(2,1)}), bf16[8,96,2048]{2,1,0:T(8,128)(2,1)}, u32[]{:S(2)}, u32[]{:S(2)}) %all-to-all-start.1) | async-done | bytes 3145760 | tf_op jit(solution)/shard_map/all_to_all | solution.py:81
  156.6 6.9 %fusion.2 = f32[768,768]{1,0:T(8,128)} fusion(bf16[768,2048]{1,0:T(8,128)(2,1)} %bitcast.10, bf16[1,1,2048,768]{3,2,1,0:T(8,128)(2,1)} %param.11), kind=kOutput, calls=%fused_computation.5 | convolution fusion | flops 2415919104 | bytes 8650752 | tf_op jit(solution)/shard_map/dot_general | solution.py:27
  163.5 0.0 copy-done
  163.5 12.7 %fusion = f32[768,2048]{1,0:T(8,128)} fusion(bf16[1,1,2048,768]{3,2,1,0:T(8,128)(2,1)} %param.11, f32[768,768]{1,0:T(8,128)} %fusion.2, f32[768,768]{1,0:T(8,128)} %fusion.7, bf16[768,2048]{1,0:T(8,128)(2,1)} %bitcast.10, bf16[1,1,2048,768]{3,2,1,0:T(8,128)(2,1)S(1)} %copy-done), kind=kOutput, calls=%fused_computation.3 | convolution fusion | flops 4837736448 | bytes 20447232 | tf_op jit(solution)/shard_map/dot_general | solution.py:37
  176.3 6.2 %add_convert_fusion = bf16[768,2048]{1,0:T(8,128)(2,1)S(1)} fusion(f32[768,2048]{1,0:T(8,128)} %fusion, bf16[1,1,2048,768]{3,2,1,0:T(8,128)(2,1)S(1)} %copy-done, f32[768,768]{1,0:T(8,128)} %fusion.7, f32[768,768]{1,0:T(8,128)} %fusion.2), kind=kOutput, calls=%fused_computation | convolution fusion | flops 2422603776 | bytes 17301504 | tf_op jit(solution)/shard_map/dot_general | solution.py:40
  182.5 0.0 copy-start.1
  182.5 75.3 %all_to_all.15 = bf16[8,96,2048]{2,1,0:T(8,128)(2,1)S(1)} all-to-all(bf16[8,96,2048]{2,1,0:T(8,128)(2,1)S(1)} %bitcast.51), channel_id=1, replica_groups=mesh['section'=4,'expert'=8] {'expert'}, dimensions={0} | all-to-all | bytes 6291456 | tf_op jit(solution)/shard_map/all_to_all | solution.py:92
  257.9 0.0 copy-start.2
  257.9 0.0 copy-done.1
  257.9 0.8 fusion.18
  258.6 0.3 copy-done.2
  258.9 0.4 fusion.22
  259.3 2.5 collective-permute-start
  261.8 10.8 %collective-permute-done = bf16[128,2048]{1,0:T(8,128)(2,1)S(1)} collective-permute-done((bf16[128,2048]{1,0:T(8,128)(2,1)S(1)}, bf16[128,2048]{1,0:T(8,128)(2,1)S(1)}, u32[]{:S(2)}, u32[]{:S(2)}) %collective-permute-start) | collective-permute-done | bytes 524320 | tf_op jit(solution)/shard_map/ppermute | solution.py:11
  272.6 0.8 copy.22
  (3 shorter events, 0.0 us)
Async XLA Ops:
  0.0 163.5 %copy-start = (bf16[1,1,2048,768]{3,2,1,0:T(8,128)(2,1)S(1)}, bf16[1,1,2048,768]{3,2,1,0:T(8,128)(2,1)}, u32[]{:S(2)}) copy-start(bf16[1,1,2048,768]{3,2,1,0:T(8,128)(2,1)} %param.12) | copy-start | bytes 9437188
  7.1 6.7 %copy-start.3 = (f32[1,2048]{1,0:T(1,128)S(1)}, f32[1,2048]{1,0:T(1,128)}, u32[]{:S(2)}) copy-start(f32[1,2048]{1,0:T(1,128)} %param.10) | copy-start | bytes 24580
  7.1 73.5 %all-to-all-start = ((bf16[8,96,2048]{2,1,0:T(8,128)(2,1)}), bf16[8,96,2048]{2,1,0:T(8,128)(2,1)}, u32[]{:S(2)}, u32[]{:S(2)}) async-start(bf16[8,96,2048]{2,1,0:T(8,128)(2,1)} %bitcast.49), calls=%async_computation | async-start | bytes 6291456 | tf_op jit(solution)/shard_map/all_to_all | solution.py:82
  80.6 76.0 %all-to-all-start.1 = ((bf16[8,96,2048]{2,1,0:T(8,128)(2,1)}), bf16[8,96,2048]{2,1,0:T(8,128)(2,1)}, u32[]{:S(2)}, u32[]{:S(2)}) async-start(bf16[8,96,2048]{2,1,0:T(8,128)(2,1)} %bitcast.48), calls=%async_computation.1 | async-start | bytes 6291456 | tf_op jit(solution)/shard_map/all_to_all | solution.py:81
  182.5 75.3 %copy-start.1 = (bf16[1,128,2048]{2,1,0:T(8,128)(2,1)S(1)}, bf16[1,128,2048]{2,1,0:T(8,128)(2,1)}, u32[]{:S(2)}) copy-start(bf16[1,128,2048]{2,1,0:T(8,128)(2,1)} %param.8) | copy-start | bytes 1572868
  257.9 1.0 copy-start.2
  259.3 13.3 %collective-permute-start = (bf16[128,2048]{1,0:T(8,128)(2,1)S(1)}, bf16[128,2048]{1,0:T(8,128)(2,1)S(1)}, u32[]{:S(2)}, u32[]{:S(2)}) collective-permute-start(bf16[128,2048]{1,0:T(8,128)(2,1)S(1)} %fusion.22), channel_id=1, source_target_pairs={{0,24},{8,0},{16,8},{24,16},{1,25},{9,1},{17,9},{25,17},{2,26},{10... | collective-permute-start | bytes 1572872 | tf_op jit(solution)/shard_map/ppermute | solution.py:11
where the time goes:
time: 277 us; the launch traced here: 273 us
  waiting for transfers between devices  135 us (49%)
  blocking collectives  75.3 us (27%)
  matrix products  41.3 us (15%)
  starting transfers between devices  15.9 us (6%)
  other arithmetic  3.47 us (1%)
    all_to_all x1, blocking collectives, per_device(): lax.all_to_all(result_rows.reshape(experts, slot_count, model_width), 'ex...  75.3 us
    all_to_all x1, waiting for transfers between devices, per_device(): lax.all_to_all(send_grads, 'expert', split_axis=0, concat_axis=0, tiled=T...  63 us
    all_to_all x1, waiting for transfers between devices, per_device(): lax.all_to_all(send_inputs, 'expert', split_axis=0, concat_axis=0, tiled=...  61.2 us
    dot_general x1, matrix products, expert_backward(): lax.dot_general(d_gate, gate_w, (((1,), (1,)), ((), ())), preferred_eleme...  12.7 us
    ppermute x1, waiting for transfers between devices, shifted(): lax.ppermute(value, axis, [(i, (i + by) % length) for i in range(length)])  10.8 us
    all_to_all x1, starting transfers between devices, per_device(): lax.all_to_all(send_inputs, 'expert', split_axis=0, concat_axis=0, tiled=...  7.94 us
    dot_general x1, matrix products, expert_backward(): pre_gate = jnp.dot(inputs, gate_w, preferred_element_type=jnp.float32)  6.95 us
    dot_general x1, matrix products, expert_backward(): lax.dot_general(grads, down_w, (((1,), (1,)), ((), ())), preferred_elemen...  6.88 us
  transfers between devices with their start and end apart: 3, of which 3 were waited for; matrix products, arithmetic and copies ran while one was open for 4% of the time, Pallas kernels for 0%

commit v1 on v0

--- a/solution.py
+++ b/solution.py
@@ -1,9 +1,13 @@
+import functools
 import jax
 import jax.numpy as jnp
 from jax import lax
+from jax.experimental import pallas as pl
+from jax.experimental.pallas import tpu as pltpu
 from jax.sharding import PartitionSpec as P
 
 epsilon = 1e-06
+chunks = 2
 
 
 def shifted(value, axis, by):
@@ -43,7 +47,7 @@
     return summed.astype(jnp.bfloat16)
 
 
-def per_device(
+def routed_device(
     saved_input, upstream, norm_gain, gate_weight, up_weight, down_weight, expert_ids, gate_share
 ):
     saved_rows = saved_input[0]
@@ -111,6 +115,235 @@
     return passed[None]
 
 
+in_vmem = pl.BlockSpec(memory_space=pltpu.VMEM)
+in_smem = pl.BlockSpec(memory_space=pltpu.SMEM)
+anywhere = pl.BlockSpec(memory_space=pl.ANY)
+
+
+def prep_kernel(experts, saved_ref, upstream_ref, gain_ref, ids_ref, share_ref, *out_refs):
+    root_ref, row_refs = out_refs[0], out_refs[1:]
+    size, width = row_refs[0].shape[0], saved_ref.shape[1]
+    lanes = row_refs[0].shape[1] - 2 * width
+    for c, ref in enumerate(row_refs):
+        cut = pl.ds(c * size, size)
+        value = saved_ref[cut, :].astype(jnp.float32)
+        mean = jnp.mean(value * value, axis=1, keepdims=True)
+        inv_root = lax.rsqrt(mean + epsilon)
+        root_ref[cut, :] = inv_root
+        ref[:, :width] = (value * inv_root * gain_ref[...]).astype(jnp.bfloat16)
+        ref[:, width : 2 * width] = upstream_ref[cut, :]
+        lane = lax.broadcasted_iota(jnp.int32, (size, lanes), 1)
+        dense = jnp.zeros((size, lanes), jnp.float32)
+        for k in range(ids_ref.shape[1]):
+            hit = lax.rem(lane, experts) == ids_ref[cut, k : k + 1]
+            dense = dense + jnp.where(hit, share_ref[cut, k : k + 1], 0.0)
+        high = dense.astype(jnp.bfloat16).astype(jnp.float32)
+        middle = (dense - high).astype(jnp.bfloat16).astype(jnp.float32)
+        low = dense - high - middle
+        parts = jnp.where(lane < experts, high, jnp.where(lane < 2 * experts, middle, low))
+        ref[:, 2 * width :] = jnp.where(lane < 3 * experts, parts, 0.0).astype(jnp.bfloat16)
+
+
+def prep(saved_rows, upstream_rows, gain_row, routed, shares, experts):
+    count, width = saved_rows.shape
+    lanes = 128
+    block = jax.ShapeDtypeStruct((count // chunks, 2 * width + lanes), jnp.bfloat16)
+    return pl.pallas_call(
+        functools.partial(prep_kernel, experts),
+        in_specs=[in_vmem] * 5,
+        out_specs=[in_vmem] * (1 + chunks),
+        out_shape=[jax.ShapeDtypeStruct((count, 1), jnp.float32)] + [block] * chunks,
+        compiler_params=pltpu.CompilerParams(vmem_limit_bytes=24 << 20),
+    )(saved_rows, upstream_rows, gain_row, routed, shares)
+
+
+def slot_kernel(experts, picked, named_ref, *refs):
+    count = 4 if picked else 2
+    block_refs, weight_refs = refs[:count], refs[count : count + 6]
+    out_refs = refs[-6:-4]
+    rows_ref, gate_grads, up_grads, share_ref = refs[-4:]
+    size = block_refs[0].shape[0]
+    width = out_refs[0].shape[1]
+    hidden = weight_refs[0].shape[1]
+    tile = 256
+    last = (((1,), (1,)), ((), ()))
+    if picked:
+
+        @pl.when(named_ref[2] == 1)
+        def _():
+            rows_ref[:size, :] = block_refs[0][...]
+            rows_ref[size:, :] = block_refs[2][...]
+
+        @pl.when(named_ref[2] == 0)
+        def _():
+            rows_ref[:size, :] = block_refs[1][...]
+            rows_ref[size:, :] = block_refs[3][...]
+    else:
+        rows_ref[:size, :] = block_refs[0][...]
+        rows_ref[size:, :] = block_refs[1][...]
+    parts = rows_ref[:, 2 * width :].astype(jnp.float32)
+    lane = lax.broadcasted_iota(jnp.int32, parts.shape, 1)
+    for w in range(2):
+        wanted = (lax.rem(lane, experts) == named_ref[w]) & (lane < 3 * experts)
+        share_ref[w] = jnp.sum(jnp.where(wanted, parts, 0.0), axis=1, keepdims=True)
+    for w in range(2):
+        gate_ref, up_ref, down_ref = weight_refs[3 * w : 3 * w + 3]
+
+        def grads_of(step, carry):
+            cut = pl.ds(pl.multiple_of(step * tile, tile), tile)
+            inputs = rows_ref[:, :width]
+            pre_gate = jnp.dot(inputs, gate_ref[:, cut], preferred_element_type=jnp.float32)
+            pre_up = jnp.dot(inputs, up_ref[:, cut], preferred_element_type=jnp.float32)
+            grad = lax.dot_general(
+                rows_ref[:, width : 2 * width],
+                down_ref[cut, :],
+                last,
+                preferred_element_type=jnp.float32,
+            )
+            grad = grad * share_ref[w]
+            sigmoid_gate = jax.nn.sigmoid(pre_gate)
+            scaled = grad * sigmoid_gate
+            d_gate = scaled * pre_up * (1.0 + pre_gate * (1.0 - sigmoid_gate))
+            gate_grads[w, :, cut] = d_gate.astype(jnp.bfloat16)
+            up_grads[w, :, cut] = (scaled * pre_gate).astype(jnp.bfloat16)
+            return carry
+
+        lax.fori_loop(0, hidden // tile, grads_of, 0)
+
+    def pieces_of(step, carry):
+        cut = pl.ds(pl.multiple_of(step * tile, tile), tile)
+        total = None
+        for w in range(2):
+            for held, weight_ref in ((gate_grads, weight_refs[3 * w]), (up_grads, weight_refs[3 * w + 1])):
+                part = lax.dot_general(
+                    held[w], weight_ref[cut, :], last, preferred_element_type=jnp.float32
+                )
+                total = part if total is None else total + part
+        out_refs[0][:, cut] = total[:size].astype(out_refs[0].dtype)
+        out_refs[1][:, cut] = total[size:].astype(out_refs[1].dtype)
+        return carry
+
+    lax.fori_loop(0, width // tile, pieces_of, 0)
+
+
+def slot_pieces(named, blocks, own, other, after, experts, width, kinds):
+    size = blocks[0].shape[0]
+    hidden = own[0].shape[1]
+    rows = 2 * size
+    return pl.pallas_call(
+        functools.partial(slot_kernel, experts, len(blocks) == 4),
+        in_specs=[in_smem] + [in_vmem] * (len(blocks) + 6) + [anywhere] * len(after),
+        out_specs=[in_vmem] * 2,
+        out_shape=[jax.ShapeDtypeStruct((size, width), kind) for kind in kinds],
+        scratch_shapes=[
+            pltpu.VMEM((rows, blocks[0].shape[1]), jnp.bfloat16),
+            pltpu.VMEM((2, rows, hidden), jnp.bfloat16),
+            pltpu.VMEM((2, rows, hidden), jnp.bfloat16),
+            pltpu.VMEM((2, rows, 1), jnp.float32),
+        ],
+        cost_estimate=pl.CostEstimate(
+            flops=20 * rows * width * hidden,
+            bytes_accessed=12 * width * hidden + 8 * rows * width,
+            transcendentals=2 * rows * hidden,
+        ),
+        compiler_params=pltpu.CompilerParams(vmem_limit_bytes=48 << 20),
+    )(named, *blocks, *own, *other, *after)
+
+
+def final_kernel(first, saved_ref, upstream_ref, gain_ref, root_ref, here_ref, second_ref, last_ref, out_ref):
+    cut = pl.ds(first, out_ref.shape[0])
+    inv_root = root_ref[cut, :]
+    normed_grad = here_ref[...] + second_ref[...].astype(jnp.float32)
+    normed_grad = normed_grad + last_ref[...].astype(jnp.float32)
+    scaled = normed_grad * gain_ref[...]
+    unit = saved_ref[cut, :].astype(jnp.float32) * inv_root
+    mean = jnp.mean(scaled * unit, axis=1, keepdims=True)
+    layer_grad = upstream_ref[cut, :].astype(jnp.float32) + inv_root * (scaled - unit * mean)
+    out_ref[...] = layer_grad.astype(jnp.bfloat16)
+
+
+def finish(first, saved_rows, upstream_rows, gain_row, inv_root, here, second, last):
+    return pl.pallas_call(
+        functools.partial(final_kernel, first),
+        in_specs=[in_vmem] * 7,
+        out_specs=in_vmem,
+        out_shape=jax.ShapeDtypeStruct(here.shape, jnp.bfloat16),
+        compiler_params=pltpu.CompilerParams(vmem_limit_bytes=24 << 20),
+    )(saved_rows, upstream_rows, gain_row, inv_root, here, second, last)
+
+
+def line_device(
+    saved_input, upstream, norm_gain, gate_weight, up_weight, down_weight, expert_ids, gate_share
+):
+    own = (gate_weight[0, 0], up_weight[0, 0], down_weight[0, 0])
+    saved_rows, upstream_rows = saved_input[0], upstream[0]
+    tok_rows, width = upstream_rows.shape
+    experts = lax.axis_size("expert")
+    me = lax.axis_index("expert")
+    is_end = (me // 2 == 0) | (me // 2 == experts // 2 - 1)
+    named = jnp.stack([me, me ^ 1, is_end.astype(jnp.int32)]).astype(jnp.int32)
+
+    def along(pairs):
+        cores = [(2 * a + h, 2 * b + h) for a, b in pairs for h in range(2)]
+        return lambda value: lax.ppermute(value, "expert", cores)
+
+    pair_hop = along([(0, 1), (1, 0), (2, 3), (3, 2)])
+    middle_hop = along([(1, 2), (2, 1)])
+    outward_hop = along([(1, 0), (2, 3)])
+    inward_hop = along([(0, 1), (3, 2)])
+    narrow = lambda value: value.astype(jnp.bfloat16)
+    wide = lambda value: value.astype(jnp.float32)
+
+    inv_root, *blocks = prep(
+        saved_rows, upstream_rows, norm_gain, expert_ids[0], gate_share[0], experts
+    )
+    swap = [(i, i ^ 1) for i in range(experts)]
+    size = tok_rows // chunks
+    moved = []
+    other = None
+    for mine in blocks:
+        near = pair_hop(mine)
+        across = middle_hop(mine)
+        if other is None:
+            other = tuple(lax.ppermute(w, "expert", swap) for w in own)
+        second = outward_hop(across)
+        far = middle_hop(near)
+        third = outward_hop(far)
+        moved.append((mine, near, second, across, third, far))
+    after = []
+    made = []
+    for mine, near, *_ in moved:
+        pair = slot_pieces(
+            named, (mine, near), own, other, after, experts, width, (jnp.float32, jnp.bfloat16)
+        )
+        after = [pair[0]]
+        made.append(pair)
+    passed = []
+    for c, (_, _, second, across, third, far) in enumerate(moved):
+        here, at_near = made[c]
+        at_second, at_third = slot_pieces(
+            named,
+            (second, across, third, far),
+            own,
+            other,
+            after,
+            experts,
+            width,
+            (jnp.bfloat16, jnp.bfloat16),
+        )
+        after = [at_third]
+        in_third = inward_hop(at_third)
+        in_second = inward_hop(at_second)
+        over_third = middle_hop(narrow(wide(at_third) + wide(in_third)))
+        over_second = middle_hop(narrow(wide(at_second) + wide(in_second)))
+        final = pair_hop(narrow(wide(at_near) + wide(over_third)))
+        layer_grad = finish(
+            c * size, saved_rows, upstream_rows, norm_gain, inv_root, here, over_second, final
+        )
+        passed.append(shifted(layer_grad, "section", -1))
+    return jnp.concatenate(passed, axis=0)[None]
+
+
 def solution(mesh):
     placed = (
         P("section", "expert", None),
@@ -122,8 +355,9 @@
         P("section", "expert", None),
         P("section", "expert", None),
     )
+    plan = line_device if mesh.shape["expert"] == 8 else routed_device
     return jax.shard_map(
-        per_device,
+        plan,
         mesh=mesh,
         in_specs=placed,
         out_specs=P("section", "expert", None),

time: 277 us -> 185 us (0.67)
  blocking collectives: 75.3 us -> 0 us
  waiting for transfers between devices: 135 us -> 63.9 us
  Pallas kernels: 0 us -> 64.9 us
  matrix products: 41.3 us -> 0 us
  starting transfers between devices: 15.9 us -> 44.8 us
  local copies, waits for them, and re-layouts: 2.29 us -> 7.08 us
    all_to_all x2 -> x0, waiting for transfers between devices: 124 us -> none  [the longest x1 63 us: per_device(): lax.all_to_all(send_grads, 'expert', split_axis=0, concat_axis=0, tiled=T...]
    all_to_all x1 -> x0, blocking collectives: 75.3 us -> none  [per_device(): lax.all_to_all(result_rows.reshape(experts, slot_count, model_width), 'ex...]
    pallas_call x0 -> x7, Pallas kernels: none -> 64.9 us  [the longest x4 63.9 us: slot_pieces(): pl.pallas_call(functools.partial(slot_kernel, experts, len(blocks) == 4),...]
    ppermute x0 -> x23, waiting for transfers between devices: none -> 60 us  [the longest x20 60 us: along(): return lambda value: lax.ppermute(value, 'expert', cores)]
    dot_general x8 -> x0, matrix products: 41.3 us -> none  [the longest x1 12.7 us: expert_backward(): lax.dot_general(d_gate, gate_w, (((1,), (1,)), ((), ())), preferred_eleme...]
    ppermute x0 -> x23, starting transfers between devices: none -> 39.8 us  [the longest x20 39.3 us: along(): return lambda value: lax.ppermute(value, 'expert', cores)]
    all_to_all x2 -> x0, starting transfers between devices: 13.4 us -> none  [the longest x1 7.94 us: per_device(): lax.all_to_all(send_inputs, 'expert', split_axis=0, concat_axis=0, tiled=...]
    ppermute x1 -> x2, waiting for transfers between devices: 10.8 us -> 3.95 us  [shifted(): lax.ppermute(value, axis, [(i, (i + by) % length) for i in range(length)])]
  transfers between devices with their start and end apart: 3 -> 25, of which waited for: 3 -> 12; matrix products, arithmetic and copies ran while one was open for 4% -> 1% of each run, Pallas kernels for 0% -> 36%
where the time goes in v1:
time: 185 us; the launch traced here: 183 us
  Pallas kernels  64.9 us (35%)
  waiting for transfers between devices  63.9 us (35%)
  starting transfers between devices  44.8 us (24%)
  local copies, waits for them, and re-layouts  7.08 us (4%)
    pallas_call x4, Pallas kernels, slot_pieces(): pl.pallas_call(functools.partial(slot_kernel, experts, len(blocks) == 4),...  63.9 us
    ppermute x20, waiting for transfers between devices, along(): return lambda value: lax.ppermute(value, 'expert', cores)  60 us
    ppermute x20, starting transfers between devices, along(): return lambda value: lax.ppermute(value, 'expert', cores)  39.3 us
    unnamed x24, local copies, waits for them, and re-layouts  7.08 us
    ppermute x2, starting transfers between devices, shifted(): lax.ppermute(value, axis, [(i, (i + by) % length) for i in range(length)])  5.06 us
    ppermute x2, waiting for transfers between devices, shifted(): lax.ppermute(value, axis, [(i, (i + by) % length) for i in range(length)])  3.95 us
  transfers between devices with their start and end apart: 25, of which 12 were waited for; matrix products, arithmetic and copies ran while one was open for 1% of the time, Pallas kernels for 36%

profile of v1, /device:TPU:8, one launch (start us, length us, event | category | flops | bytes accessed | tf_op | source)
XLA Modules:
  0.0 182.6 jit_solution(13669125141396439811)
XLA Ops:
  0.0 0.5 collective-permute-start.2
  0.5 0.8 copy.9
  1.3 0.8 copy.10
  2.1 1.0 copy-done.3
  3.1 1.0 copy-done.5
  4.2 0.7 copy-done.9
  4.9 0.4 shard_map.82
  5.3 2.0 %collective-permute-start.8 = (bf16[64,4224]{1,0:T(8,128)(2,1)S(1)}, bf16[64,4224]{1,0:T(8,128)(2,1)S(1)}, u32[]{:S(2)}, u32[]{:S(2)}) collective-permute-start(bf16[64,4224]{1,0:T(8,128)(2,1)S(1)} %get-tuple-element.19.refs_0_), channel_id=1, source_target_pairs={{0,2},{1,3},{2,0},{3,1},{4,6},{5,7},{6,4},{7,5},{8,10},{9,11},{10,... | collective-permute-start | bytes 1622024 | tf_op jit(solution)/shard_map/ppermute | solution.py:288
  7.3 13.0 %collective-permute-done.refs_1_ = bf16[64,4224]{1,0:T(8,128)(2,1)S(1)} collective-permute-done((bf16[64,4224]{1,0:T(8,128)(2,1)S(1)}, bf16[64,4224]{1,0:T(8,128)(2,1)S(1)}, u32[]{:S(2)}, u32[]{:S(2)}) %collective-permute-start) | collective-permute-done | bytes 540704 | tf_op jit(solution)/shard_map/ppermute | solution.py:288
  20.4 3.5 %collective-permute-start.4 = (bf16[64,4224]{1,0:T(8,128)(2,1)S(1)}, bf16[64,4224]{1,0:T(8,128)(2,1)S(1)}, u32[]{:S(2)}, u32[]{:S(2)}) collective-permute-start(bf16[64,4224]{1,0:T(8,128)(2,1)S(1)} %get-tuple-element.17.refs_0_), channel_id=1, source_target_pairs={{2,4},{3,5},{4,2},{5,3},{10,12},{11,13},{12,10},{13,11},{18,20},{1... | collective-permute-start | bytes 1622024 | tf_op jit(solution)/shard_map/ppermute | solution.py:288
  23.9 7.7 %collective-permute-done.8.refs_1_ = bf16[64,4224]{1,0:T(8,128)(2,1)S(1)} collective-permute-done((bf16[64,4224]{1,0:T(8,128)(2,1)S(1)}, bf16[64,4224]{1,0:T(8,128)(2,1)S(1)}, u32[]{:S(2)}, u32[]{:S(2)}) %collective-permute-start.8) | collective-permute-done | bytes 540704 | tf_op jit(solution)/shard_map/ppermute | solution.py:288
  31.6 3.5 %collective-permute-start.15 = (bf16[64,4224]{1,0:T(8,128)(2,1)S(1)}, bf16[64,4224]{1,0:T(8,128)(2,1)S(1)}, u32[]{:S(2)}, u32[]{:S(2)}) collective-permute-start(bf16[64,4224]{1,0:T(8,128)(2,1)S(1)} %get-tuple-element.19.refs_0_), channel_id=1, source_target_pairs={{2,4},{3,5},{4,2},{5,3},{10,12},{11,13},{12,10},{13,11},{18,20},{1... | collective-permute-start | bytes 1622024 | tf_op jit(solution)/shard_map/ppermute | solution.py:288
  35.1 0.8 collective-permute-done.4.refs_1_
  35.8 3.4 %collective-permute-start.6 = (bf16[64,4224]{1,0:T(8,128)(2,1)S(1)}, bf16[64,4224]{1,0:T(8,128)(2,1)S(1)}, u32[]{:S(2)}, u32[]{:S(2)}) collective-permute-start(bf16[64,4224]{1,0:T(8,128)(2,1)S(1)} %collective-permute-done.refs_1_), channel_id=1, source_target_pairs={{2,4},{3,5},{4,2},{5,3},{10,12},{11,13},{12,10},{13,11},{18,20},{1... | collective-permute-start | bytes 1622024 | tf_op jit(solution)/shard_map/ppermute | solution.py:288
  39.3 9.4 %collective-permute-done.15.refs_1_ = bf16[64,4224]{1,0:T(8,128)(2,1)S(1)} collective-permute-done((bf16[64,4224]{1,0:T(8,128)(2,1)S(1)}, bf16[64,4224]{1,0:T(8,128)(2,1)S(1)}, u32[]{:S(2)}, u32[]{:S(2)}) %collective-permute-start.15) | collective-permute-done | bytes 540704 | tf_op jit(solution)/shard_map/ppermute | solution.py:288
  48.7 0.8 copy-done.7
  49.5 3.5 %collective-permute-start.17 = (bf16[64,4224]{1,0:T(8,128)(2,1)S(1)}, bf16[64,4224]{1,0:T(8,128)(2,1)}, u32[]{:S(2)}, u32[]{:S(2)}) collective-permute-start(bf16[64,4224]{1,0:T(8,128)(2,1)S(1)} %collective-permute-done.8.refs_1_), channel_id=1, source_target_pairs={{2,4},{3,5},{4,2},{5,3},{10,12},{11,13},{12,10},{13,11},{18,20},{1... | collective-permute-start | bytes 1622024 | tf_op jit(solution)/shard_map/ppermute | solution.py:288
  53.0 0.1 pad_add_fusion.named_ref
  53.0 7.2 %collective-permute-done.6.refs_3_ = bf16[64,4224]{1,0:T(8,128)(2,1)S(1)} collective-permute-done((bf16[64,4224]{1,0:T(8,128)(2,1)S(1)}, bf16[64,4224]{1,0:T(8,128)(2,1)S(1)}, u32[]{:S(2)}, u32[]{:S(2)}) %collective-permute-start.6) | collective-permute-done | bytes 540704 | tf_op jit(solution)/shard_map/ppermute | solution.py:288
  60.2 1.3 collective-permute-start.5
  61.6 9.1 %collective-permute-done.17.refs_3_ = bf16[64,4224]{1,0:T(8,128)(2,1)} collective-permute-done((bf16[64,4224]{1,0:T(8,128)(2,1)S(1)}, bf16[64,4224]{1,0:T(8,128)(2,1)}, u32[]{:S(2)}, u32[]{:S(2)}) %collective-permute-start.17) | collective-permute-done | bytes 540704 | tf_op jit(solution)/shard_map/ppermute | solution.py:288
  70.7 1.3 collective-permute-start.16
  72.0 1.3 collective-permute-start.7
  73.4 1.3 collective-permute-start.18
  74.7 1.9 %copy-done = bf16[1,1,2048,768]{3,2,1,0:T(8,128)(2,1)S(1)} copy-done((bf16[1,1,2048,768]{3,2,1,0:T(8,128)(2,1)S(1)}, bf16[1,1,2048,768]{3,2,1,0:T(8,128)(2,1)}, u32[]{:S(2)}) %copy-start) | copy-done | bytes 3145752
  76.6 15.7 %shard_map.83 = (f32[64,2048]{1,0:T(8,128)S(1)}, bf16[64,2048]{1,0:T(8,128)(2,1)S(1)}) custom-call(s32[3]{0:T(128)S(1)} %pad_add_fusion.named_ref, bf16[64,4224]{1,0:T(8,128)(2,1)S(1)} %get-tuple-element.17.refs_0_, bf16[64,4224]{1,0:T(8,128)(2,1)S(1)} %collective-permute-done.refs_1_, bf16[2048,768]{1,0:T(8,128)(2,1)S(1)} %bitcast.14, ...), custom_call_target="tpu_custom_call" | custom-call | flops 4026531840 | bytes 20971520 | tf_op jit(solution)/shard_map/pallas_call | solution.py:233
  92.4 15.6 %shard_map.84 = (f32[64,2048]{1,0:T(8,128)S(1)}, bf16[64,2048]{1,0:T(8,128)(2,1)S(1)}) custom-call(s32[3]{0:T(128)S(1)} %pad_add_fusion.named_ref, bf16[64,4224]{1,0:T(8,128)(2,1)S(1)} %get-tuple-element.19.refs_0_, bf16[64,4224]{1,0:T(8,128)(2,1)S(1)} %collective-permute-done.8.refs_1_, bf16[2048,768]{1,0:T(8,128)(2,1)S(1)} %bitcast.15, ...), custom_call_target="tpu_custom_call" | custom-call | flops 4026531840 | bytes 20971520 | tf_op jit(solution)/shard_map/pallas_call | solution.py:233
  108.0 16.7 %shard_map.85 = (bf16[64,2048]{1,0:T(8,128)(2,1)S(1)}, bf16[64,2048]{1,0:T(8,128)(2,1)S(1)}) custom-call(s32[3]{0:T(128)S(1)} %pad_add_fusion.named_ref, bf16[64,4224]{1,0:T(8,128)(2,1)S(1)} %collective-permute-done.5.refs_0_, bf16[64,4224]{1,0:T(8,128)(2,1)S(1)} %collective-permute-done.4.refs_1_, bf16[64,4224]{1,0:T(8,128)(2,1)S(1)} %collective-permute-done.7.refs_2_, ...), custom_call_target="tpu_custom_call" | custom-call | flops 4026531840 | bytes 20971520 | tf_op jit(solution)/shard_map/pallas_call | solution.py:233
  124.7 1.3 collective-permute-start.11
  126.0 1.3 collective-permute-start.9
  127.4 15.8 %shard_map.87 = (bf16[64,2048]{1,0:T(8,128)(2,1)S(1)}, bf16[64,2048]{1,0:T(8,128)(2,1)S(1)}) custom-call(s32[3]{0:T(128)S(1)} %pad_add_fusion.named_ref, bf16[64,4224]{1,0:T(8,128)(2,1)S(1)} %collective-permute-done.16.refs_0_, bf16[64,4224]{1,0:T(8,128)(2,1)S(1)} %copy-done.8, bf16[64,4224]{1,0:T(8,128)(2,1)S(1)} %collective-permute-done.18.refs_2_, ...), custom_call_target="tpu_custom_call" | custom-call | flops 4026531840 | bytes 20971520 | tf_op jit(solution)/shard_map/pallas_call | solution.py:233
  143.3 1.4 collective-permute-start.21
  144.7 1.3 collective-permute-start.19
  146.1 3.5 %collective-permute-start.12 = (bf16[64,2048]{1,0:T(8,128)(2,1)S(1)}, bf16[64,2048]{1,0:T(8,128)(2,1)S(1)}, u32[]{:S(2)}, u32[]{:S(2)}) collective-permute-start(bf16[64,2048]{1,0:T(8,128)(2,1)S(1)} %add_convert_fusion.4), channel_id=1, source_target_pairs={{2,4},{3,5},{4,2},{5,3},{10,12},{11,13},{12,10},{13,11},{18,20},{1... | collective-permute-start | bytes 786440 | tf_op jit(solution)/shard_map/ppermute | solution.py:288
  149.6 2.4 %collective-permute-start.10 = (bf16[64,2048]{1,0:T(8,128)(2,1)S(1)}, bf16[64,2048]{1,0:T(8,128)(2,1)S(1)}, u32[]{:S(2)}, u32[]{:S(2)}) collective-permute-start(bf16[64,2048]{1,0:T(8,128)(2,1)S(1)} %add_convert_fusion.5), channel_id=1, source_target_pairs={{2,4},{3,5},{4,2},{5,3},{10,12},{11,13},{12,10},{13,11},{18,20},{1... | collective-permute-start | bytes 786440 | tf_op jit(solution)/shard_map/ppermute | solution.py:288
  152.0 2.5 %collective-permute-done.21 = bf16[64,2048]{1,0:T(8,128)(2,1)S(1)} collective-permute-done((bf16[64,2048]{1,0:T(8,128)(2,1)S(1)}, bf16[64,2048]{1,0:T(8,128)(2,1)S(1)}, u32[]{:S(2)}, u32[]{:S(2)}) %collective-permute-start.21) | collective-permute-done | bytes 262176 | tf_op jit(solution)/shard_map/ppermute | solution.py:288
  154.6 3.4 %collective-permute-start.22 = (bf16[64,2048]{1,0:T(8,128)(2,1)S(1)}, bf16[64,2048]{1,0:T(8,128)(2,1)S(1)}, u32[]{:S(2)}, u32[]{:S(2)}) collective-permute-start(bf16[64,2048]{1,0:T(8,128)(2,1)S(1)} %add_convert_fusion.1), channel_id=1, source_target_pairs={{2,4},{3,5},{4,2},{5,3},{10,12},{11,13},{12,10},{13,11},{18,20},{1... | collective-permute-start | bytes 786440 | tf_op jit(solution)/shard_map/ppermute | solution.py:288
  158.2 3.3 %collective-permute-start.20 = (bf16[64,2048]{1,0:T(8,128)(2,1)S(1)}, bf16[64,2048]{1,0:T(8,128)(2,1)S(1)}, u32[]{:S(2)}, u32[]{:S(2)}) collective-permute-start(bf16[64,2048]{1,0:T(8,128)(2,1)S(1)} %add_convert_fusion.2), channel_id=1, source_target_pairs={{2,4},{3,5},{4,2},{5,3},{10,12},{11,13},{12,10},{13,11},{18,20},{1... | collective-permute-start | bytes 786440 | tf_op jit(solution)/shard_map/ppermute | solution.py:288
  161.7 6.8 %collective-permute-done.22 = bf16[64,2048]{1,0:T(8,128)(2,1)S(1)} collective-permute-done((bf16[64,2048]{1,0:T(8,128)(2,1)S(1)}, bf16[64,2048]{1,0:T(8,128)(2,1)S(1)}, u32[]{:S(2)}, u32[]{:S(2)}) %collective-permute-start.22) | collective-permute-done | bytes 262176 | tf_op jit(solution)/shard_map/ppermute | solution.py:288
  168.6 0.4 collective-permute-done.13.last_ref
  169.1 0.3 shard_map.86
  169.4 2.6 %collective-permute-start.14 = (bf16[64,2048]{1,0:T(8,128)(2,1)S(1)}, bf16[64,2048]{1,0:T(8,128)(2,1)S(1)}, u32[]{:S(2)}, u32[]{:S(2)}) collective-permute-start(bf16[64,2048]{1,0:T(8,128)(2,1)S(1)} %shard_map.86), channel_id=1, source_target_pairs={{0,24},{8,0},{16,8},{24,16},{1,25},{9,1},{17,9},{25,17},{2,26},{10... | collective-permute-start | bytes 786440 | tf_op jit(solution)/shard_map/ppermute | solution.py:15
  172.0 3.0 %collective-permute-done.23.last_ref = bf16[64,2048]{1,0:T(8,128)(2,1)S(1)} collective-permute-done((bf16[64,2048]{1,0:T(8,128)(2,1)S(1)}, bf16[64,2048]{1,0:T(8,128)(2,1)S(1)}, u32[]{:S(2)}, u32[]{:S(2)}) %collective-permute-start.23) | collective-permute-done | bytes 262176 | tf_op jit(solution)/shard_map/ppermute | solution.py:288
  175.0 0.3 shard_map.88
  175.3 2.5 %collective-permute-start.24 = (bf16[64,2048]{1,0:T(8,128)(2,1)S(1)}, bf16[64,2048]{1,0:T(8,128)(2,1)S(1)}, u32[]{:S(2)}, u32[]{:S(2)}) collective-permute-start(bf16[64,2048]{1,0:T(8,128)(2,1)S(1)} %shard_map.88), channel_id=1, source_target_pairs={{0,24},{8,0},{16,8},{24,16},{1,25},{9,1},{17,9},{25,17},{2,26},{10... | collective-permute-start | bytes 786440 | tf_op jit(solution)/shard_map/ppermute | solution.py:15
  177.8 0.1 collective-permute-done.14
  177.9 3.8 %collective-permute-done.24 = bf16[64,2048]{1,0:T(8,128)(2,1)S(1)} collective-permute-done((bf16[64,2048]{1,0:T(8,128)(2,1)S(1)}, bf16[64,2048]{1,0:T(8,128)(2,1)S(1)}, u32[]{:S(2)}, u32[]{:S(2)}) %collective-permute-start.24) | collective-permute-done | bytes 262176 | tf_op jit(solution)/shard_map/ppermute | solution.py:15
  181.7 0.8 maximum_bitcast_fusion
  (41 shorter events, 0.7 us)
Async XLA Ops:
  0.0 72.0 %collective-permute-start.1 = (bf16[2048,768]{1,0:T(8,128)(2,1)}, bf16[2048,768]{1,0:T(8,128)(2,1)}, u32[]{:S(2)}, u32[]{:S(2)}) collective-permute-start(bf16[2048,768]{1,0:T(8,128)(2,1)} %bitcast.12), channel_id=1, source_target_pairs={{0,1},{1,0},{2,3},{3,2},{4,5},{5,4},{6,7},{7,6},{8,9},{9,8},{10,11... | collective-permute-start | bytes 9437192 | tf_op jit(solution)/shard_map/ppermute | solution.py:308
  0.0 73.4 %collective-permute-start.2 = (bf16[2048,768]{1,0:T(8,128)(2,1)}, bf16[2048,768]{1,0:T(8,128)(2,1)}, u32[]{:S(2)}, u32[]{:S(2)}) collective-permute-start(bf16[2048,768]{1,0:T(8,128)(2,1)} %bitcast.25), channel_id=1, source_target_pairs={{0,1},{1,0},{2,3},{3,2},{4,5},{5,4},{6,7},{7,6},{8,9},{9,8},{10,11... | collective-permute-start | bytes 9437192 | tf_op jit(solution)/shard_map/ppermute | solution.py:308
  0.5 74.2 %collective-permute-start.3 = (bf16[768,2048]{1,0:T(8,128)(2,1)}, bf16[768,2048]{1,0:T(8,128)(2,1)}, u32[]{:S(2)}, u32[]{:S(2)}) collective-permute-start(bf16[768,2048]{1,0:T(8,128)(2,1)} %bitcast.30), channel_id=1, source_target_pairs={{0,1},{1,0},{2,3},{3,2},{4,5},{5,4},{6,7},{7,6},{8,9},{9,8},{10,11... | collective-permute-start | bytes 9437192 | tf_op jit(solution)/shard_map/ppermute | solution.py:308
  2.1 1.0 copy-start.3
  3.1 1.0 copy-start.5
  4.2 0.7 copy-start.9
  5.3 15.1 %collective-permute-start = (bf16[64,4224]{1,0:T(8,128)(2,1)S(1)}, bf16[64,4224]{1,0:T(8,128)(2,1)S(1)}, u32[]{:S(2)}, u32[]{:S(2)}) collective-permute-start(bf16[64,4224]{1,0:T(8,128)(2,1)S(1)} %get-tuple-element.17.refs_0_), channel_id=1, source_target_pairs={{0,2},{1,3},{2,0},{3,1},{4,6},{5,7},{6,4},{7,5},{8,10},{9,11},{10,... | collective-permute-start | bytes 1622024 | tf_op jit(solution)/shard_map/ppermute | solution.py:288
  5.3 26.3 %collective-permute-start.8 = (bf16[64,4224]{1,0:T(8,128)(2,1)S(1)}, bf16[64,4224]{1,0:T(8,128)(2,1)S(1)}, u32[]{:S(2)}, u32[]{:S(2)}) collective-permute-start(bf16[64,4224]{1,0:T(8,128)(2,1)S(1)} %get-tuple-element.19.refs_0_), channel_id=1, source_target_pairs={{0,2},{1,3},{2,0},{3,1},{4,6},{5,7},{6,4},{7,5},{8,10},{9,11},{10,... | collective-permute-start | bytes 1622024 | tf_op jit(solution)/shard_map/ppermute | solution.py:288
  20.4 15.4 %collective-permute-start.4 = (bf16[64,4224]{1,0:T(8,128)(2,1)S(1)}, bf16[64,4224]{1,0:T(8,128)(2,1)S(1)}, u32[]{:S(2)}, u32[]{:S(2)}) collective-permute-start(bf16[64,4224]{1,0:T(8,128)(2,1)S(1)} %get-tuple-element.17.refs_0_), channel_id=1, source_target_pairs={{2,4},{3,5},{4,2},{5,3},{10,12},{11,13},{12,10},{13,11},{18,20},{1... | collective-permute-start | bytes 1622024 | tf_op jit(solution)/shard_map/ppermute | solution.py:288
  31.6 17.1 %collective-permute-start.15 = (bf16[64,4224]{1,0:T(8,128)(2,1)S(1)}, bf16[64,4224]{1,0:T(8,128)(2,1)S(1)}, u32[]{:S(2)}, u32[]{:S(2)}) collective-permute-start(bf16[64,4224]{1,0:T(8,128)(2,1)S(1)} %get-tuple-element.19.refs_0_), channel_id=1, source_target_pairs={{2,4},{3,5},{4,2},{5,3},{10,12},{11,13},{12,10},{13,11},{18,20},{1... | collective-permute-start | bytes 1622024 | tf_op jit(solution)/shard_map/ppermute | solution.py:288
  35.8 24.4 %collective-permute-start.6 = (bf16[64,4224]{1,0:T(8,128)(2,1)S(1)}, bf16[64,4224]{1,0:T(8,128)(2,1)S(1)}, u32[]{:S(2)}, u32[]{:S(2)}) collective-permute-start(bf16[64,4224]{1,0:T(8,128)(2,1)S(1)} %collective-permute-done.refs_1_), channel_id=1, source_target_pairs={{2,4},{3,5},{4,2},{5,3},{10,12},{11,13},{12,10},{13,11},{18,20},{1... | collective-permute-start | bytes 1622024 | tf_op jit(solution)/shard_map/ppermute | solution.py:288
  48.7 0.8 copy-start.7
  49.5 21.2 %collective-permute-start.17 = (bf16[64,4224]{1,0:T(8,128)(2,1)S(1)}, bf16[64,4224]{1,0:T(8,128)(2,1)}, u32[]{:S(2)}, u32[]{:S(2)}) collective-permute-start(bf16[64,4224]{1,0:T(8,128)(2,1)S(1)} %collective-permute-done.8.refs_1_), channel_id=1, source_target_pairs={{2,4},{3,5},{4,2},{5,3},{10,12},{11,13},{12,10},{13,11},{18,20},{1... | collective-permute-start | bytes 1622024 | tf_op jit(solution)/shard_map/ppermute | solution.py:288
  60.2 47.7 %collective-permute-start.5 = (bf16[64,4224]{1,0:T(8,128)(2,1)S(1)}, bf16[64,4224]{1,0:T(8,128)(2,1)S(1)}, u32[]{:S(2)}, u32[]{:S(2)}) collective-permute-start(bf16[64,4224]{1,0:T(8,128)(2,1)S(1)} %collective-permute-done.4.refs_1_), channel_id=1, source_target_pairs={{2,0},{3,1},{4,6},{5,7},{10,8},{11,9},{12,14},{13,15},{18,16},{19,... | collective-permute-start | bytes 1622024 | tf_op jit(solution)/shard_map/ppermute | solution.py:288
  70.7 56.6 %collective-permute-start.16 = (bf16[64,4224]{1,0:T(8,128)(2,1)}, bf16[64,4224]{1,0:T(8,128)(2,1)S(1)}, u32[]{:S(2)}, u32[]{:S(2)}) collective-permute-start(bf16[64,4224]{1,0:T(8,128)(2,1)} %copy-done.7), channel_id=1, source_target_pairs={{2,0},{3,1},{4,6},{5,7},{10,8},{11,9},{12,14},{13,15},{18,16},{19,... | collective-permute-start | bytes 1622024 | tf_op jit(solution)/shard_map/ppermute | solution.py:288
  72.0 36.0 %collective-permute-start.7 = (bf16[64,4224]{1,0:T(8,128)(2,1)S(1)}, bf16[64,4224]{1,0:T(8,128)(2,1)S(1)}, u32[]{:S(2)}, u32[]{:S(2)}) collective-permute-start(bf16[64,4224]{1,0:T(8,128)(2,1)S(1)} %collective-permute-done.6.refs_3_), channel_id=1, source_target_pairs={{2,0},{3,1},{4,6},{5,7},{10,8},{11,9},{12,14},{13,15},{18,16},{19,... | collective-permute-start | bytes 1622024 | tf_op jit(solution)/shard_map/ppermute | solution.py:288
  73.4 54.0 %collective-permute-start.18 = (bf16[64,4224]{1,0:T(8,128)(2,1)}, bf16[64,4224]{1,0:T(8,128)(2,1)S(1)}, u32[]{:S(2)}, u32[]{:S(2)}) collective-permute-start(bf16[64,4224]{1,0:T(8,128)(2,1)} %collective-permute-done.17.refs_3_), channel_id=1, source_target_pairs={{2,0},{3,1},{4,6},{5,7},{10,8},{11,9},{12,14},{13,15},{18,16},{19,... | collective-permute-start | bytes 1622024 | tf_op jit(solution)/shard_map/ppermute | solution.py:288
  74.7 1.9 %copy-start = (bf16[1,1,2048,768]{3,2,1,0:T(8,128)(2,1)S(1)}, bf16[1,1,2048,768]{3,2,1,0:T(8,128)(2,1)}, u32[]{:S(2)}) copy-start(bf16[1,1,2048,768]{3,2,1,0:T(8,128)(2,1)} %param.11) | copy-start | bytes 9437188
  76.6 15.8 %copy-start.1 = (bf16[1,1,2048,768]{3,2,1,0:T(8,128)(2,1)S(1)}, bf16[1,1,2048,768]{3,2,1,0:T(8,128)(2,1)}, u32[]{:S(2)}) copy-start(bf16[1,1,2048,768]{3,2,1,0:T(8,128)(2,1)} %param.11) | copy-start | bytes 9437188
  108.0 19.4 %copy-start.2 = (bf16[1,1,2048,768]{3,2,1,0:T(8,128)(2,1)S(1)}, bf16[1,1,2048,768]{3,2,1,0:T(8,128)(2,1)}, u32[]{:S(2)}) copy-start(bf16[1,1,2048,768]{3,2,1,0:T(8,128)(2,1)} %param.11) | copy-start | bytes 9437188
  108.0 19.4 %copy-start.8 = (bf16[64,4224]{1,0:T(8,128)(2,1)S(1)}, bf16[64,4224]{1,0:T(8,128)(2,1)}, u32[]{:S(2)}) copy-start(bf16[64,4224]{1,0:T(8,128)(2,1)} %copy-done.7) | copy-start | bytes 1622020
  124.7 21.3 %collective-permute-start.11 = (bf16[64,2048]{1,0:T(8,128)(2,1)S(1)}, bf16[64,2048]{1,0:T(8,128)(2,1)S(1)}, u32[]{:S(2)}, u32[]{:S(2)}) collective-permute-start(bf16[64,2048]{1,0:T(8,128)(2,1)S(1)} %get-tuple-element.23.refs_10_), channel_id=1, source_target_pairs={{0,2},{1,3},{6,4},{7,5},{8,10},{9,11},{14,12},{15,13},{16,18},{17,... | collective-permute-start | bytes 786440 | tf_op jit(solution)/shard_map/ppermute | solution.py:288
  126.0 23.5 %collective-permute-start.9 = (bf16[64,2048]{1,0:T(8,128)(2,1)S(1)}, bf16[64,2048]{1,0:T(8,128)(2,1)S(1)}, u32[]{:S(2)}, u32[]{:S(2)}) collective-permute-start(bf16[64,2048]{1,0:T(8,128)(2,1)S(1)} %get-tuple-element.21), channel_id=1, source_target_pairs={{0,2},{1,3},{6,4},{7,5},{8,10},{9,11},{14,12},{15,13},{16,18},{17,... | collective-permute-start | bytes 786440 | tf_op jit(solution)/shard_map/ppermute | solution.py:288
  143.2 25.8 %copy-start.4 = (bf16[1,128,2048]{2,1,0:T(8,128)(2,1)S(1)}, bf16[1,128,2048]{2,1,0:T(8,128)(2,1)}, u32[]{:S(2)}) copy-start(bf16[1,128,2048]{2,1,0:T(8,128)(2,1)} %param.8) | copy-start | bytes 1572868
  143.2 25.8 %copy-start.6 = (bf16[1,128,2048]{2,1,0:T(8,128)(2,1)S(1)}, bf16[1,128,2048]{2,1,0:T(8,128)(2,1)}, u32[]{:S(2)}) copy-start(bf16[1,128,2048]{2,1,0:T(8,128)(2,1)} %param.9) | copy-start | bytes 1572868
  143.3 25.8 %copy-start.10 = (f32[1,2048]{1,0:T(1,128)S(1)}, f32[1,2048]{1,0:T(1,128)}, u32[]{:S(2)}) copy-start(f32[1,2048]{1,0:T(1,128)} %gain_ref.5) | copy-start | bytes 24580
  143.3 11.3 %collective-permute-start.21 = (bf16[64,2048]{1,0:T(8,128)(2,1)S(1)}, bf16[64,2048]{1,0:T(8,128)(2,1)S(1)}, u32[]{:S(2)}, u32[]{:S(2)}) collective-permute-start(bf16[64,2048]{1,0:T(8,128)(2,1)S(1)} %get-tuple-element.26), channel_id=1, source_target_pairs={{0,2},{1,3},{6,4},{7,5},{8,10},{9,11},{14,12},{15,13},{16,18},{17,... | collective-permute-start | bytes 786440 | tf_op jit(solution)/shard_map/ppermute | solution.py:288
  144.7 13.4 %collective-permute-start.19 = (bf16[64,2048]{1,0:T(8,128)(2,1)S(1)}, bf16[64,2048]{1,0:T(8,128)(2,1)S(1)}, u32[]{:S(2)}, u32[]{:S(2)}) collective-permute-start(bf16[64,2048]{1,0:T(8,128)(2,1)S(1)} %get-tuple-element.24), channel_id=1, source_target_pairs={{0,2},{1,3},{6,4},{7,5},{8,10},{9,11},{14,12},{15,13},{16,18},{17,... | collective-permute-start | bytes 786440 | tf_op jit(solution)/shard_map/ppermute | solution.py:288
  146.1 15.4 %collective-permute-start.12 = (bf16[64,2048]{1,0:T(8,128)(2,1)S(1)}, bf16[64,2048]{1,0:T(8,128)(2,1)S(1)}, u32[]{:S(2)}, u32[]{:S(2)}) collective-permute-start(bf16[64,2048]{1,0:T(8,128)(2,1)S(1)} %add_convert_fusion.4), channel_id=1, source_target_pairs={{2,4},{3,5},{4,2},{5,3},{10,12},{11,13},{12,10},{13,11},{18,20},{1... | collective-permute-start | bytes 786440 | tf_op jit(solution)/shard_map/ppermute | solution.py:288
  149.6 19.0 %collective-permute-start.10 = (bf16[64,2048]{1,0:T(8,128)(2,1)S(1)}, bf16[64,2048]{1,0:T(8,128)(2,1)S(1)}, u32[]{:S(2)}, u32[]{:S(2)}) collective-permute-start(bf16[64,2048]{1,0:T(8,128)(2,1)S(1)} %add_convert_fusion.5), channel_id=1, source_target_pairs={{2,4},{3,5},{4,2},{5,3},{10,12},{11,13},{12,10},{13,11},{18,20},{1... | collective-permute-start | bytes 786440 | tf_op jit(solution)/shard_map/ppermute | solution.py:288
  154.6 13.8 %collective-permute-start.22 = (bf16[64,2048]{1,0:T(8,128)(2,1)S(1)}, bf16[64,2048]{1,0:T(8,128)(2,1)S(1)}, u32[]{:S(2)}, u32[]{:S(2)}) collective-permute-start(bf16[64,2048]{1,0:T(8,128)(2,1)S(1)} %add_convert_fusion.1), channel_id=1, source_target_pairs={{2,4},{3,5},{4,2},{5,3},{10,12},{11,13},{12,10},{13,11},{18,20},{1... | collective-permute-start | bytes 786440 | tf_op jit(solution)/shard_map/ppermute | solution.py:288
  158.2 13.8 %collective-permute-start.20 = (bf16[64,2048]{1,0:T(8,128)(2,1)S(1)}, bf16[64,2048]{1,0:T(8,128)(2,1)S(1)}, u32[]{:S(2)}, u32[]{:S(2)}) collective-permute-start(bf16[64,2048]{1,0:T(8,128)(2,1)S(1)} %add_convert_fusion.2), channel_id=1, source_target_pairs={{2,4},{3,5},{4,2},{5,3},{10,12},{11,13},{12,10},{13,11},{18,20},{1... | collective-permute-start | bytes 786440 | tf_op jit(solution)/shard_map/ppermute | solution.py:288
  161.6 7.5 %collective-permute-start.13 = (bf16[64,2048]{1,0:T(8,128)(2,1)S(1)}, bf16[64,2048]{1,0:T(8,128)(2,1)S(1)}, u32[]{:S(2)}, u32[]{:S(2)}) collective-permute-start(bf16[64,2048]{1,0:T(8,128)(2,1)S(1)} %add_convert_fusion.3), channel_id=1, source_target_pairs={{0,2},{1,3},{2,0},{3,1},{4,6},{5,7},{6,4},{7,5},{8,10},{9,11},{10,... | collective-permute-start | bytes 786440 | tf_op jit(solution)/shard_map/ppermute | solution.py:288
  168.5 6.4 %collective-permute-start.23 = (bf16[64,2048]{1,0:T(8,128)(2,1)S(1)}, bf16[64,2048]{1,0:T(8,128)(2,1)S(1)}, u32[]{:S(2)}, u32[]{:S(2)}) collective-permute-start(bf16[64,2048]{1,0:T(8,128)(2,1)S(1)} %add_convert_fusion), channel_id=1, source_target_pairs={{0,2},{1,3},{2,0},{3,1},{4,6},{5,7},{6,4},{7,5},{8,10},{9,11},{10,... | collective-permute-start | bytes 786440 | tf_op jit(solution)/shard_map/ppermute | solution.py:288
  169.4 8.5 %collective-permute-start.14 = (bf16[64,2048]{1,0:T(8,128)(2,1)S(1)}, bf16[64,2048]{1,0:T(8,128)(2,1)S(1)}, u32[]{:S(2)}, u32[]{:S(2)}) collective-permute-start(bf16[64,2048]{1,0:T(8,128)(2,1)S(1)} %shard_map.86), channel_id=1, source_target_pairs={{0,24},{8,0},{16,8},{24,16},{1,25},{9,1},{17,9},{25,17},{2,26},{10... | collective-permute-start | bytes 786440 | tf_op jit(solution)/shard_map/ppermute | solution.py:15
  175.3 6.4 %collective-permute-start.24 = (bf16[64,2048]{1,0:T(8,128)(2,1)S(1)}, bf16[64,2048]{1,0:T(8,128)(2,1)S(1)}, u32[]{:S(2)}, u32[]{:S(2)}) collective-permute-start(bf16[64,2048]{1,0:T(8,128)(2,1)S(1)} %shard_map.88), channel_id=1, source_target_pairs={{0,24},{8,0},{16,8},{24,16},{1,25},{9,1},{17,9},{25,17},{2,26},{10... | collective-permute-start | bytes 786440 | tf_op jit(solution)/shard_map/ppermute | solution.py:15

commit v2 on v0

--- a/solution.py
+++ b/solution.py
@@ -1,6 +1,9 @@
+import functools
 import jax
 import jax.numpy as jnp
 from jax import lax
+from jax.experimental import pallas as pl
+from jax.experimental.pallas import tpu as pltpu
 from jax.sharding import PartitionSpec as P
 
 epsilon = 1e-06
@@ -43,7 +46,7 @@
     return summed.astype(jnp.bfloat16)
 
 
-def per_device(
+def routed_device(
     saved_input, upstream, norm_gain, gate_weight, up_weight, down_weight, expert_ids, gate_share
 ):
     saved_rows = saved_input[0]
@@ -111,6 +114,236 @@
     return passed[None]
 
 
+tile = 256
+last_dims = (((1,), (1,)), ((), ()))
+in_vmem = pl.BlockSpec(memory_space=pltpu.VMEM)
+in_smem = pl.BlockSpec(memory_space=pltpu.SMEM)
+anywhere = pl.BlockSpec(memory_space=pl.ANY)
+
+
+def tile_cut(step):
+    return pl.ds(pl.multiple_of(step * tile, tile), tile)
+
+
+def shared_kernel(experts, upstream_ref, ids_ref, share_ref, out_ref):
+    size, width = upstream_ref.shape
+    lanes = out_ref.shape[1] - width
+    out_ref[:, :width] = upstream_ref[...]
+    lane = lax.broadcasted_iota(jnp.int32, (size, lanes), 1)
+    dense = jnp.zeros((size, lanes), jnp.float32)
+    for k in range(ids_ref.shape[1]):
+        hit = lax.rem(lane, experts) == ids_ref[:, k : k + 1]
+        dense = dense + jnp.where(hit, share_ref[:, k : k + 1], 0.0)
+    high = dense.astype(jnp.bfloat16).astype(jnp.float32)
+    middle = (dense - high).astype(jnp.bfloat16).astype(jnp.float32)
+    low = dense - high - middle
+    parts = jnp.where(lane < experts, high, jnp.where(lane < 2 * experts, middle, low))
+    out_ref[:, width:] = jnp.where(lane < 3 * experts, parts, 0.0).astype(jnp.bfloat16)
+
+
+def shared_rows(upstream_rows, routed, shares, experts):
+    count, width = upstream_rows.shape
+    return pl.pallas_call(
+        functools.partial(shared_kernel, experts),
+        in_specs=[in_vmem] * 3,
+        out_specs=in_vmem,
+        out_shape=jax.ShapeDtypeStruct((count, width + 128), jnp.bfloat16),
+        compiler_params=pltpu.CompilerParams(vmem_limit_bytes=16 << 20),
+    )(upstream_rows, routed, shares)
+
+
+def factors_kernel(pairs, saved_ref, gain_ref, *refs):
+    weight_refs = refs[: 2 * pairs]
+    gate_ref, up_ref, rows_ref = refs[-3:]
+    value = saved_ref[...].astype(jnp.float32)
+    inv_root = lax.rsqrt(jnp.mean(value * value, axis=1, keepdims=True) + epsilon)
+    rows_ref[...] = (value * inv_root * gain_ref[...]).astype(jnp.bfloat16)
+
+    def body(step, carry):
+        cut = tile_cut(step)
+        for w in range(pairs):
+            inputs = rows_ref[...]
+            pre_gate = jnp.dot(
+                inputs, weight_refs[2 * w][:, cut], preferred_element_type=jnp.float32
+            )
+            pre_up = jnp.dot(
+                inputs, weight_refs[2 * w + 1][:, cut], preferred_element_type=jnp.float32
+            )
+            sigmoid_gate = jax.nn.sigmoid(pre_gate)
+            gate_ref[w, :, cut] = pre_up * sigmoid_gate * (1.0 + pre_gate * (1.0 - sigmoid_gate))
+            up_ref[w, :, cut] = pre_gate * sigmoid_gate
+        return carry
+
+    lax.fori_loop(0, gate_ref.shape[2] // tile, body, 0)
+
+
+def slot_factors(rows, gain_row, weights, after):
+    pairs = len(weights)
+    count, width = rows.shape
+    hidden = weights[0][0].shape[1]
+    flat = [w for gate_w, up_w, _ in weights for w in (gate_w, up_w)]
+    shape = jax.ShapeDtypeStruct((pairs, count, hidden), jnp.float32)
+    return pl.pallas_call(
+        functools.partial(factors_kernel, pairs),
+        in_specs=[in_vmem] * (2 + len(flat)) + [anywhere] * len(after),
+        out_specs=[in_vmem] * 2,
+        out_shape=[shape] * 2,
+        scratch_shapes=[pltpu.VMEM((count, width), jnp.bfloat16)],
+        cost_estimate=pl.CostEstimate(
+            flops=8 * pairs * count * width * hidden,
+            bytes_accessed=4 * pairs * width * hidden,
+            transcendentals=pairs * count * hidden,
+        ),
+        compiler_params=pltpu.CompilerParams(vmem_limit_bytes=40 << 20),
+    )(rows, gain_row, *flat, *after)
+
+
+def pieces_kernel(experts, pairs, start, named_ref, rows_ref, gain_ref, gate_ref, up_ref, *refs):
+    weight_refs, refs = refs[: 3 * pairs], refs[3 * pairs :]
+    base_ref = refs[0] if start else None
+    out_ref, gate_grads, up_grads = refs[-3:]
+    width = out_ref.shape[1]
+    hidden = gate_ref.shape[2]
+    parts = rows_ref[:, width:].astype(jnp.float32)
+    lane = lax.broadcasted_iota(jnp.int32, parts.shape, 1)
+    shares = []
+    for w in range(pairs):
+        wanted = (lax.rem(lane, experts) == named_ref[w]) & (lane < 3 * experts)
+        shares.append(jnp.sum(jnp.where(wanted, parts, 0.0), axis=1, keepdims=True))
+
+    def grads_of(step, carry):
+        cut = tile_cut(step)
+        for w in range(pairs):
+            grad = lax.dot_general(
+                rows_ref[:, :width],
+                weight_refs[3 * w + 2][cut, :],
+                last_dims,
+                preferred_element_type=jnp.float32,
+            )
+            grad = grad * shares[w]
+            gate_grads[w, :, cut] = (grad * gate_ref[w, :, cut]).astype(jnp.bfloat16)
+            up_grads[w, :, cut] = (grad * up_ref[w, :, cut]).astype(jnp.bfloat16)
+        return carry
+
+    lax.fori_loop(0, hidden // tile, grads_of, 0)
+
+    def pieces_of(step, carry):
+        cut = tile_cut(step)
+        total = None
+        for w in range(pairs):
+            for held, weight_ref in ((gate_grads, weight_refs[3 * w]), (up_grads, weight_refs[3 * w + 1])):
+                part = lax.dot_general(
+                    held[w], weight_ref[cut, :], last_dims, preferred_element_type=jnp.float32
+                )
+                total = part if total is None else total + part
+        total = total * gain_ref[:, cut]
+        if start:
+            total = total + base_ref[:, cut]
+        out_ref[:, cut] = total.astype(out_ref.dtype)
+        return carry
+
+    lax.fori_loop(0, width // tile, pieces_of, 0)
+
+
+def slot_pieces(named, rows, gain_row, factors, weights, experts, kind, base, after):
+    pairs, count, hidden = factors[0].shape
+    width = weights[0][0].shape[0]
+    flat = [w for group in weights for w in group]
+    start = [] if base is None else [base]
+    return pl.pallas_call(
+        functools.partial(pieces_kernel, experts, pairs, len(start)),
+        in_specs=[in_smem]
+        + [in_vmem] * (4 + len(flat) + len(start))
+        + [anywhere] * len(after),
+        out_specs=in_vmem,
+        out_shape=jax.ShapeDtypeStruct((count, width), kind),
+        scratch_shapes=[pltpu.VMEM((pairs, count, hidden), jnp.bfloat16)] * 2,
+        cost_estimate=pl.CostEstimate(
+            flops=12 * pairs * count * width * hidden,
+            bytes_accessed=6 * pairs * width * hidden,
+            transcendentals=0,
+        ),
+        compiler_params=pltpu.CompilerParams(vmem_limit_bytes=40 << 20),
+    )(named, rows, gain_row, *factors, *flat, *start, *after)
+
+
+def final_kernel(saved_ref, upstream_ref, *refs):
+    out_ref = refs[-1]
+    value = saved_ref[...].astype(jnp.float32)
+    inv_root = lax.rsqrt(jnp.mean(value * value, axis=1, keepdims=True) + epsilon)
+    scaled = refs[0][...].astype(jnp.float32)
+    for ref in refs[1:-1]:
+        scaled = scaled + ref[...].astype(jnp.float32)
+    unit = value * inv_root
+    mean = jnp.mean(scaled * unit, axis=1, keepdims=True)
+    layer_grad = upstream_ref[...].astype(jnp.float32) + inv_root * (scaled - unit * mean)
+    out_ref[...] = layer_grad.astype(jnp.bfloat16)
+
+
+def finish(saved_rows, upstream_rows, pieces):
+    return pl.pallas_call(
+        final_kernel,
+        in_specs=[in_vmem] * (2 + len(pieces)),
+        out_specs=in_vmem,
+        out_shape=jax.ShapeDtypeStruct(saved_rows.shape, jnp.bfloat16),
+        compiler_params=pltpu.CompilerParams(vmem_limit_bytes=24 << 20),
+    )(saved_rows, upstream_rows, *pieces)
+
+
+def line_device(
+    saved_input, upstream, norm_gain, gate_weight, up_weight, down_weight, expert_ids, gate_share
+):
+    own = (gate_weight[0, 0], up_weight[0, 0], down_weight[0, 0])
+    saved_rows, upstream_rows = saved_input[0], upstream[0]
+    experts = lax.axis_size("expert")
+    sections = lax.axis_size("section")
+    me = lax.axis_index("expert")
+    named = jnp.stack([me, me ^ 1]).astype(jnp.int32)
+    swapped = jnp.stack([me ^ 1, me]).astype(jnp.int32)
+
+    def hop(by):
+        return lambda value: lax.ppermute(value, "expert", [(i, i ^ by) for i in range(experts)])
+
+    def handed(by):
+        pairs = [
+            (s * experts + i, (s - 1) % sections * experts + (i ^ by))
+            for s in range(sections)
+            for i in range(experts)
+        ]
+        return lambda value: lax.ppermute(value, ("section", "expert"), pairs)
+
+    other = tuple(hop(1)(w) for w in own)
+    x_two, x_one = hop(4)(saved_rows), hop(2)(saved_rows)
+    shared = shared_rows(upstream_rows, expert_ids[0], gate_share[0], experts)
+    u_two, u_one = hop(4)(shared), hop(2)(shared)
+    x_three = hop(2)(x_two)
+    u_three = hop(2)(u_two)
+    next_saved, next_upstream = handed(0)(saved_rows), handed(0)(upstream_rows)
+
+    both = (own, other)
+    narrow = jnp.bfloat16
+    gain = norm_gain
+
+    def pieces_of(names, rows, factors, weights, kind=narrow, base=None, after=()):
+        return slot_pieces(names, rows, gain, factors, weights, experts, kind, base, after)
+
+    factors = slot_factors(saved_rows, gain, (own,), [])
+    here = pieces_of(named, shared, factors, (own,), jnp.float32)
+    factors = slot_factors(saved_rows, gain, (other,), [here])
+    here = pieces_of(swapped, shared, factors, (other,), narrow, here)
+    two_factors = slot_factors(x_two, gain, both, [here])
+    one_factors = slot_factors(x_one, gain, both, [two_factors[0]])
+    two = pieces_of(named, u_two, two_factors, both, after=[one_factors[0]])
+    one = pieces_of(named, u_one, one_factors, both, after=[two, next_saved])
+    here_next = handed(0)(here)
+    one_next = handed(2)(one)
+    two_next = handed(4)(two)
+    three_factors = slot_factors(x_three, gain, both, [one, next_upstream, here_next])
+    three = pieces_of(named, u_three, three_factors, both)
+    pieces = [here_next, one_next, two_next, handed(6)(three)]
+    return finish(next_saved, next_upstream, pieces)[None]
+
+
 def solution(mesh):
     placed = (
         P("section", "expert", None),
@@ -122,8 +355,9 @@
         P("section", "expert", None),
         P("section", "expert", None),
     )
+    plan = line_device if mesh.shape["expert"] == 8 else routed_device
     return jax.shard_map(
-        per_device,
+        plan,
         mesh=mesh,
         in_specs=placed,
         out_specs=P("section", "expert", None),

time: 277 us -> 127 us (0.46); the launches traced: 273 us -> 127 us
  waiting for transfers between devices: 135 us -> 28.6 us
  blocking collectives: 75.3 us -> 0 us
  Pallas kernels: 0 us -> 71.7 us
  matrix products: 41.3 us -> 0 us
  local copies, waits for them, and re-layouts: 2.29 us -> 8.07 us
  other arithmetic: 3.47 us -> 0.16 us
    all_to_all x2 -> x0, waiting for transfers between devices: 124 us -> none  [the longest x1 63 us: per_device(): lax.all_to_all(send_grads, 'expert', split_axis=0, concat_axis=0, tiled=T...]
    all_to_all x1 -> x0, blocking collectives: 75.3 us -> none  [per_device(): lax.all_to_all(result_rows.reshape(experts, slot_count, model_width), 'ex...]
    pallas_call x0 -> x12, Pallas kernels: none -> 71.7 us  [the longest x5 48.5 us: slot_pieces(): pl.pallas_call(functools.partial(pieces_kernel, experts, pairs, len(start...]
    dot_general x8 -> x0, matrix products: 41.3 us -> none  [the longest x1 12.7 us: expert_backward(): lax.dot_general(d_gate, gate_w, (((1,), (1,)), ((), ())), preferred_eleme...]
    ppermute x1 -> x15, waiting for transfers between devices: 10.8 us -> 28.6 us  [the longest x6 23.6 us: handed(): return lambda value: lax.ppermute(value, ('section', 'expert'), pairs)]
    ppermute x1 -> x15, starting transfers between devices: 2.51 us -> 18.1 us  [the longest x6 10.9 us: handed(): return lambda value: lax.ppermute(value, ('section', 'expert'), pairs)]
    all_to_all x2 -> x0, starting transfers between devices: 13.4 us -> none  [the longest x1 7.94 us: per_device(): lax.all_to_all(send_inputs, 'expert', split_axis=0, concat_axis=0, tiled=...]
    unnamed x10 -> x26, local copies, waits for them, and re-layouts: 2.02 us -> 8.07 us
  transfers between devices with their start and end apart: 3 -> 15, of which waited for: 3 -> 4; matrix products, arithmetic and copies ran while one was open for 4% -> 1% of each run, Pallas kernels for 0% -> 55%
where the time goes in v2:
time: 127 us
  Pallas kernels  71.7 us (56%)
  waiting for transfers between devices  28.6 us (23%)
  starting transfers between devices  18.1 us (14%)
  local copies, waits for them, and re-layouts  8.07 us (6%)
    pallas_call x5, Pallas kernels, slot_pieces(): pl.pallas_call(functools.partial(pieces_kernel, experts, pairs, len(start...  48.5 us
    ppermute x6, waiting for transfers between devices, handed(): return lambda value: lax.ppermute(value, ('section', 'expert'), pairs)  23.6 us
    pallas_call x5, Pallas kernels, slot_factors(): pl.pallas_call(functools.partial(factors_kernel, pairs), in_specs=[in_vme...  20.2 us
    ppermute x6, starting transfers between devices, handed(): return lambda value: lax.ppermute(value, ('section', 'expert'), pairs)  10.9 us
    unnamed x26, local copies, waits for them, and re-layouts  8.07 us
    ppermute x9, starting transfers between devices, hop(): lax.ppermute(value, 'expert', [(i, i ^ by) for i in range(experts)])  7.23 us
    ppermute x9, waiting for transfers between devices, hop(): lax.ppermute(value, 'expert', [(i, i ^ by) for i in range(experts)])  5.03 us
  transfers between devices with their start and end apart: 15, of which 4 were waited for; matrix products, arithmetic and copies ran while one was open for 1% of the time, Pallas kernels for 55%

profile of v2, /device:TPU:8, one launch (start us, length us, event | category | flops | bytes accessed | tf_op | source)
XLA Modules:
  0.0 126.8 jit_solution(16215565360346032670)
XLA Ops:
  0.0 0.0 collective-permute-start.2
  0.0 0.5 collective-permute-start.3
  0.5 2.6 %collective-permute-start.8 = (bf16[128,2048]{1,0:T(8,128)(2,1)}, bf16[128,2048]{1,0:T(8,128)(2,1)}, u32[]{:S(2)}, u32[]{:S(2)}) collective-permute-start(bf16[128,2048]{1,0:T(8,128)(2,1)} %bitcast.saved_ref), channel_id=1, source_target_pairs={{0,4},{1,5},{2,6},{3,7},{4,0},{5,1},{6,2},{7,3},{8,12},{9,13},{10,... | collective-permute-start | bytes 1572872 | tf_op jit(solution)/shard_map/ppermute | solution.py:305
  3.1 0.4 collective-permute-start.7
  3.6 0.8 copy.9
  4.3 0.8 copy.10
  5.1 1.3 %shard_map.82.rows_ref = bf16[128,2176]{1,0:T(8,128)(2,1)S(1)} custom-call(bf16[128,2048]{1,0:T(8,128)(2,1)} %bitcast.1.upstream_ref, s32[128,4]{1,0:T(8,128)S(1)} %bitcast.33, f32[128,4]{1,0:T(8,128)S(1)} %bitcast.34), custom_call_target="tpu_custom_call" | custom-call | tf_op jit(solution)/shard_map/pallas_call | solution.py:146
  6.4 0.1 pad_add_fusion.1.named_ref
  6.5 1.9 %copy-done = bf16[1,1,2048,768]{3,2,1,0:T(8,128)(2,1)S(1)} copy-done((bf16[1,1,2048,768]{3,2,1,0:T(8,128)(2,1)S(1)}, bf16[1,1,2048,768]{3,2,1,0:T(8,128)(2,1)}, u32[]{:S(2)}) %copy-start) | copy-done | bytes 3145752
  8.4 1.9 %copy-done.2 = bf16[1,1,2048,768]{3,2,1,0:T(8,128)(2,1)S(1)} copy-done((bf16[1,1,2048,768]{3,2,1,0:T(8,128)(2,1)S(1)}, bf16[1,1,2048,768]{3,2,1,0:T(8,128)(2,1)}, u32[]{:S(2)}) %copy-start.2) | copy-done | bytes 3145752
  10.3 0.7 copy-done.8
  11.0 2.8 %shard_map.83 = (f32[1,128,768]{2,1,0:T(8,128)S(1)}, f32[1,128,768]{2,1,0:T(8,128)S(1)}) custom-call(bf16[128,2048]{1,0:T(8,128)(2,1)} %bitcast.saved_ref, f32[1,2048]{1,0:T(1,128)S(1)} %copy-done.8, bf16[2048,768]{1,0:T(8,128)(2,1)S(1)} %bitcast.11, bf16[2048,768]{1,0:T(8,128)(2,1)S(1)} %bitcast.20), custom_call_target="tpu_custom_call" | custom-call | flops 1610612736 | bytes 6291456 | tf_op jit(solution)/shard_map/pallas_call | solution.py:186
  13.8 0.1 copy-done.6
  14.0 5.2 %shard_map.84.refs_2_.refs_3_ = f32[128,2048]{1,0:T(8,128)S(1)} custom-call(s32[2]{0:T(128)S(1)} %pad_add_fusion.1.named_ref, bf16[128,2176]{1,0:T(8,128)(2,1)S(1)} %shard_map.82.rows_ref, f32[1,2048]{1,0:T(1,128)S(1)} %copy-done.8, f32[1,128,768]{2,1,0:T(8,128)S(1)} %get-tuple-element.15.gate_ref, f32[1,128,768]{2,1,0:T(8,128)S(1)} %get-tuple-element.16.up_ref, ...), custom_call_target="tpu_custom_call" | custom-call | flops 2415919104 | bytes 9437184 | tf_op jit(solution)/shard_map/pallas_call | solution.py:253
  19.2 0.1 pad_add_fusion.named_ref
  19.3 0.0 collective-permute-start.9
  19.4 0.0 collective-permute-done.3.refs_1_.refs_3_.refs_4_
  19.4 2.7 %collective-permute-start = (bf16[128,2048]{1,0:T(8,128)(2,1)}, bf16[128,2048]{1,0:T(8,128)(2,1)S(1)}, u32[]{:S(2)}, u32[]{:S(2)}) collective-permute-start(bf16[128,2048]{1,0:T(8,128)(2,1)} %bitcast.saved_ref), channel_id=1, source_target_pairs={{0,24},{1,25},{2,26},{3,27},{4,28},{5,29},{6,30},{7,31},{8,0},{9,1... | collective-permute-start | bytes 1572872 | tf_op jit(solution)/shard_map/ppermute | solution.py:313
  22.1 3.7 %shard_map.85 = (f32[1,128,768]{2,1,0:T(8,128)S(1)}, f32[1,128,768]{2,1,0:T(8,128)S(1)}) custom-call(bf16[128,2048]{1,0:T(8,128)(2,1)} %bitcast.saved_ref, f32[1,2048]{1,0:T(1,128)S(1)} %copy-done.8, bf16[2048,768]{1,0:T(8,128)(2,1)S(1)} %collective-permute-done.2.refs_0_.refs_2_.refs_3_, bf16[2048,768]{1,0:T(8,128)(2,1)} %collective-permute-done.3.refs_1_.refs_3_.refs_4_, ...), custom_call_target="tpu_custom_call" | custom-call | flops 1610612736 | bytes 6291456 | tf_op jit(solution)/shard_map/pallas_call | solution.py:186
  25.8 0.0 collective-permute-done.4.refs_2_.refs_5_
  25.8 1.7 %collective-permute-start.6 = (bf16[128,2176]{1,0:T(8,128)(2,1)S(1)}, bf16[128,2176]{1,0:T(8,128)(2,1)S(1)}, u32[]{:S(2)}, u32[]{:S(2)}) collective-permute-start(bf16[128,2176]{1,0:T(8,128)(2,1)S(1)} %shard_map.82.rows_ref), channel_id=1, source_target_pairs={{0,2},{1,3},{2,0},{3,1},{4,6},{5,7},{6,4},{7,5},{8,10},{9,11},{10,... | collective-permute-start | bytes 1671176 | tf_op jit(solution)/shard_map/ppermute | solution.py:305
  27.5 8.5 %shard_map.86.refs_4_ = bf16[128,2048]{1,0:T(8,128)(2,1)} custom-call(s32[2]{0:T(128)S(1)} %pad_add_fusion.named_ref, bf16[128,2176]{1,0:T(8,128)(2,1)S(1)} %shard_map.82.rows_ref, f32[1,2048]{1,0:T(1,128)S(1)} %copy-done.8, f32[1,128,768]{2,1,0:T(8,128)S(1)} %get-tuple-element.17.gate_ref, f32[1,128,768]{2,1,0:T(8,128)S(1)} %get-tuple-element.18.up_ref, ...), custom_call_target="tpu_custom_call" | custom-call | flops 2415919104 | bytes 9437184 | tf_op jit(solution)/shard_map/pallas_call | solution.py:253
  36.0 0.0 collective-permute-done.8.saved_ref
  36.0 0.7 collective-permute-start.1
  36.7 4.6 %shard_map.87 = (f32[2,128,768]{2,1,0:T(8,128)S(1)}, f32[2,128,768]{2,1,0:T(8,128)S(1)}) custom-call(bf16[128,2048]{1,0:T(8,128)(2,1)} %collective-permute-done.8.saved_ref, f32[1,2048]{1,0:T(1,128)S(1)} %copy-done.8, bf16[2048,768]{1,0:T(8,128)(2,1)S(1)} %bitcast.13, bf16[2048,768]{1,0:T(8,128)(2,1)S(1)} %bitcast.22, ...), custom_call_target="tpu_custom_call" | custom-call | flops 3221225472 | bytes 12582912 | tf_op jit(solution)/shard_map/pallas_call | solution.py:186
  41.3 0.5 collective-permute-start.13
  41.8 4.7 %shard_map.88 = (f32[2,128,768]{2,1,0:T(8,128)S(1)}, f32[2,128,768]{2,1,0:T(8,128)S(1)}) custom-call(bf16[128,2048]{1,0:T(8,128)(2,1)} %collective-permute-done.7.saved_ref, f32[1,2048]{1,0:T(1,128)S(1)} %copy-done.8, bf16[2048,768]{1,0:T(8,128)(2,1)S(1)} %bitcast.14, bf16[2048,768]{1,0:T(8,128)(2,1)S(1)} %bitcast.23, ...), custom_call_target="tpu_custom_call" | custom-call | flops 3221225472 | bytes 12582912 | tf_op jit(solution)/shard_map/pallas_call | solution.py:186
  46.5 3.7 %collective-permute-done.9.rows_ref = bf16[128,2176]{1,0:T(8,128)(2,1)S(1)} collective-permute-done((bf16[128,2176]{1,0:T(8,128)(2,1)S(1)}, bf16[128,2176]{1,0:T(8,128)(2,1)S(1)}, u32[]{:S(2)}, u32[]{:S(2)}) %collective-permute-start.9) | collective-permute-done | bytes 557088 | tf_op jit(solution)/shard_map/ppermute | solution.py:305
  50.2 2.4 %collective-permute-start.5 = (bf16[128,2048]{1,0:T(8,128)(2,1)}, bf16[128,2048]{1,0:T(8,128)(2,1)S(1)}, u32[]{:S(2)}, u32[]{:S(2)}) collective-permute-start(bf16[128,2048]{1,0:T(8,128)(2,1)} %shard_map.86.refs_4_), channel_id=1, source_target_pairs={{0,24},{1,25},{2,26},{3,27},{4,28},{5,29},{6,30},{7,31},{8,0},{9,1... | collective-permute-start | bytes 1572872 | tf_op jit(solution)/shard_map/ppermute | solution.py:313
  52.7 11.6 %shard_map.89.refs_6_ = bf16[128,2048]{1,0:T(8,128)(2,1)S(1)} custom-call(s32[2]{0:T(128)S(1)} %pad_add_fusion.1.named_ref, bf16[128,2176]{1,0:T(8,128)(2,1)S(1)} %collective-permute-done.9.rows_ref, f32[1,2048]{1,0:T(1,128)S(1)} %copy-done.8, f32[2,128,768]{2,1,0:T(8,128)S(1)} %get-tuple-element.19.refs_4_.gate_ref, ...), custom_call_target="tpu_custom_call" | custom-call | flops 4831838208 | bytes 18874368 | tf_op jit(solution)/shard_map/pallas_call | solution.py:253
  64.3 1.5 %collective-permute-start.12 = (bf16[128,2176]{1,0:T(8,128)(2,1)S(1)}, bf16[128,2176]{1,0:T(8,128)(2,1)S(1)}, u32[]{:S(2)}, u32[]{:S(2)}) collective-permute-start(bf16[128,2176]{1,0:T(8,128)(2,1)S(1)} %collective-permute-done.9.rows_ref), channel_id=1, source_target_pairs={{0,2},{1,3},{2,0},{3,1},{4,6},{5,7},{6,4},{7,5},{8,10},{9,11},{10,... | collective-permute-start | bytes 1671176 | tf_op jit(solution)/shard_map/ppermute | solution.py:305
  65.8 0.0 collective-permute-done.6.rows_ref
  65.8 0.8 copy-done.10
  66.6 2.0 %collective-permute-start.11 = (bf16[128,2048]{1,0:T(8,128)(2,1)S(1)}, bf16[128,2048]{1,0:T(8,128)(2,1)S(1)}, u32[]{:S(2)}, u32[]{:S(2)}) collective-permute-start(bf16[128,2048]{1,0:T(8,128)(2,1)S(1)} %shard_map.89.refs_6_), channel_id=1, source_target_pairs={{0,28},{1,29},{2,30},{3,31},{4,24},{5,25},{6,26},{7,27},{8,4},{9,5... | collective-permute-start | bytes 1572872 | tf_op jit(solution)/shard_map/ppermute | solution.py:313
  68.5 1.1 copy-done.11
  69.6 11.7 %shard_map.90.refs_4_ = bf16[128,2048]{1,0:T(8,128)(2,1)S(1)} custom-call(s32[2]{0:T(128)S(1)} %pad_add_fusion.1.named_ref, bf16[128,2176]{1,0:T(8,128)(2,1)S(1)} %copy-done.11, f32[1,2048]{1,0:T(1,128)S(1)} %copy-done.9, f32[2,128,768]{2,1,0:T(8,128)S(1)} %get-tuple-element.20.refs_6_.gate_ref, f32[2,128,768]{2,1,0:T(8,128)S(1)} %get-tuple-element.21.up_ref, ...), custom_call_target="tpu_custom_call" | custom-call | flops 4831838208 | bytes 18874368 | tf_op jit(solution)/shard_map/pallas_call | solution.py:253
  81.3 0.0 collective-permute-done.1.refs_5_.upstream_ref
  81.3 2.9 %collective-permute-start.10 = (bf16[128,2048]{1,0:T(8,128)(2,1)S(1)}, bf16[128,2048]{1,0:T(8,128)(2,1)S(1)}, u32[]{:S(2)}, u32[]{:S(2)}) collective-permute-start(bf16[128,2048]{1,0:T(8,128)(2,1)S(1)} %shard_map.90.refs_4_), channel_id=1, source_target_pairs={{0,26},{1,27},{2,24},{3,25},{4,30},{5,31},{6,28},{7,29},{8,2},{9,3... | collective-permute-start | bytes 1572872 | tf_op jit(solution)/shard_map/ppermute | solution.py:313
  84.2 0.0 collective-permute-done.13.saved_ref
  84.2 0.0 collective-permute-done.5.refs_6_.refs_0_
  84.2 4.4 %shard_map.91 = (f32[2,128,768]{2,1,0:T(8,128)S(1)}, f32[2,128,768]{2,1,0:T(8,128)S(1)}) custom-call(bf16[128,2048]{1,0:T(8,128)(2,1)S(1)} %collective-permute-done.13.saved_ref, f32[1,2048]{1,0:T(1,128)S(1)} %copy-done.9, bf16[2048,768]{1,0:T(8,128)(2,1)S(1)} %bitcast.17, bf16[2048,768]{1,0:T(8,128)(2,1)S(1)} %bitcast.26, bf16[2048,768]{1,0:T(8,128)(2,1)S(1)} %copy-done.5, ...), custom_call_target="tpu_custom_call" | custom-call | flops 3221225472 | bytes 12582912 | tf_op jit(solution)/shard_map/pallas_call | solution.py:186
  88.7 1.3 collective-permute-done.12.rows_ref
  89.9 11.5 %shard_map.92 = bf16[128,2048]{1,0:T(8,128)(2,1)S(1)} custom-call(s32[2]{0:T(128)S(1)} %pad_add_fusion.1.named_ref, bf16[128,2176]{1,0:T(8,128)(2,1)S(1)} %collective-permute-done.12.rows_ref, f32[1,2048]{1,0:T(1,128)S(1)} %copy-done.9, f32[2,128,768]{2,1,0:T(8,128)S(1)} %get-tuple-element.23.gate_ref, f32[2,128,768]{2,1,0:T(8,128)S(1)} %get-tuple-element.24.up_ref, ...), custom_call_target="tpu_custom_call" | custom-call | flops 4831838208 | bytes 18874368 | tf_op jit(solution)/shard_map/pallas_call | solution.py:253
  101.5 0.1 collective-permute-start.14
  101.6 0.3 collective-permute-done.10.refs_1_
  101.9 0.0 collective-permute-done.11.refs_2_
  101.9 23.3 %collective-permute-done.14.refs_3_ = bf16[128,2048]{1,0:T(8,128)(2,1)S(1)} collective-permute-done((bf16[128,2048]{1,0:T(8,128)(2,1)S(1)}, bf16[128,2048]{1,0:T(8,128)(2,1)S(1)}, u32[]{:S(2)}, u32[]{:S(2)}) %collective-permute-start.14) | collective-permute-done | bytes 524320 | tf_op jit(solution)/shard_map/ppermute | solution.py:313
  125.2 1.6 %shard_map.93 = bf16[128,2048]{1,0:T(8,128)(2,1)} custom-call(bf16[128,2048]{1,0:T(8,128)(2,1)S(1)} %collective-permute-done.refs_7_.saved_ref, bf16[128,2048]{1,0:T(8,128)(2,1)S(1)} %collective-permute-done.1.refs_5_.upstream_ref, bf16[128,2048]{1,0:T(8,128)(2,1)S(1)} %collective-permute-done.5.refs_6_.refs_0_, ...), custom_call_target="tpu_custom_call" | custom-call | tf_op jit(solution)/shard_map/pallas_call | solution.py:284
  (22 shorter events, 0.0 us)
Async XLA Ops:
  0.0 19.3 %collective-permute-start.2 = (bf16[2048,768]{1,0:T(8,128)(2,1)}, bf16[2048,768]{1,0:T(8,128)(2,1)S(1)}, u32[]{:S(2)}, u32[]{:S(2)}) collective-permute-start(bf16[2048,768]{1,0:T(8,128)(2,1)} %bitcast.10), channel_id=1, source_target_pairs={{0,1},{1,0},{2,3},{3,2},{4,5},{5,4},{6,7},{7,6},{8,9},{9,8},{10,11... | collective-permute-start | bytes 9437192 | tf_op jit(solution)/shard_map/ppermute | solution.py:305
  0.0 19.4 %collective-permute-start.3 = (bf16[2048,768]{1,0:T(8,128)(2,1)}, bf16[2048,768]{1,0:T(8,128)(2,1)}, u32[]{:S(2)}, u32[]{:S(2)}) collective-permute-start(bf16[2048,768]{1,0:T(8,128)(2,1)} %bitcast.19), channel_id=1, source_target_pairs={{0,1},{1,0},{2,3},{3,2},{4,5},{5,4},{6,7},{7,6},{8,9},{9,8},{10,11... | collective-permute-start | bytes 9437192 | tf_op jit(solution)/shard_map/ppermute | solution.py:305
  0.5 25.3 %collective-permute-start.4 = (bf16[768,2048]{1,0:T(8,128)(2,1)}, bf16[768,2048]{1,0:T(8,128)(2,1)}, u32[]{:S(2)}, u32[]{:S(2)}) collective-permute-start(bf16[768,2048]{1,0:T(8,128)(2,1)} %bitcast.28), channel_id=1, source_target_pairs={{0,1},{1,0},{2,3},{3,2},{4,5},{5,4},{6,7},{7,6},{8,9},{9,8},{10,11... | collective-permute-start | bytes 9437192 | tf_op jit(solution)/shard_map/ppermute | solution.py:305
  0.5 35.5 %collective-permute-start.8 = (bf16[128,2048]{1,0:T(8,128)(2,1)}, bf16[128,2048]{1,0:T(8,128)(2,1)}, u32[]{:S(2)}, u32[]{:S(2)}) collective-permute-start(bf16[128,2048]{1,0:T(8,128)(2,1)} %bitcast.saved_ref), channel_id=1, source_target_pairs={{0,4},{1,5},{2,6},{3,7},{4,0},{5,1},{6,2},{7,3},{8,12},{9,13},{10,... | collective-permute-start | bytes 1572872 | tf_op jit(solution)/shard_map/ppermute | solution.py:305
  3.1 38.2 %collective-permute-start.7 = (bf16[128,2048]{1,0:T(8,128)(2,1)}, bf16[128,2048]{1,0:T(8,128)(2,1)}, u32[]{:S(2)}, u32[]{:S(2)}) collective-permute-start(bf16[128,2048]{1,0:T(8,128)(2,1)} %bitcast.saved_ref), channel_id=1, source_target_pairs={{0,2},{1,3},{2,0},{3,1},{4,6},{5,7},{6,4},{7,5},{8,10},{9,11},{10,... | collective-permute-start | bytes 1572872 | tf_op jit(solution)/shard_map/ppermute | solution.py:305
  6.5 1.9 %copy-start = (bf16[1,1,2048,768]{3,2,1,0:T(8,128)(2,1)S(1)}, bf16[1,1,2048,768]{3,2,1,0:T(8,128)(2,1)}, u32[]{:S(2)}) copy-start(bf16[1,1,2048,768]{3,2,1,0:T(8,128)(2,1)} %param.11) | copy-start | bytes 9437188
  8.4 1.9 %copy-start.2 = (bf16[1,1,2048,768]{3,2,1,0:T(8,128)(2,1)S(1)}, bf16[1,1,2048,768]{3,2,1,0:T(8,128)(2,1)}, u32[]{:S(2)}) copy-start(bf16[1,1,2048,768]{3,2,1,0:T(8,128)(2,1)} %param.12) | copy-start | bytes 9437188
  10.3 0.7 copy-start.8
  11.0 2.8 %copy-start.1 = (bf16[1,1,2048,768]{3,2,1,0:T(8,128)(2,1)S(1)}, bf16[1,1,2048,768]{3,2,1,0:T(8,128)(2,1)}, u32[]{:S(2)}) copy-start(bf16[1,1,2048,768]{3,2,1,0:T(8,128)(2,1)} %param.11) | copy-start | bytes 9437188
  11.0 3.0 %copy-start.6 = (bf16[1,1,768,2048]{3,2,1,0:T(8,128)(2,1)S(1)}, bf16[1,1,768,2048]{3,2,1,0:T(8,128)(2,1)}, u32[]{:S(2)}) copy-start(bf16[1,1,768,2048]{3,2,1,0:T(8,128)(2,1)} %param.13) | copy-start | bytes 9437188
  19.3 22.5 %copy-start.4 = (bf16[2048,768]{1,0:T(8,128)(2,1)}, bf16[2048,768]{1,0:T(8,128)(2,1)S(1)}, u32[]{:S(2)}) copy-start(bf16[2048,768]{1,0:T(8,128)(2,1)S(1)} %collective-permute-done.2.refs_0_.refs_2_.refs_3_) | copy-start | bytes 9437188
  19.3 30.9 %collective-permute-start.9 = (bf16[128,2176]{1,0:T(8,128)(2,1)S(1)}, bf16[128,2176]{1,0:T(8,128)(2,1)S(1)}, u32[]{:S(2)}, u32[]{:S(2)}) collective-permute-start(bf16[128,2176]{1,0:T(8,128)(2,1)S(1)} %shard_map.82.rows_ref), channel_id=1, source_target_pairs={{0,4},{1,5},{2,6},{3,7},{4,0},{5,1},{6,2},{7,3},{8,12},{9,13},{10,... | collective-permute-start | bytes 1671176 | tf_op jit(solution)/shard_map/ppermute | solution.py:305
  19.4 44.9 %collective-permute-start = (bf16[128,2048]{1,0:T(8,128)(2,1)}, bf16[128,2048]{1,0:T(8,128)(2,1)S(1)}, u32[]{:S(2)}, u32[]{:S(2)}) collective-permute-start(bf16[128,2048]{1,0:T(8,128)(2,1)} %bitcast.saved_ref), channel_id=1, source_target_pairs={{0,24},{1,25},{2,26},{3,27},{4,28},{5,29},{6,30},{7,31},{8,0},{9,1... | collective-permute-start | bytes 1572872 | tf_op jit(solution)/shard_map/ppermute | solution.py:313
  25.8 39.9 %collective-permute-start.6 = (bf16[128,2176]{1,0:T(8,128)(2,1)S(1)}, bf16[128,2176]{1,0:T(8,128)(2,1)S(1)}, u32[]{:S(2)}, u32[]{:S(2)}) collective-permute-start(bf16[128,2176]{1,0:T(8,128)(2,1)S(1)} %shard_map.82.rows_ref), channel_id=1, source_target_pairs={{0,2},{1,3},{2,0},{3,1},{4,6},{5,7},{6,4},{7,5},{8,10},{9,11},{10,... | collective-permute-start | bytes 1671176 | tf_op jit(solution)/shard_map/ppermute | solution.py:305
  27.5 9.2 %copy-start.3 = (bf16[1,1,2048,768]{3,2,1,0:T(8,128)(2,1)S(1)}, bf16[1,1,2048,768]{3,2,1,0:T(8,128)(2,1)}, u32[]{:S(2)}) copy-start(bf16[1,1,2048,768]{3,2,1,0:T(8,128)(2,1)} %param.12) | copy-start | bytes 9437188
  36.0 45.3 %collective-permute-start.1 = (bf16[128,2048]{1,0:T(8,128)(2,1)}, bf16[128,2048]{1,0:T(8,128)(2,1)S(1)}, u32[]{:S(2)}, u32[]{:S(2)}) collective-permute-start(bf16[128,2048]{1,0:T(8,128)(2,1)} %bitcast.1.upstream_ref), channel_id=1, source_target_pairs={{0,24},{1,25},{2,26},{3,27},{4,28},{5,29},{6,30},{7,31},{8,0},{9,1... | collective-permute-start | bytes 1572872 | tf_op jit(solution)/shard_map/ppermute | solution.py:313
  41.3 42.9 %collective-permute-start.13 = (bf16[128,2048]{1,0:T(8,128)(2,1)}, bf16[128,2048]{1,0:T(8,128)(2,1)S(1)}, u32[]{:S(2)}, u32[]{:S(2)}) collective-permute-start(bf16[128,2048]{1,0:T(8,128)(2,1)} %collective-permute-done.8.saved_ref), channel_id=1, source_target_pairs={{0,2},{1,3},{2,0},{3,1},{4,6},{5,7},{6,4},{7,5},{8,10},{9,11},{10,... | collective-permute-start | bytes 1572872 | tf_op jit(solution)/shard_map/ppermute | solution.py:305
  41.8 10.9 %copy-start.7 = (bf16[1,1,768,2048]{3,2,1,0:T(8,128)(2,1)S(1)}, bf16[1,1,768,2048]{3,2,1,0:T(8,128)(2,1)}, u32[]{:S(2)}) copy-start(bf16[1,1,768,2048]{3,2,1,0:T(8,128)(2,1)} %param.13) | copy-start | bytes 9437188
  50.2 34.0 %collective-permute-start.5 = (bf16[128,2048]{1,0:T(8,128)(2,1)}, bf16[128,2048]{1,0:T(8,128)(2,1)S(1)}, u32[]{:S(2)}, u32[]{:S(2)}) collective-permute-start(bf16[128,2048]{1,0:T(8,128)(2,1)} %shard_map.86.refs_4_), channel_id=1, source_target_pairs={{0,24},{1,25},{2,26},{3,27},{4,28},{5,29},{6,30},{7,31},{8,0},{9,1... | collective-permute-start | bytes 1572872 | tf_op jit(solution)/shard_map/ppermute | solution.py:313
  52.7 15.8 %copy-start.9 = (f32[1,2048]{1,0:T(1,128)S(1)}, f32[1,2048]{1,0:T(1,128)}, u32[]{:S(2)}) copy-start(f32[1,2048]{1,0:T(1,128)} %gain_ref.19) | copy-start | bytes 24580
  64.3 25.7 %collective-permute-start.12 = (bf16[128,2176]{1,0:T(8,128)(2,1)S(1)}, bf16[128,2176]{1,0:T(8,128)(2,1)S(1)}, u32[]{:S(2)}, u32[]{:S(2)}) collective-permute-start(bf16[128,2176]{1,0:T(8,128)(2,1)S(1)} %collective-permute-done.9.rows_ref), channel_id=1, source_target_pairs={{0,2},{1,3},{2,0},{3,1},{4,6},{5,7},{6,4},{7,5},{8,10},{9,11},{10,... | collective-permute-start | bytes 1671176 | tf_op jit(solution)/shard_map/ppermute | solution.py:305
  65.8 0.8 copy-start.10
  66.6 35.3 %collective-permute-start.11 = (bf16[128,2048]{1,0:T(8,128)(2,1)S(1)}, bf16[128,2048]{1,0:T(8,128)(2,1)S(1)}, u32[]{:S(2)}, u32[]{:S(2)}) collective-permute-start(bf16[128,2048]{1,0:T(8,128)(2,1)S(1)} %shard_map.89.refs_6_), channel_id=1, source_target_pairs={{0,28},{1,29},{2,30},{3,31},{4,24},{5,25},{6,26},{7,27},{8,4},{9,5... | collective-permute-start | bytes 1572872 | tf_op jit(solution)/shard_map/ppermute | solution.py:313
  68.5 1.1 copy-start.11
  69.6 14.6 %copy-start.5 = (bf16[2048,768]{1,0:T(8,128)(2,1)S(1)}, bf16[2048,768]{1,0:T(8,128)(2,1)}, u32[]{:S(2)}) copy-start(bf16[2048,768]{1,0:T(8,128)(2,1)} %copy-done.4) | copy-start | bytes 9437188
  81.3 20.6 %collective-permute-start.10 = (bf16[128,2048]{1,0:T(8,128)(2,1)S(1)}, bf16[128,2048]{1,0:T(8,128)(2,1)S(1)}, u32[]{:S(2)}, u32[]{:S(2)}) collective-permute-start(bf16[128,2048]{1,0:T(8,128)(2,1)S(1)} %shard_map.90.refs_4_), channel_id=1, source_target_pairs={{0,26},{1,27},{2,24},{3,25},{4,30},{5,31},{6,28},{7,29},{8,2},{9,3... | collective-permute-start | bytes 1572872 | tf_op jit(solution)/shard_map/ppermute | solution.py:313
  101.5 23.7 %collective-permute-start.14 = (bf16[128,2048]{1,0:T(8,128)(2,1)S(1)}, bf16[128,2048]{1,0:T(8,128)(2,1)S(1)}, u32[]{:S(2)}, u32[]{:S(2)}) collective-permute-start(bf16[128,2048]{1,0:T(8,128)(2,1)S(1)} %shard_map.92), channel_id=1, source_target_pairs={{0,30},{1,31},{2,28},{3,29},{4,26},{5,27},{6,24},{7,25},{8,6},{9,7... | collective-permute-start | bytes 1572872 | tf_op jit(solution)/shard_map/ppermute | solution.py:313

commit v3 on v2

--- a/solution.py
+++ b/solution.py
@@ -115,7 +115,6 @@
 
 
 tile = 256
-last_dims = (((1,), (1,)), ((), ()))
 in_vmem = pl.BlockSpec(memory_space=pltpu.VMEM)
 in_smem = pl.BlockSpec(memory_space=pltpu.SMEM)
 anywhere = pl.BlockSpec(memory_space=pl.ANY)
@@ -148,7 +147,7 @@
         in_specs=[in_vmem] * 3,
         out_specs=in_vmem,
         out_shape=jax.ShapeDtypeStruct((count, width + 128), jnp.bfloat16),
-        compiler_params=pltpu.CompilerParams(vmem_limit_bytes=16 << 20),
+        compiler_params=pltpu.CompilerParams(vmem_limit_bytes=8 << 20),
     )(upstream_rows, routed, shares)
 
 
@@ -194,30 +193,88 @@
             bytes_accessed=4 * pairs * width * hidden,
             transcendentals=pairs * count * hidden,
         ),
-        compiler_params=pltpu.CompilerParams(vmem_limit_bytes=40 << 20),
+        compiler_params=pltpu.CompilerParams(vmem_limit_bytes=8 << 20),
     )(rows, gain_row, *flat, *after)
 
 
-def pieces_kernel(experts, pairs, start, named_ref, rows_ref, gain_ref, gate_ref, up_ref, *refs):
-    weight_refs, refs = refs[: 3 * pairs], refs[3 * pairs :]
+def share_of(rows_ref, width, experts, named):
+    parts = rows_ref[:, width:].astype(jnp.float32)
+    lane = lax.broadcasted_iota(jnp.int32, parts.shape, 1)
+    wanted = (lax.rem(lane, experts) == named) & (lane < 3 * experts)
+    return jnp.sum(jnp.where(wanted, parts, 0.0), axis=1, keepdims=True)
+
+
+def turning_kernel(experts, start, named_ref, rows_ref, gain_ref, gate_ref, up_ref, *refs):
+    weight_refs, refs = refs[:3], refs[3:]
     base_ref = refs[0] if start else None
+    out_ref, gate_turned, up_turned, down_turned, gate_grads, up_grads = refs[-6:]
+    width = out_ref.shape[1]
+    hidden = gate_ref.shape[2]
+    share = share_of(rows_ref, width, experts, named_ref[0])
+
+    def grads_of(step, carry):
+        cut = tile_cut(step)
+        turned = weight_refs[2][cut, :].T
+        down_turned[:, cut] = turned
+        grad = jnp.dot(rows_ref[:, :width], turned, preferred_element_type=jnp.float32)
+        grad = grad * share
+        gate_grads[:, cut] = (grad * gate_ref[0, :, cut]).astype(jnp.bfloat16)
+        up_grads[:, cut] = (grad * up_ref[0, :, cut]).astype(jnp.bfloat16)
+        return carry
+
+    lax.fori_loop(0, hidden // tile, grads_of, 0)
+
+    def pieces_of(step, carry):
+        cut = tile_cut(step)
+        gate_tile = weight_refs[0][cut, :].T
+        up_tile = weight_refs[1][cut, :].T
+        gate_turned[:, cut] = gate_tile
+        up_turned[:, cut] = up_tile
+        total = jnp.dot(gate_grads[...], gate_tile, preferred_element_type=jnp.float32)
+        total = total + jnp.dot(up_grads[...], up_tile, preferred_element_type=jnp.float32)
+        total = total * gain_ref[:, cut]
+        if start:
+            total = total + base_ref[:, cut]
+        out_ref[:, cut] = total.astype(out_ref.dtype)
+        return carry
+
+    lax.fori_loop(0, width // tile, pieces_of, 0)
+
+
+def turning_pieces(named, rows, gain_row, factors, weights, experts, kind, base):
+    _, count, hidden = factors[0].shape
+    width = weights[0].shape[0]
+    start = [] if base is None else [base]
+    turned = jax.ShapeDtypeStruct((hidden, width), jnp.bfloat16)
+    down_turned = jax.ShapeDtypeStruct((width, hidden), jnp.bfloat16)
+    return pl.pallas_call(
+        functools.partial(turning_kernel, experts, len(start)),
+        in_specs=[in_smem] + [in_vmem] * (7 + len(start)),
+        out_specs=[in_vmem] * 4,
+        out_shape=[jax.ShapeDtypeStruct((count, width), kind), turned, turned, down_turned],
+        scratch_shapes=[pltpu.VMEM((count, hidden), jnp.bfloat16)] * 2,
+        cost_estimate=pl.CostEstimate(
+            flops=12 * count * width * hidden,
+            bytes_accessed=6 * width * hidden,
+            transcendentals=0,
+        ),
+        compiler_params=pltpu.CompilerParams(vmem_limit_bytes=12 << 20),
+    )(named, rows, gain_row, *factors, *weights, *start)
+
+
+def pieces_kernel(experts, pairs, named_ref, rows_ref, gain_ref, gate_ref, up_ref, *refs):
+    weight_refs = refs[: 3 * pairs]
     out_ref, gate_grads, up_grads = refs[-3:]
     width = out_ref.shape[1]
     hidden = gate_ref.shape[2]
-    parts = rows_ref[:, width:].astype(jnp.float32)
-    lane = lax.broadcasted_iota(jnp.int32, parts.shape, 1)
-    shares = []
-    for w in range(pairs):
-        wanted = (lax.rem(lane, experts) == named_ref[w]) & (lane < 3 * experts)
-        shares.append(jnp.sum(jnp.where(wanted, parts, 0.0), axis=1, keepdims=True))
+    shares = [share_of(rows_ref, width, experts, named_ref[w]) for w in range(pairs)]
 
     def grads_of(step, carry):
         cut = tile_cut(step)
         for w in range(pairs):
-            grad = lax.dot_general(
+            grad = jnp.dot(
                 rows_ref[:, :width],
-                weight_refs[3 * w + 2][cut, :],
-                last_dims,
+                weight_refs[3 * w + 2][:, cut],
                 preferred_element_type=jnp.float32,
             )
             grad = grad * shares[w]
@@ -232,39 +289,31 @@
         total = None
         for w in range(pairs):
             for held, weight_ref in ((gate_grads, weight_refs[3 * w]), (up_grads, weight_refs[3 * w + 1])):
-                part = lax.dot_general(
-                    held[w], weight_ref[cut, :], last_dims, preferred_element_type=jnp.float32
-                )
+                part = jnp.dot(held[w], weight_ref[:, cut], preferred_element_type=jnp.float32)
                 total = part if total is None else total + part
-        total = total * gain_ref[:, cut]
-        if start:
-            total = total + base_ref[:, cut]
-        out_ref[:, cut] = total.astype(out_ref.dtype)
+        out_ref[:, cut] = (total * gain_ref[:, cut]).astype(out_ref.dtype)
         return carry
 
     lax.fori_loop(0, width // tile, pieces_of, 0)
 
 
-def slot_pieces(named, rows, gain_row, factors, weights, experts, kind, base, after):
+def slot_pieces(named, rows, gain_row, factors, weights, experts, after):
     pairs, count, hidden = factors[0].shape
-    width = weights[0][0].shape[0]
+    width = weights[0][0].shape[1]
     flat = [w for group in weights for w in group]
-    start = [] if base is None else [base]
-    return pl.pallas_call(
-        functools.partial(pieces_kernel, experts, pairs, len(start)),
-        in_specs=[in_smem]
-        + [in_vmem] * (4 + len(flat) + len(start))
-        + [anywhere] * len(after),
+    return pl.pallas_call(
+        functools.partial(pieces_kernel, experts, pairs),
+        in_specs=[in_smem] + [in_vmem] * (4 + len(flat)) + [anywhere] * len(after),
         out_specs=in_vmem,
-        out_shape=jax.ShapeDtypeStruct((count, width), kind),
+        out_shape=jax.ShapeDtypeStruct((count, width), jnp.bfloat16),
         scratch_shapes=[pltpu.VMEM((pairs, count, hidden), jnp.bfloat16)] * 2,
         cost_estimate=pl.CostEstimate(
             flops=12 * pairs * count * width * hidden,
             bytes_accessed=6 * pairs * width * hidden,
             transcendentals=0,
         ),
-        compiler_params=pltpu.CompilerParams(vmem_limit_bytes=40 << 20),
-    )(named, rows, gain_row, *factors, *flat, *start, *after)
+        compiler_params=pltpu.CompilerParams(vmem_limit_bytes=8 << 20),
+    )(named, rows, gain_row, *factors, *flat, *after)
 
 
 def final_kernel(saved_ref, upstream_ref, *refs):
@@ -286,8 +335,26 @@
         in_specs=[in_vmem] * (2 + len(pieces)),
         out_specs=in_vmem,
         out_shape=jax.ShapeDtypeStruct(saved_rows.shape, jnp.bfloat16),
-        compiler_params=pltpu.CompilerParams(vmem_limit_bytes=24 << 20),
+        compiler_params=pltpu.CompilerParams(vmem_limit_bytes=8 << 20),
     )(saved_rows, upstream_rows, *pieces)
+
+
+def joined_kernel(at_ends, is_end_ref, some_ref, *refs):
+    out_ref = refs[-1]
+    total = jnp.where(is_end_ref[0] == at_ends, some_ref[...].astype(jnp.float32), 0.0)
+    for ref in refs[:-1]:
+        total = total + ref[...].astype(jnp.float32)
+    out_ref[...] = total.astype(out_ref.dtype)
+
+
+def joined(is_end, at_ends, some, pieces, kind):
+    return pl.pallas_call(
+        functools.partial(joined_kernel, at_ends),
+        in_specs=[in_smem] + [in_vmem] * (1 + len(pieces)),
+        out_specs=in_vmem,
+        out_shape=jax.ShapeDtypeStruct(some.shape, kind),
+        compiler_params=pltpu.CompilerParams(vmem_limit_bytes=8 << 20),
+    )(is_end, some, *pieces)
 
 
 def line_device(
@@ -317,31 +384,47 @@
     shared = shared_rows(upstream_rows, expert_ids[0], gate_share[0], experts)
     u_two, u_one = hop(4)(shared), hop(2)(shared)
     x_three = hop(2)(x_two)
+
+    both = (own, other)
+    gain = norm_gain
+    ends = (0, 1, experts - 2, experts - 1)
+    is_end = ((me < 2) | (me >= experts - 2)).astype(jnp.int32).reshape(1)
+
+    def second_hop(value):
+        pairs = []
+        for s in range(sections):
+            for i in range(experts):
+                target = (s, i ^ 2) if i in ends else ((s - 1) % sections, i ^ 4)
+                pairs.append((s * experts + i, target[0] * experts + target[1]))
+        return lax.ppermute(value, ("section", "expert"), pairs)
+
+    factors = slot_factors(saved_rows, gain, (own,), [])
+    later_saved, later_upstream, _ = lax.optimization_barrier(
+        (saved_rows, upstream_rows, factors[0])
+    )
+    next_saved, next_upstream = handed(0)(later_saved), handed(0)(later_upstream)
+    here, *own_turned = turning_pieces(named, shared, gain, factors, own, experts, jnp.float32, None)
+    factors = slot_factors(saved_rows, gain, (other,), [here])
+    here, *other_turned = turning_pieces(
+        swapped, shared, gain, factors, other, experts, jnp.bfloat16, here
+    )
+    turned = (own_turned, other_turned)
+    two_factors = slot_factors(x_two, gain, both, [here])
+    one_factors = slot_factors(x_one, gain, both, [two_factors[0], next_saved])
+    u_two, one_gate = lax.optimization_barrier((u_two, one_factors[0]))
+    one_factors = (one_gate, one_factors[1])
     u_three = hop(2)(u_two)
-    next_saved, next_upstream = handed(0)(saved_rows), handed(0)(upstream_rows)
-
-    both = (own, other)
-    narrow = jnp.bfloat16
-    gain = norm_gain
-
-    def pieces_of(names, rows, factors, weights, kind=narrow, base=None, after=()):
-        return slot_pieces(names, rows, gain, factors, weights, experts, kind, base, after)
-
-    factors = slot_factors(saved_rows, gain, (own,), [])
-    here = pieces_of(named, shared, factors, (own,), jnp.float32)
-    factors = slot_factors(saved_rows, gain, (other,), [here])
-    here = pieces_of(swapped, shared, factors, (other,), narrow, here)
-    two_factors = slot_factors(x_two, gain, both, [here])
-    one_factors = slot_factors(x_one, gain, both, [two_factors[0]])
-    two = pieces_of(named, u_two, two_factors, both, after=[one_factors[0]])
-    one = pieces_of(named, u_one, one_factors, both, after=[two, next_saved])
+    two = slot_pieces(named, u_two, gain, two_factors, turned, experts, [one_factors[0], next_upstream])
+    two_next = second_hop(two)
     here_next = handed(0)(here)
+    three_factors = slot_factors(x_three, gain, both, [two])
+    three = slot_pieces(named, u_three, gain, three_factors, turned, experts, [here_next])
+    three = joined(is_end, 0, two_next, [three], jnp.bfloat16)
+    three_next = handed(6)(three)
+    one = slot_pieces(named, u_one, gain, one_factors, turned, experts, [three])
     one_next = handed(2)(one)
-    two_next = handed(4)(two)
-    three_factors = slot_factors(x_three, gain, both, [one, next_upstream, here_next])
-    three = pieces_of(named, u_three, three_factors, both)
-    pieces = [here_next, one_next, two_next, handed(6)(three)]
-    return finish(next_saved, next_upstream, pieces)[None]
+    summed = joined(is_end, 1, two_next, [here_next, three_next], jnp.float32)
+    return finish(next_saved, next_upstream, [summed, one_next])[None]
 
 
 def solution(mesh):

time: 127 us -> 131 us (1.031); the launches traced: 127 us -> 129 us
  Pallas kernels: 71.7 us -> 57.9 us
  local copies, waits for them, and re-layouts: 8.07 us -> 16.5 us
  starting transfers between devices: 18.1 us -> 22.7 us
  waiting for transfers between devices: 28.6 us -> 31.7 us
    pallas_call x5 -> x7, Pallas kernels: 48.5 us -> 32.2 us  [the longest x3 16.3 us: slot_pieces(): pl.pallas_call(functools.partial(pieces_kernel, experts, pairs), in_specs...]
    unnamed x26 -> x44, local copies, waits for them, and re-layouts: 8.07 us -> 16.5 us
    ppermute x9, waiting for transfers between devices: 5.03 us -> 10.4 us  [hop(): lax.ppermute(value, 'expert', [(i, i ^ by) for i in range(experts)])]
    ppermute x0 -> x1, starting transfers between devices: none -> 4.4 us  [second_hop(): return lax.ppermute(value, ('section', 'expert'), pairs)]
    pallas_call x5, Pallas kernels: 20.2 us -> 24.1 us  [slot_factors(): pl.pallas_call(functools.partial(factors_kernel, pairs), in_specs=[in_vme...]
    ppermute x6 -> x5, waiting for transfers between devices: 23.6 us -> 21.3 us  [handed(): return lambda value: lax.ppermute(value, ('section', 'expert'), pairs)]
    ppermute x6 -> x5, starting transfers between devices: 10.9 us -> 10.7 us  [handed(): return lambda value: lax.ppermute(value, ('section', 'expert'), pairs)]
  transfers between devices with their start and end apart: 15 -> 15, of which waited for: 4 -> 3; matrix products, arithmetic and copies ran while one was open for 1% -> 1% of each run, Pallas kernels for 55% -> 44%
where the time goes in v3:
time: 131 us; the launch traced here: 129 us
  Pallas kernels  57.9 us (44%)
  waiting for transfers between devices  31.7 us (24%)
  starting transfers between devices  22.7 us (17%)
  local copies, waits for them, and re-layouts  16.5 us (13%)
    pallas_call x5, Pallas kernels, slot_factors(): pl.pallas_call(functools.partial(factors_kernel, pairs), in_specs=[in_vme...  24.1 us
    ppermute x5, waiting for transfers between devices, handed(): return lambda value: lax.ppermute(value, ('section', 'expert'), pairs)  21.3 us
    unnamed x44, local copies, waits for them, and re-layouts  16.5 us
    pallas_call x3, Pallas kernels, slot_pieces(): pl.pallas_call(functools.partial(pieces_kernel, experts, pairs), in_specs...  16.3 us
    pallas_call x2, Pallas kernels, turning_pieces(): pl.pallas_call(functools.partial(turning_kernel, experts, len(start)), in...  15.5 us
    ppermute x5, starting transfers between devices, handed(): return lambda value: lax.ppermute(value, ('section', 'expert'), pairs)  10.7 us
    ppermute x9, waiting for transfers between devices, hop(): lax.ppermute(value, 'expert', [(i, i ^ by) for i in range(experts)])  10.4 us
    ppermute x9, starting transfers between devices, hop(): lax.ppermute(value, 'expert', [(i, i ^ by) for i in range(experts)])  7.61 us
  transfers between devices with their start and end apart: 15, of which 3 were waited for; matrix products, arithmetic and copies ran while one was open for 1% of the time, Pallas kernels for 44%

profile of v3, /device:TPU:8, one launch (start us, length us, event | category | flops | bytes accessed | tf_op | source)
XLA Modules:
  0.0 129.2 jit_solution(3417124131549693136)
XLA Ops:
  0.0 0.5 collective-permute-start.5
  0.5 0.0 collective-permute-start.7
  0.5 2.6 %collective-permute-start.6 = (bf16[128,2048]{1,0:T(8,128)(2,1)}, bf16[128,2048]{1,0:T(8,128)(2,1)}, u32[]{:S(2)}, u32[]{:S(2)}) collective-permute-start(bf16[128,2048]{1,0:T(8,128)(2,1)} %bitcast.saved_ref), channel_id=1, source_target_pairs={{0,4},{1,5},{2,6},{3,7},{4,0},{5,1},{6,2},{7,3},{8,12},{9,13},{10,... | collective-permute-start | bytes 1572872 | tf_op jit(solution)/shard_map/ppermute | solution.py:372
  3.1 0.4 collective-permute-start.3
  3.6 0.8 copy.9
  4.3 0.8 copy.10
  5.1 1.0 copy-done.19
  6.2 0.2 shard_map.83.rows_ref
  6.4 0.1 pad_add_fusion.named_ref
  6.5 2.0 %copy-done = bf16[1,1,2048,768]{3,2,1,0:T(8,128)(2,1)S(1)} copy-done((bf16[1,1,2048,768]{3,2,1,0:T(8,128)(2,1)S(1)}, bf16[1,1,2048,768]{3,2,1,0:T(8,128)(2,1)}, u32[]{:S(2)}) %copy-start) | copy-done | bytes 3145752
  8.5 1.9 %copy-done.2 = bf16[1,1,2048,768]{3,2,1,0:T(8,128)(2,1)S(1)} copy-done((bf16[1,1,2048,768]{3,2,1,0:T(8,128)(2,1)S(1)}, bf16[1,1,2048,768]{3,2,1,0:T(8,128)(2,1)}, u32[]{:S(2)}) %copy-start.2) | copy-done | bytes 3145752
  10.4 0.7 copy-done.17
  11.1 2.8 %shard_map.82 = (f32[1,128,768]{2,1,0:T(8,128)S(1)}, f32[1,128,768]{2,1,0:T(8,128)S(1)}) custom-call(bf16[128,2048]{1,0:T(8,128)(2,1)} %bitcast.saved_ref, f32[1,2048]{1,0:T(1,128)S(1)} %copy-done.17, bf16[2048,768]{1,0:T(8,128)(2,1)S(1)} %bitcast.12, bf16[2048,768]{1,0:T(8,128)(2,1)S(1)} %bitcast.18), custom_call_target="tpu_custom_call" | custom-call | flops 1610612736 | bytes 6291456 | tf_op jit(solution)/shard_map/pallas_call | solution.py:185
  14.0 0.1 copy-done.3
  14.1 1.9 %copy-done.16 = bf16[1,1,768,2048]{3,2,1,0:T(8,128)(2,1)S(1)} copy-done((bf16[1,1,768,2048]{3,2,1,0:T(8,128)(2,1)S(1)}, bf16[1,1,768,2048]{3,2,1,0:T(8,128)(2,1)}, u32[]{:S(2)}) %copy-start.16) | copy-done | bytes 3145752
  16.0 6.0 %shard_map.84 = (f32[128,2048]{1,0:T(8,128)S(1)}, bf16[768,2048]{1,0:T(8,128)(2,1)S(1)}, bf16[768,2048]{1,0:T(8,128)(2,1)S(1)}, bf16[2048,768]{1,0:T(8,128)(2,1)S(1)}) custom-call(s32[2]{0:T(128)S(1)} %pad_add_fusion.named_ref, bf16[128,2176]{1,0:T(8,128)(2,1)S(1)} %shard_map.83.rows_ref, f32[1,2048]{1,0:T(1,128)S(1)} %copy-done.18, ...), custom_call_target="tpu_custom_call" | custom-call | flops 2415919104 | bytes 9437184 | tf_op jit(solution)/shard_map/pallas_call | solution.py:250
  22.0 1.7 %copy-done.5 = bf16[768,2048]{1,0:T(8,128)(2,1)} copy-done((bf16[768,2048]{1,0:T(8,128)(2,1)}, bf16[768,2048]{1,0:T(8,128)(2,1)S(1)}, u32[]{:S(2)}) %copy-start.5) | copy-done | bytes 3145752
  23.7 1.6 %copy-done.7 = bf16[768,2048]{1,0:T(8,128)(2,1)} copy-done((bf16[768,2048]{1,0:T(8,128)(2,1)}, bf16[768,2048]{1,0:T(8,128)(2,1)S(1)}, u32[]{:S(2)}) %copy-start.7) | copy-done | bytes 3145752
  25.4 1.7 %copy-done.9 = bf16[2048,768]{1,0:T(8,128)(2,1)} copy-done((bf16[2048,768]{1,0:T(8,128)(2,1)}, bf16[2048,768]{1,0:T(8,128)(2,1)S(1)}, u32[]{:S(2)}) %copy-start.9) | copy-done | bytes 3145752
  27.1 1.0 copy-done.13
  28.1 0.1 pad_add_fusion.1.named_ref
  28.1 0.0 collective-permute-start.2
  28.2 1.9 %collective-permute-start.13 = (bf16[128,2176]{1,0:T(8,128)(2,1)}, bf16[128,2176]{1,0:T(8,128)(2,1)S(1)}, u32[]{:S(2)}, u32[]{:S(2)}) collective-permute-start(bf16[128,2176]{1,0:T(8,128)(2,1)} %copy-done.11), channel_id=1, source_target_pairs={{0,2},{1,3},{2,0},{3,1},{4,6},{5,7},{6,4},{7,5},{8,10},{9,11},{10,... | collective-permute-start | bytes 1671176 | tf_op jit(solution)/shard_map/ppermute | solution.py:372
  30.1 1.2 copy-done.14
  31.3 4.8 %shard_map.85 = (f32[1,128,768]{2,1,0:T(8,128)S(1)}, f32[1,128,768]{2,1,0:T(8,128)S(1)}) custom-call(bf16[128,2048]{1,0:T(8,128)(2,1)} %bitcast.saved_ref, f32[1,2048]{1,0:T(1,128)S(1)} %copy-done.18, bf16[2048,768]{1,0:T(8,128)(2,1)} %collective-permute-done.4.refs_0_.refs_2_, bf16[2048,768]{1,0:T(8,128)(2,1)} %collective-permute-done.5.refs_1_.refs_3_, ...), custom_call_target="tpu_custom_call" | custom-call | flops 1610612736 | bytes 6291456 | tf_op jit(solution)/shard_map/pallas_call | solution.py:185
  36.0 0.0 collective-permute-done.7.refs_2_
  36.0 2.5 %collective-permute-start = (bf16[128,2048]{1,0:T(8,128)(2,1)}, bf16[128,2048]{1,0:T(8,128)(2,1)S(1)}, u32[]{:S(2)}, u32[]{:S(2)}) collective-permute-start(bf16[128,2048]{1,0:T(8,128)(2,1)} %bitcast.saved_ref), channel_id=1, source_target_pairs={{0,24},{1,25},{2,26},{3,27},{4,28},{5,29},{6,30},{7,31},{8,0},{9,1... | collective-permute-start | bytes 1572872 | tf_op jit(solution)/shard_map/ppermute | solution.py:380
  38.6 9.4 %shard_map.86 = (bf16[128,2048]{1,0:T(8,128)(2,1)S(1)}, bf16[768,2048]{1,0:T(8,128)(2,1)S(1)}, bf16[768,2048]{1,0:T(8,128)(2,1)S(1)}, bf16[2048,768]{1,0:T(8,128)(2,1)S(1)}) custom-call(s32[2]{0:T(128)S(1)} %pad_add_fusion.1.named_ref, bf16[128,2176]{1,0:T(8,128)(2,1)S(1)} %copy-done.12, f32[1,2048]{1,0:T(1,128)S(1)} %copy-done.18, ...), custom_call_target="tpu_custom_call" | custom-call | flops 2415919104 | bytes 9437184 | tf_op jit(solution)/shard_map/pallas_call | solution.py:250
  48.0 0.6 collective-permute-start.1
  48.6 5.5 %shard_map.87 = (f32[2,128,768]{2,1,0:T(8,128)S(1)}, f32[2,128,768]{2,1,0:T(8,128)S(1)}) custom-call(bf16[128,2048]{1,0:T(8,128)(2,1)} %collective-permute-done.6.saved_ref, f32[1,2048]{1,0:T(1,128)S(1)} %copy-done.18, bf16[2048,768]{1,0:T(8,128)(2,1)S(1)} %bitcast.14, bf16[2048,768]{1,0:T(8,128)(2,1)S(1)} %bitcast.20, ...), custom_call_target="tpu_custom_call" | custom-call | flops 3221225472 | bytes 12582912 | tf_op jit(solution)/shard_map/pallas_call | solution.py:185
  54.1 0.0 collective-permute-done.refs_5_.saved_ref
  54.1 0.5 collective-permute-start.11
  54.6 1.4 %collective-permute-start.9 = (bf16[128,2048]{1,0:T(8,128)(2,1)S(1)}, bf16[128,2048]{1,0:T(8,128)(2,1)S(1)}, u32[]{:S(2)}, u32[]{:S(2)}) collective-permute-start(bf16[128,2048]{1,0:T(8,128)(2,1)S(1)} %get-tuple-element.34.refs_4_), channel_id=1, source_target_pairs={{0,24},{1,25},{2,26},{3,27},{4,28},{5,29},{6,30},{7,31},{8,0},{9,1... | collective-permute-start | bytes 1572872 | tf_op jit(solution)/shard_map/ppermute | solution.py:380
  56.1 5.6 %shard_map.88 = (f32[2,128,768]{2,1,0:T(8,128)S(1)}, f32[2,128,768]{2,1,0:T(8,128)S(1)}) custom-call(bf16[128,2048]{1,0:T(8,128)(2,1)} %collective-permute-done.3.saved_ref, f32[1,2048]{1,0:T(1,128)S(1)} %copy-done.18, bf16[2048,768]{1,0:T(8,128)(2,1)S(1)} %bitcast.15, bf16[2048,768]{1,0:T(8,128)(2,1)S(1)} %bitcast.21, ...), custom_call_target="tpu_custom_call" | custom-call | flops 3221225472 | bytes 12582912 | tf_op jit(solution)/shard_map/pallas_call | solution.py:185
  61.8 1.6 %collective-permute-start.10 = (bf16[128,2176]{1,0:T(8,128)(2,1)S(1)}, bf16[128,2176]{1,0:T(8,128)(2,1)S(1)}, u32[]{:S(2)}, u32[]{:S(2)}) collective-permute-start(bf16[128,2176]{1,0:T(8,128)(2,1)S(1)} %collective-permute-done.2.rows_ref), channel_id=1, source_target_pairs={{0,2},{1,3},{2,0},{3,1},{4,6},{5,7},{6,4},{7,5},{8,10},{9,11},{10,... | collective-permute-start | bytes 1671176 | tf_op jit(solution)/shard_map/ppermute | solution.py:372
  63.4 5.4 %shard_map.89.refs_4_ = bf16[128,2048]{1,0:T(8,128)(2,1)S(1)} custom-call(s32[2]{0:T(128)S(1)} %pad_add_fusion.named_ref, bf16[128,2176]{1,0:T(8,128)(2,1)S(1)} %collective-permute-done.2.rows_ref, f32[1,2048]{1,0:T(1,128)S(1)} %copy-done.18, f32[2,128,768]{2,1,0:T(8,128)S(1)} %get-tuple-element.35.refs_4_.gate_ref, ...), custom_call_target="tpu_custom_call" | custom-call | flops 4831838208 | bytes 18874368 | tf_op jit(solution)/shard_map/pallas_call | solution.py:304
  68.9 4.4 %collective-permute-start.8 = (bf16[128,2048]{1,0:T(8,128)(2,1)S(1)}, bf16[128,2048]{1,0:T(8,128)(2,1)S(1)}, u32[]{:S(2)}, u32[]{:S(2)}) collective-permute-start(bf16[128,2048]{1,0:T(8,128)(2,1)S(1)} %shard_map.89.refs_4_), channel_id=1, source_target_pairs={{0,2},{1,3},{2,30},{3,31},{4,24},{5,25},{6,4},{7,5},{8,10},{9,11},... | collective-permute-start | bytes 1572872 | tf_op jit(solution)/shard_map/ppermute | solution.py:399
  73.3 5.4 %shard_map.90 = (f32[2,128,768]{2,1,0:T(8,128)S(1)}, f32[2,128,768]{2,1,0:T(8,128)S(1)}) custom-call(bf16[128,2048]{1,0:T(8,128)(2,1)S(1)} %collective-permute-done.11.saved_ref, f32[1,2048]{1,0:T(1,128)S(1)} %copy-done.18, bf16[2048,768]{1,0:T(8,128)(2,1)S(1)} %bitcast.16, bf16[2048,768]{1,0:T(8,128)(2,1)S(1)} %bitcast.22, ...), custom_call_target="tpu_custom_call" | custom-call | flops 3221225472 | bytes 12582912 | tf_op jit(solution)/shard_map/pallas_call | solution.py:185
  78.7 10.4 %collective-permute-done.10.rows_ref = bf16[128,2176]{1,0:T(8,128)(2,1)S(1)} collective-permute-done((bf16[128,2176]{1,0:T(8,128)(2,1)S(1)}, bf16[128,2176]{1,0:T(8,128)(2,1)S(1)}, u32[]{:S(2)}, u32[]{:S(2)}) %collective-permute-start.10) | collective-permute-done | bytes 557088 | tf_op jit(solution)/shard_map/ppermute | solution.py:372
  89.0 5.4 %shard_map.91.refs_0_ = bf16[128,2048]{1,0:T(8,128)(2,1)S(1)} custom-call(s32[2]{0:T(128)S(1)} %pad_add_fusion.named_ref, bf16[128,2176]{1,0:T(8,128)(2,1)S(1)} %collective-permute-done.10.rows_ref, f32[1,2048]{1,0:T(1,128)S(1)} %copy-done.18, f32[2,128,768]{2,1,0:T(8,128)S(1)} %get-tuple-element.46.gate_ref, f32[2,128,768]{2,1,0:T(8,128)S(1)} %get-tuple-element.47.up_ref, ...), custom_call_target="tpu_custom_call" | custom-call | flops 4831838208 | bytes 18874368 | tf_op jit(solution)/shard_map/pallas_call | solution.py:304
  94.5 0.2 shard_map.92.refs_6_
  94.7 2.8 %collective-permute-start.12 = (bf16[128,2048]{1,0:T(8,128)(2,1)S(1)}, bf16[128,2048]{1,0:T(8,128)(2,1)S(1)}, u32[]{:S(2)}, u32[]{:S(2)}) collective-permute-start(bf16[128,2048]{1,0:T(8,128)(2,1)S(1)} %shard_map.92.refs_6_), channel_id=1, source_target_pairs={{0,30},{1,31},{2,28},{3,29},{4,26},{5,27},{6,24},{7,25},{8,6},{9,7... | collective-permute-start | bytes 1572872 | tf_op jit(solution)/shard_map/ppermute | solution.py:380
  97.5 5.5 %shard_map.94 = bf16[128,2048]{1,0:T(8,128)(2,1)S(1)} custom-call(s32[2]{0:T(128)S(1)} %pad_add_fusion.named_ref, bf16[128,2176]{1,0:T(8,128)(2,1)S(1)} %collective-permute-done.13.rows_ref, f32[1,2048]{1,0:T(1,128)S(1)} %copy-done.18, f32[2,128,768]{2,1,0:T(8,128)S(1)} %get-tuple-element.45.refs_6_.gate_ref, f32[2,128,768]{2,1,0:T(8,128)S(1)} %get-tuple-element.48.up_ref, ...), custom_call_target="tpu_custom_call" | custom-call | flops 4831838208 | bytes 18874368 | tf_op jit(solution)/shard_map/pallas_call | solution.py:304
  102.9 3.4 %collective-permute-start.14 = (bf16[128,2048]{1,0:T(8,128)(2,1)S(1)}, bf16[128,2048]{1,0:T(8,128)(2,1)S(1)}, u32[]{:S(2)}, u32[]{:S(2)}) collective-permute-start(bf16[128,2048]{1,0:T(8,128)(2,1)S(1)} %shard_map.94), channel_id=1, source_target_pairs={{0,26},{1,27},{2,24},{3,25},{4,30},{5,31},{6,28},{7,29},{8,2},{9,3... | collective-permute-start | bytes 1572872 | tf_op jit(solution)/shard_map/ppermute | solution.py:380
  106.3 19.0 %collective-permute-done.12.refs_1_ = bf16[128,2048]{1,0:T(8,128)(2,1)S(1)} collective-permute-done((bf16[128,2048]{1,0:T(8,128)(2,1)S(1)}, bf16[128,2048]{1,0:T(8,128)(2,1)S(1)}, u32[]{:S(2)}, u32[]{:S(2)}) %collective-permute-start.12) | collective-permute-done | bytes 524320 | tf_op jit(solution)/shard_map/ppermute | solution.py:380
  125.3 0.2 shard_map.93.refs_0_
  125.6 2.2 %collective-permute-done.14.refs_1_ = bf16[128,2048]{1,0:T(8,128)(2,1)S(1)} collective-permute-done((bf16[128,2048]{1,0:T(8,128)(2,1)S(1)}, bf16[128,2048]{1,0:T(8,128)(2,1)S(1)}, u32[]{:S(2)}, u32[]{:S(2)}) %collective-permute-start.14) | collective-permute-done | bytes 524320 | tf_op jit(solution)/shard_map/ppermute | solution.py:380
  127.8 1.5 %shard_map.95 = bf16[128,2048]{1,0:T(8,128)(2,1)} custom-call(bf16[128,2048]{1,0:T(8,128)(2,1)S(1)} %collective-permute-done.refs_5_.saved_ref, bf16[128,2048]{1,0:T(8,128)(2,1)S(1)} %collective-permute-done.1.refs_7_.upstream_ref, f32[128,2048]{1,0:T(8,128)S(1)} %shard_map.93.refs_0_, bf16[128,2048]{1,0:T(8,128)(2,1)S(1)} %collective-permute-done.14.refs_1_), custom_call_target="tpu_custom_call" | custom-call | tf_op jit(solution)/shard_map/pallas_call | solution.py:333
  (42 shorter events, 0.1 us)
Async XLA Ops:
  0.0 28.1 %collective-permute-start.4 = (bf16[2048,768]{1,0:T(8,128)(2,1)}, bf16[2048,768]{1,0:T(8,128)(2,1)}, u32[]{:S(2)}, u32[]{:S(2)}) collective-permute-start(bf16[2048,768]{1,0:T(8,128)(2,1)} %bitcast.11), channel_id=1, source_target_pairs={{0,1},{1,0},{2,3},{3,2},{4,5},{5,4},{6,7},{7,6},{8,9},{9,8},{10,11... | collective-permute-start | bytes 9437192 | tf_op jit(solution)/shard_map/ppermute | solution.py:372
  0.0 28.1 %collective-permute-start.5 = (bf16[2048,768]{1,0:T(8,128)(2,1)}, bf16[2048,768]{1,0:T(8,128)(2,1)}, u32[]{:S(2)}, u32[]{:S(2)}) collective-permute-start(bf16[2048,768]{1,0:T(8,128)(2,1)} %bitcast.17), channel_id=1, source_target_pairs={{0,1},{1,0},{2,3},{3,2},{4,5},{5,4},{6,7},{7,6},{8,9},{9,8},{10,11... | collective-permute-start | bytes 9437192 | tf_op jit(solution)/shard_map/ppermute | solution.py:372
  0.5 35.5 %collective-permute-start.7 = (bf16[768,2048]{1,0:T(8,128)(2,1)}, bf16[768,2048]{1,0:T(8,128)(2,1)}, u32[]{:S(2)}, u32[]{:S(2)}) collective-permute-start(bf16[768,2048]{1,0:T(8,128)(2,1)} %bitcast.23), channel_id=1, source_target_pairs={{0,1},{1,0},{2,3},{3,2},{4,5},{5,4},{6,7},{7,6},{8,9},{9,8},{10,11... | collective-permute-start | bytes 9437192 | tf_op jit(solution)/shard_map/ppermute | solution.py:372
  0.5 47.5 %collective-permute-start.6 = (bf16[128,2048]{1,0:T(8,128)(2,1)}, bf16[128,2048]{1,0:T(8,128)(2,1)}, u32[]{:S(2)}, u32[]{:S(2)}) collective-permute-start(bf16[128,2048]{1,0:T(8,128)(2,1)} %bitcast.saved_ref), channel_id=1, source_target_pairs={{0,4},{1,5},{2,6},{3,7},{4,0},{5,1},{6,2},{7,3},{8,12},{9,13},{10,... | collective-permute-start | bytes 1572872 | tf_op jit(solution)/shard_map/ppermute | solution.py:372
  3.1 51.5 %collective-permute-start.3 = (bf16[128,2048]{1,0:T(8,128)(2,1)}, bf16[128,2048]{1,0:T(8,128)(2,1)}, u32[]{:S(2)}, u32[]{:S(2)}) collective-permute-start(bf16[128,2048]{1,0:T(8,128)(2,1)} %bitcast.saved_ref), channel_id=1, source_target_pairs={{0,2},{1,3},{2,0},{3,1},{4,6},{5,7},{6,4},{7,5},{8,10},{9,11},{10,... | collective-permute-start | bytes 1572872 | tf_op jit(solution)/shard_map/ppermute | solution.py:372
  5.1 1.0 copy-start.19
  6.4 7.5 %copy-start.11 = (bf16[128,2176]{1,0:T(8,128)(2,1)}, bf16[128,2176]{1,0:T(8,128)(2,1)S(1)}, u32[]{:S(2)}) copy-start(bf16[128,2176]{1,0:T(8,128)(2,1)S(1)} %shard_map.83.rows_ref) | copy-start | bytes 1671172
  6.5 2.0 %copy-start = (bf16[1,1,2048,768]{3,2,1,0:T(8,128)(2,1)S(1)}, bf16[1,1,2048,768]{3,2,1,0:T(8,128)(2,1)}, u32[]{:S(2)}) copy-start(bf16[1,1,2048,768]{3,2,1,0:T(8,128)(2,1)} %param.11) | copy-start | bytes 9437188
  8.5 1.9 %copy-start.2 = (bf16[1,1,2048,768]{3,2,1,0:T(8,128)(2,1)S(1)}, bf16[1,1,2048,768]{3,2,1,0:T(8,128)(2,1)}, u32[]{:S(2)}) copy-start(bf16[1,1,2048,768]{3,2,1,0:T(8,128)(2,1)} %param.12) | copy-start | bytes 9437188
  10.4 0.7 copy-start.17
  11.1 2.9 %copy-start.1 = (bf16[1,1,2048,768]{3,2,1,0:T(8,128)(2,1)S(1)}, bf16[1,1,2048,768]{3,2,1,0:T(8,128)(2,1)}, u32[]{:S(2)}) copy-start(bf16[1,1,2048,768]{3,2,1,0:T(8,128)(2,1)} %param.11) | copy-start | bytes 9437188
  11.1 3.0 %copy-start.3 = (bf16[1,1,2048,768]{3,2,1,0:T(8,128)(2,1)S(1)}, bf16[1,1,2048,768]{3,2,1,0:T(8,128)(2,1)}, u32[]{:S(2)}) copy-start(bf16[1,1,2048,768]{3,2,1,0:T(8,128)(2,1)} %param.12) | copy-start | bytes 9437188
  11.1 3.0 %copy-start.18 = (f32[1,2048]{1,0:T(1,128)S(1)}, f32[1,2048]{1,0:T(1,128)}, u32[]{:S(2)}) copy-start(f32[1,2048]{1,0:T(1,128)} %gain_ref.19) | copy-start | bytes 24580
  14.1 1.9 %copy-start.16 = (bf16[1,1,768,2048]{3,2,1,0:T(8,128)(2,1)S(1)}, bf16[1,1,768,2048]{3,2,1,0:T(8,128)(2,1)}, u32[]{:S(2)}) copy-start(bf16[1,1,768,2048]{3,2,1,0:T(8,128)(2,1)} %param.13) | copy-start | bytes 9437188
  22.0 1.7 %copy-start.5 = (bf16[768,2048]{1,0:T(8,128)(2,1)}, bf16[768,2048]{1,0:T(8,128)(2,1)S(1)}, u32[]{:S(2)}) copy-start(bf16[768,2048]{1,0:T(8,128)(2,1)S(1)} %get-tuple-element.39.refs_0_) | copy-start | bytes 9437188
  23.7 1.6 %copy-start.7 = (bf16[768,2048]{1,0:T(8,128)(2,1)}, bf16[768,2048]{1,0:T(8,128)(2,1)S(1)}, u32[]{:S(2)}) copy-start(bf16[768,2048]{1,0:T(8,128)(2,1)S(1)} %get-tuple-element.40.refs_1_) | copy-start | bytes 9437188
  25.4 1.7 %copy-start.9 = (bf16[2048,768]{1,0:T(8,128)(2,1)}, bf16[2048,768]{1,0:T(8,128)(2,1)S(1)}, u32[]{:S(2)}) copy-start(bf16[2048,768]{1,0:T(8,128)(2,1)S(1)} %get-tuple-element.41.refs_2_) | copy-start | bytes 9437188
  27.1 1.0 copy-start.13
  28.1 33.6 %collective-permute-start.2 = (bf16[128,2176]{1,0:T(8,128)(2,1)}, bf16[128,2176]{1,0:T(8,128)(2,1)S(1)}, u32[]{:S(2)}, u32[]{:S(2)}) collective-permute-start(bf16[128,2176]{1,0:T(8,128)(2,1)} %copy-done.11), channel_id=1, source_target_pairs={{0,4},{1,5},{2,6},{3,7},{4,0},{5,1},{6,2},{7,3},{8,12},{9,13},{10,... | collective-permute-start | bytes 1671176 | tf_op jit(solution)/shard_map/ppermute | solution.py:372
  28.2 69.3 %collective-permute-start.13 = (bf16[128,2176]{1,0:T(8,128)(2,1)}, bf16[128,2176]{1,0:T(8,128)(2,1)S(1)}, u32[]{:S(2)}, u32[]{:S(2)}) collective-permute-start(bf16[128,2176]{1,0:T(8,128)(2,1)} %copy-done.11), channel_id=1, source_target_pairs={{0,2},{1,3},{2,0},{3,1},{4,6},{5,7},{6,4},{7,5},{8,10},{9,11},{10,... | collective-permute-start | bytes 1671176 | tf_op jit(solution)/shard_map/ppermute | solution.py:372
  30.0 1.2 copy-start.14
  31.3 7.3 %copy-start.12 = (bf16[128,2176]{1,0:T(8,128)(2,1)S(1)}, bf16[128,2176]{1,0:T(8,128)(2,1)}, u32[]{:S(2)}) copy-start(bf16[128,2176]{1,0:T(8,128)(2,1)} %copy-done.11) | copy-start | bytes 1671172
  31.3 7.3 %copy-start.15 = (f32[128,2048]{1,0:T(8,128)S(1)}, f32[128,2048]{1,0:T(8,128)}, u32[]{:S(2)}) copy-start(f32[128,2048]{1,0:T(8,128)} %copy-done.13) | copy-start | bytes 3145732
  36.0 18.1 %collective-permute-start = (bf16[128,2048]{1,0:T(8,128)(2,1)}, bf16[128,2048]{1,0:T(8,128)(2,1)S(1)}, u32[]{:S(2)}, u32[]{:S(2)}) collective-permute-start(bf16[128,2048]{1,0:T(8,128)(2,1)} %bitcast.saved_ref), channel_id=1, source_target_pairs={{0,24},{1,25},{2,26},{3,27},{4,28},{5,29},{6,30},{7,31},{8,0},{9,1... | collective-permute-start | bytes 1572872 | tf_op jit(solution)/shard_map/ppermute | solution.py:380
  38.5 9.5 %copy-start.20 = (bf16[1,128,2048]{2,1,0:T(8,128)(2,1)S(1)}, bf16[1,128,2048]{2,1,0:T(8,128)(2,1)}, u32[]{:S(2)}) copy-start(bf16[1,128,2048]{2,1,0:T(8,128)(2,1)} %param.9) | copy-start | bytes 1572868
  38.6 10.1 %copy-start.4 = (bf16[1,1,2048,768]{3,2,1,0:T(8,128)(2,1)S(1)}, bf16[1,1,2048,768]{3,2,1,0:T(8,128)(2,1)}, u32[]{:S(2)}) copy-start(bf16[1,1,2048,768]{3,2,1,0:T(8,128)(2,1)} %param.12) | copy-start | bytes 9437188
  48.0 15.4 %collective-permute-start.1 = (bf16[128,2048]{1,0:T(8,128)(2,1)S(1)}, bf16[128,2048]{1,0:T(8,128)(2,1)S(1)}, u32[]{:S(2)}, u32[]{:S(2)}) collective-permute-start(bf16[128,2048]{1,0:T(8,128)(2,1)S(1)} %bitcast.26), channel_id=1, source_target_pairs={{0,24},{1,25},{2,26},{3,27},{4,28},{5,29},{6,30},{7,31},{8,0},{9,1... | collective-permute-start | bytes 1572872 | tf_op jit(solution)/shard_map/ppermute | solution.py:380
  54.1 19.2 %collective-permute-start.11 = (bf16[128,2048]{1,0:T(8,128)(2,1)}, bf16[128,2048]{1,0:T(8,128)(2,1)S(1)}, u32[]{:S(2)}, u32[]{:S(2)}) collective-permute-start(bf16[128,2048]{1,0:T(8,128)(2,1)} %collective-permute-done.6.saved_ref), channel_id=1, source_target_pairs={{0,2},{1,3},{2,0},{3,1},{4,6},{5,7},{6,4},{7,5},{8,10},{9,11},{10,... | collective-permute-start | bytes 1572872 | tf_op jit(solution)/shard_map/ppermute | solution.py:372
  54.6 24.0 %collective-permute-start.9 = (bf16[128,2048]{1,0:T(8,128)(2,1)S(1)}, bf16[128,2048]{1,0:T(8,128)(2,1)S(1)}, u32[]{:S(2)}, u32[]{:S(2)}) collective-permute-start(bf16[128,2048]{1,0:T(8,128)(2,1)S(1)} %get-tuple-element.34.refs_4_), channel_id=1, source_target_pairs={{0,24},{1,25},{2,26},{3,27},{4,28},{5,29},{6,30},{7,31},{8,0},{9,1... | collective-permute-start | bytes 1572872 | tf_op jit(solution)/shard_map/ppermute | solution.py:380
  56.1 7.3 %copy-start.6 = (bf16[768,2048]{1,0:T(8,128)(2,1)S(1)}, bf16[768,2048]{1,0:T(8,128)(2,1)}, u32[]{:S(2)}) copy-start(bf16[768,2048]{1,0:T(8,128)(2,1)} %copy-done.5) | copy-start | bytes 9437188
  56.1 7.3 %copy-start.8 = (bf16[768,2048]{1,0:T(8,128)(2,1)S(1)}, bf16[768,2048]{1,0:T(8,128)(2,1)}, u32[]{:S(2)}) copy-start(bf16[768,2048]{1,0:T(8,128)(2,1)} %copy-done.7) | copy-start | bytes 9437188
  56.1 7.3 %copy-start.10 = (bf16[2048,768]{1,0:T(8,128)(2,1)S(1)}, bf16[2048,768]{1,0:T(8,128)(2,1)}, u32[]{:S(2)}) copy-start(bf16[2048,768]{1,0:T(8,128)(2,1)} %copy-done.9) | copy-start | bytes 9437188
  61.8 27.3 %collective-permute-start.10 = (bf16[128,2176]{1,0:T(8,128)(2,1)S(1)}, bf16[128,2176]{1,0:T(8,128)(2,1)S(1)}, u32[]{:S(2)}, u32[]{:S(2)}) collective-permute-start(bf16[128,2176]{1,0:T(8,128)(2,1)S(1)} %collective-permute-done.2.rows_ref), channel_id=1, source_target_pairs={{0,2},{1,3},{2,0},{3,1},{4,6},{5,7},{6,4},{7,5},{8,10},{9,11},{10,... | collective-permute-start | bytes 1671176 | tf_op jit(solution)/shard_map/ppermute | solution.py:372
  68.9 25.6 %collective-permute-start.8 = (bf16[128,2048]{1,0:T(8,128)(2,1)S(1)}, bf16[128,2048]{1,0:T(8,128)(2,1)S(1)}, u32[]{:S(2)}, u32[]{:S(2)}) collective-permute-start(bf16[128,2048]{1,0:T(8,128)(2,1)S(1)} %shard_map.89.refs_4_), channel_id=1, source_target_pairs={{0,2},{1,3},{2,30},{3,31},{4,24},{5,25},{6,4},{7,5},{8,10},{9,11},... | collective-permute-start | bytes 1572872 | tf_op jit(solution)/shard_map/ppermute | solution.py:399
  94.7 30.7 %collective-permute-start.12 = (bf16[128,2048]{1,0:T(8,128)(2,1)S(1)}, bf16[128,2048]{1,0:T(8,128)(2,1)S(1)}, u32[]{:S(2)}, u32[]{:S(2)}) collective-permute-start(bf16[128,2048]{1,0:T(8,128)(2,1)S(1)} %shard_map.92.refs_6_), channel_id=1, source_target_pairs={{0,30},{1,31},{2,28},{3,29},{4,26},{5,27},{6,24},{7,25},{8,6},{9,7... | collective-permute-start | bytes 1572872 | tf_op jit(solution)/shard_map/ppermute | solution.py:380
  102.9 24.8 %collective-permute-start.14 = (bf16[128,2048]{1,0:T(8,128)(2,1)S(1)}, bf16[128,2048]{1,0:T(8,128)(2,1)S(1)}, u32[]{:S(2)}, u32[]{:S(2)}) collective-permute-start(bf16[128,2048]{1,0:T(8,128)(2,1)S(1)} %shard_map.94), channel_id=1, source_target_pairs={{0,26},{1,27},{2,24},{3,25},{4,30},{5,31},{6,28},{7,29},{8,2},{9,3... | collective-permute-start | bytes 1572872 | tf_op jit(solution)/shard_map/ppermute | solution.py:380

commit v4 on v3

--- a/solution.py
+++ b/solution.py
@@ -379,13 +379,10 @@
         ]
         return lambda value: lax.ppermute(value, ("section", "expert"), pairs)
 
-    other = tuple(hop(1)(w) for w in own)
+    shared = shared_rows(upstream_rows, expert_ids[0], gate_share[0], experts)
     x_two, x_one = hop(4)(saved_rows), hop(2)(saved_rows)
-    shared = shared_rows(upstream_rows, expert_ids[0], gate_share[0], experts)
-    u_two, u_one = hop(4)(shared), hop(2)(shared)
-    x_three = hop(2)(x_two)
-
-    both = (own, other)
+    gate_other, up_other = hop(1)(own[0]), hop(1)(own[1])
+    u_two = hop(4)(shared)
     gain = norm_gain
     ends = (0, 1, experts - 2, experts - 1)
     is_end = ((me < 2) | (me >= experts - 2)).astype(jnp.int32).reshape(1)
@@ -398,33 +395,42 @@
                 pairs.append((s * experts + i, target[0] * experts + target[1]))
         return lax.ppermute(value, ("section", "expert"), pairs)
 
-    factors = slot_factors(saved_rows, gain, (own,), [])
-    later_saved, later_upstream, _ = lax.optimization_barrier(
-        (saved_rows, upstream_rows, factors[0])
-    )
-    next_saved, next_upstream = handed(0)(later_saved), handed(0)(later_upstream)
-    here, *own_turned = turning_pieces(named, shared, gain, factors, own, experts, jnp.float32, None)
-    factors = slot_factors(saved_rows, gain, (other,), [here])
+    own_factors = slot_factors(saved_rows, gain, (own,), [])
+    later, gate = lax.optimization_barrier((shared, own_factors[0]))
+    own_factors = (gate, own_factors[1])
+    other = (gate_other, up_other, hop(1)(own[2]))
+    u_one = hop(2)(later)
+    other_factors = slot_factors(saved_rows, gain, (other,), [gate])
+    both = (own, other)
+    here, *own_turned = turning_pieces(
+        named, shared, gain, own_factors, own, experts, jnp.float32, None
+    )
     here, *other_turned = turning_pieces(
-        swapped, shared, gain, factors, other, experts, jnp.bfloat16, here
+        swapped, shared, gain, other_factors, other, experts, jnp.bfloat16, here
     )
     turned = (own_turned, other_turned)
+    x_three = hop(2)(x_two)
     two_factors = slot_factors(x_two, gain, both, [here])
-    one_factors = slot_factors(x_one, gain, both, [two_factors[0], next_saved])
-    u_two, one_gate = lax.optimization_barrier((u_two, one_factors[0]))
-    one_factors = (one_gate, one_factors[1])
+    one_factors = slot_factors(x_one, gain, both, [two_factors[0]])
+    three_factors = slot_factors(x_three, gain, both, [one_factors[0]])
+    u_two, saved_later, three_gate = lax.optimization_barrier(
+        (u_two, saved_rows, three_factors[0])
+    )
+    three_factors = (three_gate, three_factors[1])
+    next_saved = handed(0)(saved_later)
+    here_next = handed(0)(here)
     u_three = hop(2)(u_two)
-    two = slot_pieces(named, u_two, gain, two_factors, turned, experts, [one_factors[0], next_upstream])
+    two = slot_pieces(named, u_two, gain, two_factors, turned, experts, [here_next])
     two_next = second_hop(two)
-    here_next = handed(0)(here)
-    three_factors = slot_factors(x_three, gain, both, [two])
-    three = slot_pieces(named, u_three, gain, three_factors, turned, experts, [here_next])
+    upstream_later, two = lax.optimization_barrier((upstream_rows, two))
+    next_upstream = handed(0)(upstream_later)
+    one = slot_pieces(named, u_one, gain, one_factors, turned, experts, [two, next_saved])
+    one_next = handed(2)(one)
+    three = slot_pieces(named, u_three, gain, three_factors, turned, experts, [one, next_upstream])
     three = joined(is_end, 0, two_next, [three], jnp.bfloat16)
+    summed = joined(is_end, 1, two_next, [here_next, one_next], jnp.float32)
     three_next = handed(6)(three)
-    one = slot_pieces(named, u_one, gain, one_factors, turned, experts, [three])
-    one_next = handed(2)(one)
-    summed = joined(is_end, 1, two_next, [here_next, three_next], jnp.float32)
-    return finish(next_saved, next_upstream, [summed, one_next])[None]
+    return finish(next_saved, next_upstream, [summed, three_next])[None]
 
 
 def solution(mesh):

time: 131 us -> 146 us (1.11)
  local copies, waits for them, and re-layouts: 16.5 us -> 26.6 us
  starting transfers between devices: 22.7 us -> 32.8 us
  waiting for transfers between devices: 31.7 us -> 22.9 us
  Pallas kernels: 57.9 us -> 62.7 us
    ppermute x5, starting transfers between devices: 10.7 us -> 22 us  [handed(): return lambda value: lax.ppermute(value, ('section', 'expert'), pairs)]
    unnamed x44 -> x74, local copies, waits for them, and re-layouts: 16.5 us -> 26.6 us
    ppermute x9, waiting for transfers between devices: 10.4 us -> 5.22 us  [hop(): lax.ppermute(value, 'expert', [(i, i ^ by) for i in range(experts)])]
    ppermute x5, waiting for transfers between devices: 21.3 us -> 17.6 us  [handed(): return lambda value: lax.ppermute(value, ('section', 'expert'), pairs)]
    ppermute x1, starting transfers between devices: 4.4 us -> 2.19 us  [second_hop(): return lax.ppermute(value, ('section', 'expert'), pairs)]
    pallas_call x1, Pallas kernels: 0.22 us -> 2.08 us  [shared_rows(): pl.pallas_call(functools.partial(shared_kernel, experts), in_specs=[in_vm...]
    pallas_call x3, Pallas kernels: 16.3 us -> 18.2 us  [slot_pieces(): pl.pallas_call(functools.partial(pieces_kernel, experts, pairs), in_specs...]
  transfers between devices with their start and end apart: 15 -> 15, of which waited for: 3 -> 4; matrix products, arithmetic and copies ran while one was open for 1% -> 1% of each run, Pallas kernels for 44% -> 42%
where the time goes in v4:
time: 146 us; the launch traced here: 145 us
  Pallas kernels  62.7 us (43%)
  starting transfers between devices  32.8 us (22%)
  local copies, waits for them, and re-layouts  26.6 us (18%)
  waiting for transfers between devices  22.9 us (16%)
    unnamed x74, local copies, waits for them, and re-layouts  26.6 us
    pallas_call x5, Pallas kernels, slot_factors(): pl.pallas_call(functools.partial(factors_kernel, pairs), in_specs=[in_vme...  24.4 us
    ppermute x5, starting transfers between devices, handed(): return lambda value: lax.ppermute(value, ('section', 'expert'), pairs)  22 us
    pallas_call x3, Pallas kernels, slot_pieces(): pl.pallas_call(functools.partial(pieces_kernel, experts, pairs), in_specs...  18.2 us
    ppermute x5, waiting for transfers between devices, handed(): return lambda value: lax.ppermute(value, ('section', 'expert'), pairs)  17.6 us
    pallas_call x2, Pallas kernels, turning_pieces(): pl.pallas_call(functools.partial(turning_kernel, experts, len(start)), in...  16.2 us
    ppermute x9, starting transfers between devices, hop(): lax.ppermute(value, 'expert', [(i, i ^ by) for i in range(experts)])  8.64 us
    ppermute x9, waiting for transfers between devices, hop(): lax.ppermute(value, 'expert', [(i, i ^ by) for i in range(experts)])  5.22 us
  transfers between devices with their start and end apart: 15, of which 4 were waited for; matrix products, arithmetic and copies ran while one was open for 1% of the time, Pallas kernels for 42%

profile of v4, /device:TPU:8, one launch (start us, length us, event | category | flops | bytes accessed | tf_op | source)
XLA Modules:
  0.0 145.4 jit_solution(13051957664867985972)
XLA Ops:
  0.0 0.5 collective-permute-start.4
  0.5 2.6 %collective-permute-start.1 = (bf16[128,2048]{1,0:T(8,128)(2,1)}, bf16[128,2048]{1,0:T(8,128)(2,1)}, u32[]{:S(2)}, u32[]{:S(2)}) collective-permute-start(bf16[128,2048]{1,0:T(8,128)(2,1)} %bitcast.3.saved_ref), channel_id=1, source_target_pairs={{0,4},{1,5},{2,6},{3,7},{4,0},{5,1},{6,2},{7,3},{8,12},{9,13},{10,... | collective-permute-start | bytes 1572872 | tf_op jit(solution)/shard_map/ppermute | solution.py:372
  3.1 0.4 collective-permute-start.5
  3.6 1.9 %copy-done = bf16[1,1,2048,768]{3,2,1,0:T(8,128)(2,1)S(1)} copy-done((bf16[1,1,2048,768]{3,2,1,0:T(8,128)(2,1)S(1)}, bf16[1,1,2048,768]{3,2,1,0:T(8,128)(2,1)}, u32[]{:S(2)}) %copy-start) | copy-done | bytes 3145752
  5.4 1.9 %copy-done.2 = bf16[1,1,2048,768]{3,2,1,0:T(8,128)(2,1)S(1)} copy-done((bf16[1,1,2048,768]{3,2,1,0:T(8,128)(2,1)S(1)}, bf16[1,1,2048,768]{3,2,1,0:T(8,128)(2,1)}, u32[]{:S(2)}) %copy-start.2) | copy-done | bytes 3145752
  7.3 0.7 copy-done.22
  8.0 2.8 %shard_map.83 = (f32[1,128,768]{2,1,0:T(8,128)S(1)}, f32[1,128,768]{2,1,0:T(8,128)S(1)}) custom-call(bf16[128,2048]{1,0:T(8,128)(2,1)} %bitcast.3.saved_ref, f32[1,2048]{1,0:T(1,128)S(1)} %copy-done.22, bf16[2048,768]{1,0:T(8,128)(2,1)S(1)} %bitcast.12, bf16[2048,768]{1,0:T(8,128)(2,1)S(1)} %bitcast.18), custom_call_target="tpu_custom_call" | custom-call | flops 1610612736 | bytes 6291456 | tf_op jit(solution)/shard_map/pallas_call | solution.py:185
  10.9 0.7 copy-done.30
  11.6 0.7 copy.9
  12.4 0.7 copy.10
  13.1 0.8 copy-done.32
  13.9 0.8 copy-done.33
  14.8 2.1 %shard_map.82.rows_ref = bf16[128,2176]{1,0:T(8,128)(2,1)} custom-call(bf16[128,2048]{1,0:T(8,128)(2,1)} %bitcast.upstream_ref, s32[128,4]{1,0:T(8,128)S(1)} %bitcast.25, f32[128,4]{1,0:T(8,128)S(1)} %bitcast.26), custom_call_target="tpu_custom_call" | custom-call | tf_op jit(solution)/shard_map/pallas_call | solution.py:145
  17.0 1.9 %copy-done.3 = bf16[1,1,2048,768]{3,2,1,0:T(8,128)(2,1)S(1)} copy-done((bf16[1,1,2048,768]{3,2,1,0:T(8,128)(2,1)S(1)}, bf16[1,1,2048,768]{3,2,1,0:T(8,128)(2,1)}, u32[]{:S(2)}) %copy-start.3) | copy-done | bytes 3145752
  18.9 1.9 %copy-done.19 = bf16[1,1,768,2048]{3,2,1,0:T(8,128)(2,1)S(1)} copy-done((bf16[1,1,768,2048]{3,2,1,0:T(8,128)(2,1)S(1)}, bf16[1,1,768,2048]{3,2,1,0:T(8,128)(2,1)}, u32[]{:S(2)}) %copy-start.19) | copy-done | bytes 3145752
  20.8 1.0 copy-done.31
  21.8 6.6 %shard_map.85 = (f32[128,2048]{1,0:T(8,128)S(1)}, bf16[768,2048]{1,0:T(8,128)(2,1)S(1)}, bf16[768,2048]{1,0:T(8,128)(2,1)S(1)}, bf16[2048,768]{1,0:T(8,128)(2,1)S(1)}) custom-call(s32[2]{0:T(128)S(1)} %pad_add_fusion.1.named_ref, bf16[128,2176]{1,0:T(8,128)(2,1)} %shard_map.82.rows_ref, f32[1,2048]{1,0:T(1,128)S(1)} %copy-done.23, ...), custom_call_target="tpu_custom_call" | custom-call | flops 2415919104 | bytes 9437184 | tf_op jit(solution)/shard_map/pallas_call | solution.py:250
  28.5 1.3 collective-permute-start
  29.8 0.7 collective-permute-start.11
  30.4 1.4 collective-permute-start.2
  31.8 4.6 %shard_map.84 = (f32[1,128,768]{2,1,0:T(8,128)S(1)}, f32[1,128,768]{2,1,0:T(8,128)S(1)}) custom-call(bf16[128,2048]{1,0:T(8,128)(2,1)} %bitcast.3.saved_ref, f32[1,2048]{1,0:T(1,128)S(1)} %copy-done.23, bf16[2048,768]{1,0:T(8,128)(2,1)} %collective-permute-done.3.refs_0_.refs_2_, bf16[2048,768]{1,0:T(8,128)(2,1)} %collective-permute-done.4.refs_1_.refs_3_, ...), custom_call_target="tpu_custom_call" | custom-call | flops 1610612736 | bytes 6291456 | tf_op jit(solution)/shard_map/pallas_call | solution.py:185
  36.5 9.6 %shard_map.86 = (bf16[128,2048]{1,0:T(8,128)(2,1)S(1)}, bf16[768,2048]{1,0:T(8,128)(2,1)S(1)}, bf16[768,2048]{1,0:T(8,128)(2,1)S(1)}, bf16[2048,768]{1,0:T(8,128)(2,1)S(1)}) custom-call(s32[2]{0:T(128)S(1)} %pad_add_fusion.named_ref, bf16[128,2176]{1,0:T(8,128)(2,1)} %shard_map.82.rows_ref, f32[1,2048]{1,0:T(1,128)S(1)} %copy-done.23, ...), custom_call_target="tpu_custom_call" | custom-call | flops 2415919104 | bytes 9437184 | tf_op jit(solution)/shard_map/pallas_call | solution.py:250
  46.1 2.5 %collective-permute-start.8 = (bf16[128,2048]{1,0:T(8,128)(2,1)S(1)}, bf16[128,2048]{1,0:T(8,128)(2,1)S(1)}, u32[]{:S(2)}, u32[]{:S(2)}) collective-permute-start(bf16[128,2048]{1,0:T(8,128)(2,1)S(1)} %get-tuple-element.36.refs_4_), channel_id=1, source_target_pairs={{0,24},{1,25},{2,26},{3,27},{4,28},{5,29},{6,30},{7,31},{8,0},{9,1... | collective-permute-start | bytes 1572872 | tf_op jit(solution)/shard_map/ppermute | solution.py:380
  48.6 6.1 %shard_map.87 = (f32[2,128,768]{2,1,0:T(8,128)S(1)}, f32[2,128,768]{2,1,0:T(8,128)S(1)}) custom-call(bf16[128,2048]{1,0:T(8,128)(2,1)} %collective-permute-done.1.saved_ref, f32[1,2048]{1,0:T(1,128)S(1)} %copy-done.23, bf16[2048,768]{1,0:T(8,128)(2,1)S(1)} %bitcast.14, bf16[2048,768]{1,0:T(8,128)(2,1)S(1)} %bitcast.20, ...), custom_call_target="tpu_custom_call" | custom-call | flops 3221225472 | bytes 12582912 | tf_op jit(solution)/shard_map/pallas_call | solution.py:185
  54.7 5.5 %shard_map.88 = (f32[2,128,768]{2,1,0:T(8,128)S(1)}, f32[2,128,768]{2,1,0:T(8,128)S(1)}) custom-call(bf16[128,2048]{1,0:T(8,128)(2,1)} %collective-permute-done.5.saved_ref, f32[1,2048]{1,0:T(1,128)S(1)} %copy-done.23, bf16[2048,768]{1,0:T(8,128)(2,1)S(1)} %bitcast.15, bf16[2048,768]{1,0:T(8,128)(2,1)S(1)} %bitcast.21, ...), custom_call_target="tpu_custom_call" | custom-call | flops 3221225472 | bytes 12582912 | tf_op jit(solution)/shard_map/pallas_call | solution.py:185
  60.2 0.9 copy-done.28
  61.1 5.2 %collective-permute-done.2.saved_ref = bf16[128,2048]{1,0:T(8,128)(2,1)S(1)} collective-permute-done((bf16[128,2048]{1,0:T(8,128)(2,1)}, bf16[128,2048]{1,0:T(8,128)(2,1)S(1)}, u32[]{:S(2)}, u32[]{:S(2)}) %collective-permute-start.2) | collective-permute-done | bytes 524320 | tf_op jit(solution)/shard_map/ppermute | solution.py:372
  66.3 5.4 %shard_map.89 = (f32[2,128,768]{2,1,0:T(8,128)S(1)}, f32[2,128,768]{2,1,0:T(8,128)S(1)}) custom-call(bf16[128,2048]{1,0:T(8,128)(2,1)S(1)} %collective-permute-done.2.saved_ref, f32[1,2048]{1,0:T(1,128)S(1)} %copy-done.23, bf16[2048,768]{1,0:T(8,128)(2,1)S(1)} %bitcast.16, bf16[2048,768]{1,0:T(8,128)(2,1)S(1)} %bitcast.22, ...), custom_call_target="tpu_custom_call" | custom-call | flops 3221225472 | bytes 12582912 | tf_op jit(solution)/shard_map/pallas_call | solution.py:185
  71.7 2.5 %collective-permute-start.7 = (bf16[128,2048]{1,0:T(8,128)(2,1)}, bf16[128,2048]{1,0:T(8,128)(2,1)S(1)}, u32[]{:S(2)}, u32[]{:S(2)}) collective-permute-start(bf16[128,2048]{1,0:T(8,128)(2,1)} %bitcast.3.saved_ref), channel_id=1, source_target_pairs={{0,24},{1,25},{2,26},{3,27},{4,28},{5,29},{6,30},{7,31},{8,0},{9,1... | collective-permute-start | bytes 1572872 | tf_op jit(solution)/shard_map/ppermute | solution.py:380
  74.2 1.7 %collective-permute-start.13 = (bf16[128,2176]{1,0:T(8,128)(2,1)}, bf16[128,2176]{1,0:T(8,128)(2,1)}, u32[]{:S(2)}, u32[]{:S(2)}) collective-permute-start(bf16[128,2176]{1,0:T(8,128)(2,1)} %collective-permute-done.rows_ref), channel_id=1, source_target_pairs={{0,2},{1,3},{2,0},{3,1},{4,6},{5,7},{6,4},{7,5},{8,10},{9,11},{10,... | collective-permute-start | bytes 1671176 | tf_op jit(solution)/shard_map/ppermute | solution.py:372
  76.0 6.1 %shard_map.90.refs_6_ = bf16[128,2048]{1,0:T(8,128)(2,1)S(1)} custom-call(s32[2]{0:T(128)S(1)} %pad_add_fusion.1.named_ref, bf16[128,2176]{1,0:T(8,128)(2,1)} %collective-permute-done.rows_ref, f32[1,2048]{1,0:T(1,128)S(1)} %copy-done.23, f32[2,128,768]{2,1,0:T(8,128)S(1)} %get-tuple-element.37.refs_4_.gate_ref, ...), custom_call_target="tpu_custom_call" | custom-call | flops 4831838208 | bytes 18874368 | tf_op jit(solution)/shard_map/pallas_call | solution.py:304
  82.2 0.6 collective-permute-start.9
  82.8 2.2 %collective-permute-start.10 = (bf16[128,2048]{1,0:T(8,128)(2,1)S(1)}, bf16[128,2048]{1,0:T(8,128)(2,1)S(1)}, u32[]{:S(2)}, u32[]{:S(2)}) collective-permute-start(bf16[128,2048]{1,0:T(8,128)(2,1)S(1)} %shard_map.90.refs_6_), channel_id=1, source_target_pairs={{0,2},{1,3},{2,30},{3,31},{4,24},{5,25},{6,4},{7,5},{8,10},{9,11},... | collective-permute-start | bytes 1572872 | tf_op jit(solution)/shard_map/ppermute | solution.py:396
  85.0 2.0 %collective-permute-done.7.refs_7_.saved_ref = bf16[128,2048]{1,0:T(8,128)(2,1)S(1)} collective-permute-done((bf16[128,2048]{1,0:T(8,128)(2,1)}, bf16[128,2048]{1,0:T(8,128)(2,1)S(1)}, u32[]{:S(2)}, u32[]{:S(2)}) %collective-permute-start.7) | collective-permute-done | bytes 524320 | tf_op jit(solution)/shard_map/ppermute | solution.py:380
  86.9 1.9 %copy-done.6 = bf16[768,2048]{1,0:T(8,128)(2,1)S(1)} copy-done((bf16[768,2048]{1,0:T(8,128)(2,1)S(1)}, bf16[768,2048]{1,0:T(8,128)(2,1)}, u32[]{:S(2)}) %copy-start.6) | copy-done | bytes 3145752
  88.8 1.9 %copy-done.8 = bf16[768,2048]{1,0:T(8,128)(2,1)S(1)} copy-done((bf16[768,2048]{1,0:T(8,128)(2,1)S(1)}, bf16[768,2048]{1,0:T(8,128)(2,1)}, u32[]{:S(2)}) %copy-start.8) | copy-done | bytes 3145752
  90.7 1.9 %copy-done.10 = bf16[2048,768]{1,0:T(8,128)(2,1)S(1)} copy-done((bf16[2048,768]{1,0:T(8,128)(2,1)S(1)}, bf16[2048,768]{1,0:T(8,128)(2,1)}, u32[]{:S(2)}) %copy-start.10) | copy-done | bytes 3145752
  92.6 1.9 %copy-done.12 = bf16[768,2048]{1,0:T(8,128)(2,1)S(1)} copy-done((bf16[768,2048]{1,0:T(8,128)(2,1)S(1)}, bf16[768,2048]{1,0:T(8,128)(2,1)}, u32[]{:S(2)}) %copy-start.12) | copy-done | bytes 3145752
  94.5 1.9 %copy-done.14 = bf16[768,2048]{1,0:T(8,128)(2,1)S(1)} copy-done((bf16[768,2048]{1,0:T(8,128)(2,1)S(1)}, bf16[768,2048]{1,0:T(8,128)(2,1)}, u32[]{:S(2)}) %copy-start.14) | copy-done | bytes 3145752
  96.4 1.9 %copy-done.16 = bf16[2048,768]{1,0:T(8,128)(2,1)S(1)} copy-done((bf16[2048,768]{1,0:T(8,128)(2,1)S(1)}, bf16[2048,768]{1,0:T(8,128)(2,1)}, u32[]{:S(2)}) %copy-start.16) | copy-done | bytes 3145752
  98.3 1.1 copy-done.29
  99.4 6.1 %shard_map.91.refs_6_ = bf16[128,2048]{1,0:T(8,128)(2,1)S(1)} custom-call(s32[2]{0:T(128)S(1)} %pad_add_fusion.1.named_ref, bf16[128,2176]{1,0:T(8,128)(2,1)} %collective-permute-done.11.rows_ref, f32[1,2048]{1,0:T(1,128)S(1)} %copy-done.23, f32[2,128,768]{2,1,0:T(8,128)S(1)} %copy-done.18, f32[2,128,768]{2,1,0:T(8,128)S(1)} %copy-done.29, ...), custom_call_target="tpu_custom_call" | custom-call | flops 4831838208 | bytes 18874368 | tf_op jit(solution)/shard_map/pallas_call | solution.py:304
  105.5 15.7 %collective-permute-start.12 = (bf16[128,2048]{1,0:T(8,128)(2,1)S(1)}, bf16[128,2048]{1,0:T(8,128)(2,1)S(1)}, u32[]{:S(2)}, u32[]{:S(2)}) collective-permute-start(bf16[128,2048]{1,0:T(8,128)(2,1)S(1)} %shard_map.91.refs_6_), channel_id=1, source_target_pairs={{0,26},{1,27},{2,24},{3,25},{4,30},{5,31},{6,28},{7,29},{8,2},{9,3... | collective-permute-start | bytes 1572872 | tf_op jit(solution)/shard_map/ppermute | solution.py:380
  121.2 6.0 %shard_map.93.refs_0_ = bf16[128,2048]{1,0:T(8,128)(2,1)S(1)} custom-call(s32[2]{0:T(128)S(1)} %pad_add_fusion.1.named_ref, bf16[128,2176]{1,0:T(8,128)(2,1)} %collective-permute-done.13.rows_ref, f32[1,2048]{1,0:T(1,128)S(1)} %copy-done.23, f32[2,128,768]{2,1,0:T(8,128)S(1)} %copy-done.25, f32[2,128,768]{2,1,0:T(8,128)S(1)} %copy-done.27, ...), custom_call_target="tpu_custom_call" | custom-call | flops 4831838208 | bytes 18874368 | tf_op jit(solution)/shard_map/pallas_call | solution.py:304
  127.5 0.6 collective-permute-start.14
  128.1 9.4 %collective-permute-done.12.refs_1_ = bf16[128,2048]{1,0:T(8,128)(2,1)S(1)} collective-permute-done((bf16[128,2048]{1,0:T(8,128)(2,1)S(1)}, bf16[128,2048]{1,0:T(8,128)(2,1)S(1)}, u32[]{:S(2)}, u32[]{:S(2)}) %collective-permute-start.12) | collective-permute-done | bytes 524320 | tf_op jit(solution)/shard_map/ppermute | solution.py:380
  137.7 6.3 %collective-permute-done.14.refs_1_ = bf16[128,2048]{1,0:T(8,128)(2,1)S(1)} collective-permute-done((bf16[128,2048]{1,0:T(8,128)(2,1)S(1)}, bf16[128,2048]{1,0:T(8,128)(2,1)S(1)}, u32[]{:S(2)}, u32[]{:S(2)}) %collective-permute-start.14) | collective-permute-done | bytes 524320 | tf_op jit(solution)/shard_map/ppermute | solution.py:380
  144.0 1.5 shard_map.95
  (72 shorter events, 0.7 us)
Async XLA Ops:
  0.0 29.8 %collective-permute-start.3 = (bf16[2048,768]{1,0:T(8,128)(2,1)}, bf16[2048,768]{1,0:T(8,128)(2,1)}, u32[]{:S(2)}, u32[]{:S(2)}) collective-permute-start(bf16[2048,768]{1,0:T(8,128)(2,1)} %bitcast.11), channel_id=1, source_target_pairs={{0,1},{1,0},{2,3},{3,2},{4,5},{5,4},{6,7},{7,6},{8,9},{9,8},{10,11... | collective-permute-start | bytes 9437192 | tf_op jit(solution)/shard_map/ppermute | solution.py:372
  0.0 30.4 %collective-permute-start.4 = (bf16[2048,768]{1,0:T(8,128)(2,1)}, bf16[2048,768]{1,0:T(8,128)(2,1)}, u32[]{:S(2)}, u32[]{:S(2)}) collective-permute-start(bf16[2048,768]{1,0:T(8,128)(2,1)} %bitcast.17), channel_id=1, source_target_pairs={{0,1},{1,0},{2,3},{3,2},{4,5},{5,4},{6,7},{7,6},{8,9},{9,8},{10,11... | collective-permute-start | bytes 9437192 | tf_op jit(solution)/shard_map/ppermute | solution.py:372
  0.5 36.0 %collective-permute-start.6 = (bf16[768,2048]{1,0:T(8,128)(2,1)}, bf16[768,2048]{1,0:T(8,128)(2,1)}, u32[]{:S(2)}, u32[]{:S(2)}) collective-permute-start(bf16[768,2048]{1,0:T(8,128)(2,1)} %bitcast.23), channel_id=1, source_target_pairs={{0,1},{1,0},{2,3},{3,2},{4,5},{5,4},{6,7},{7,6},{8,9},{9,8},{10,11... | collective-permute-start | bytes 9437192 | tf_op jit(solution)/shard_map/ppermute | solution.py:372
  0.5 27.9 %collective-permute-start.1 = (bf16[128,2048]{1,0:T(8,128)(2,1)}, bf16[128,2048]{1,0:T(8,128)(2,1)}, u32[]{:S(2)}, u32[]{:S(2)}) collective-permute-start(bf16[128,2048]{1,0:T(8,128)(2,1)} %bitcast.3.saved_ref), channel_id=1, source_target_pairs={{0,4},{1,5},{2,6},{3,7},{4,0},{5,1},{6,2},{7,3},{8,12},{9,13},{10,... | collective-permute-start | bytes 1572872 | tf_op jit(solution)/shard_map/ppermute | solution.py:372
  3.1 51.6 %collective-permute-start.5 = (bf16[128,2048]{1,0:T(8,128)(2,1)}, bf16[128,2048]{1,0:T(8,128)(2,1)}, u32[]{:S(2)}, u32[]{:S(2)}) collective-permute-start(bf16[128,2048]{1,0:T(8,128)(2,1)} %bitcast.3.saved_ref), channel_id=1, source_target_pairs={{0,2},{1,3},{2,0},{3,1},{4,6},{5,7},{6,4},{7,5},{8,10},{9,11},{10,... | collective-permute-start | bytes 1572872 | tf_op jit(solution)/shard_map/ppermute | solution.py:372
  3.6 1.9 %copy-start = (bf16[1,1,2048,768]{3,2,1,0:T(8,128)(2,1)S(1)}, bf16[1,1,2048,768]{3,2,1,0:T(8,128)(2,1)}, u32[]{:S(2)}) copy-start(bf16[1,1,2048,768]{3,2,1,0:T(8,128)(2,1)} %param.11) | copy-start | bytes 9437188
  5.4 1.9 %copy-start.2 = (bf16[1,1,2048,768]{3,2,1,0:T(8,128)(2,1)S(1)}, bf16[1,1,2048,768]{3,2,1,0:T(8,128)(2,1)}, u32[]{:S(2)}) copy-start(bf16[1,1,2048,768]{3,2,1,0:T(8,128)(2,1)} %param.12) | copy-start | bytes 9437188
  8.0 3.6 %copy-start.34 = (s32[1,128,4]{1,2,0:T(4,128)S(1)}, s32[1,128,4]{1,2,0:T(4,128)}, u32[]{:S(2)}) copy-start(s32[1,128,4]{1,2,0:T(4,128)} %param.14) | copy-start | bytes 6148
  8.0 4.3 %copy-start.35 = (f32[1,128,4]{1,2,0:T(4,128)S(1)}, f32[1,128,4]{1,2,0:T(4,128)}, u32[]{:S(2)}) copy-start(f32[1,128,4]{1,2,0:T(4,128)} %param.15) | copy-start | bytes 6148
  8.0 9.0 %copy-start.1 = (bf16[1,1,2048,768]{3,2,1,0:T(8,128)(2,1)S(1)}, bf16[1,1,2048,768]{3,2,1,0:T(8,128)(2,1)}, u32[]{:S(2)}) copy-start(bf16[1,1,2048,768]{3,2,1,0:T(8,128)(2,1)} %param.11) | copy-start | bytes 9437188
  8.0 9.0 %copy-start.23 = (f32[1,2048]{1,0:T(1,128)S(1)}, f32[1,2048]{1,0:T(1,128)}, u32[]{:S(2)}) copy-start(f32[1,2048]{1,0:T(1,128)} %gain_ref.19) | copy-start | bytes 24580
  13.1 0.8 copy-start.32
  17.0 1.9 %copy-start.3 = (bf16[1,1,2048,768]{3,2,1,0:T(8,128)(2,1)S(1)}, bf16[1,1,2048,768]{3,2,1,0:T(8,128)(2,1)}, u32[]{:S(2)}) copy-start(bf16[1,1,2048,768]{3,2,1,0:T(8,128)(2,1)} %param.12) | copy-start | bytes 9437188
  18.9 1.9 %copy-start.19 = (bf16[1,1,768,2048]{3,2,1,0:T(8,128)(2,1)S(1)}, bf16[1,1,768,2048]{3,2,1,0:T(8,128)(2,1)}, u32[]{:S(2)}) copy-start(bf16[1,1,768,2048]{3,2,1,0:T(8,128)(2,1)} %param.13) | copy-start | bytes 9437188
  20.8 1.0 copy-start.31
  28.4 47.6 %copy-start.5 = (bf16[768,2048]{1,0:T(8,128)(2,1)}, bf16[768,2048]{1,0:T(8,128)(2,1)S(1)}, u32[]{:S(2)}) copy-start(bf16[768,2048]{1,0:T(8,128)(2,1)S(1)} %get-tuple-element.43.refs_0_) | copy-start | bytes 9437188
  28.4 47.5 %copy-start.7 = (bf16[768,2048]{1,0:T(8,128)(2,1)}, bf16[768,2048]{1,0:T(8,128)(2,1)S(1)}, u32[]{:S(2)}) copy-start(bf16[768,2048]{1,0:T(8,128)(2,1)S(1)} %get-tuple-element.44.refs_1_) | copy-start | bytes 9437188
  28.4 47.5 %copy-start.9 = (bf16[2048,768]{1,0:T(8,128)(2,1)}, bf16[2048,768]{1,0:T(8,128)(2,1)S(1)}, u32[]{:S(2)}) copy-start(bf16[2048,768]{1,0:T(8,128)(2,1)S(1)} %get-tuple-element.45.refs_2_) | copy-start | bytes 9437188
  28.5 43.3 %collective-permute-start = (bf16[128,2176]{1,0:T(8,128)(2,1)}, bf16[128,2176]{1,0:T(8,128)(2,1)}, u32[]{:S(2)}, u32[]{:S(2)}) collective-permute-start(bf16[128,2176]{1,0:T(8,128)(2,1)} %shard_map.82.rows_ref), channel_id=1, source_target_pairs={{0,4},{1,5},{2,6},{3,7},{4,0},{5,1},{6,2},{7,3},{8,12},{9,13},{10,... | collective-permute-start | bytes 1671176 | tf_op jit(solution)/shard_map/ppermute | solution.py:372
  29.8 55.2 %collective-permute-start.11 = (bf16[128,2176]{1,0:T(8,128)(2,1)}, bf16[128,2176]{1,0:T(8,128)(2,1)}, u32[]{:S(2)}, u32[]{:S(2)}) collective-permute-start(bf16[128,2176]{1,0:T(8,128)(2,1)} %shard_map.82.rows_ref), channel_id=1, source_target_pairs={{0,2},{1,3},{2,0},{3,1},{4,6},{5,7},{6,4},{7,5},{8,10},{9,11},{10,... | collective-permute-start | bytes 1671176 | tf_op jit(solution)/shard_map/ppermute | solution.py:372
  30.4 35.9 %collective-permute-start.2 = (bf16[128,2048]{1,0:T(8,128)(2,1)}, bf16[128,2048]{1,0:T(8,128)(2,1)S(1)}, u32[]{:S(2)}, u32[]{:S(2)}) collective-permute-start(bf16[128,2048]{1,0:T(8,128)(2,1)} %collective-permute-done.1.saved_ref), channel_id=1, source_target_pairs={{0,2},{1,3},{2,0},{3,1},{4,6},{5,7},{6,4},{7,5},{8,10},{9,11},{10,... | collective-permute-start | bytes 1572872 | tf_op jit(solution)/shard_map/ppermute | solution.py:372
  36.5 12.1 %copy-start.4 = (bf16[1,1,2048,768]{3,2,1,0:T(8,128)(2,1)S(1)}, bf16[1,1,2048,768]{3,2,1,0:T(8,128)(2,1)}, u32[]{:S(2)}) copy-start(bf16[1,1,2048,768]{3,2,1,0:T(8,128)(2,1)} %param.12) | copy-start | bytes 9437188
  46.1 29.9 %copy-start.11 = (bf16[768,2048]{1,0:T(8,128)(2,1)}, bf16[768,2048]{1,0:T(8,128)(2,1)S(1)}, u32[]{:S(2)}) copy-start(bf16[768,2048]{1,0:T(8,128)(2,1)S(1)} %get-tuple-element.46.refs_3_) | copy-start | bytes 9437188
  46.1 29.9 %copy-start.13 = (bf16[768,2048]{1,0:T(8,128)(2,1)}, bf16[768,2048]{1,0:T(8,128)(2,1)S(1)}, u32[]{:S(2)}) copy-start(bf16[768,2048]{1,0:T(8,128)(2,1)S(1)} %get-tuple-element.47.refs_4_) | copy-start | bytes 9437188
  46.1 29.9 %copy-start.15 = (bf16[2048,768]{1,0:T(8,128)(2,1)}, bf16[2048,768]{1,0:T(8,128)(2,1)S(1)}, u32[]{:S(2)}) copy-start(bf16[2048,768]{1,0:T(8,128)(2,1)S(1)} %get-tuple-element.48.refs_5_) | copy-start | bytes 9437188
  46.1 29.9 %collective-permute-start.8 = (bf16[128,2048]{1,0:T(8,128)(2,1)S(1)}, bf16[128,2048]{1,0:T(8,128)(2,1)S(1)}, u32[]{:S(2)}, u32[]{:S(2)}) collective-permute-start(bf16[128,2048]{1,0:T(8,128)(2,1)S(1)} %get-tuple-element.36.refs_4_), channel_id=1, source_target_pairs={{0,24},{1,25},{2,26},{3,27},{4,28},{5,29},{6,30},{7,31},{8,0},{9,1... | collective-permute-start | bytes 1572872 | tf_op jit(solution)/shard_map/ppermute | solution.py:380
  60.2 0.9 copy-start.28
  61.1 10.6 %copy-start.17 = (f32[2,128,768]{2,1,0:T(8,128)}, f32[2,128,768]{2,1,0:T(8,128)S(1)}, u32[]{:S(2)}) copy-start(f32[2,128,768]{2,1,0:T(8,128)S(1)} %get-tuple-element.38.refs_4_.gate_ref) | copy-start | bytes 2359300
  71.7 10.4 %copy-start.24 = (f32[2,128,768]{2,1,0:T(8,128)}, f32[2,128,768]{2,1,0:T(8,128)S(1)}, u32[]{:S(2)}) copy-start(f32[2,128,768]{2,1,0:T(8,128)S(1)} %get-tuple-element.53.gate_ref) | copy-start | bytes 2359300
  71.7 10.4 %copy-start.26 = (f32[2,128,768]{2,1,0:T(8,128)}, f32[2,128,768]{2,1,0:T(8,128)S(1)}, u32[]{:S(2)}) copy-start(f32[2,128,768]{2,1,0:T(8,128)S(1)} %get-tuple-element.54.up_ref) | copy-start | bytes 2359300
  71.7 15.2 %collective-permute-start.7 = (bf16[128,2048]{1,0:T(8,128)(2,1)}, bf16[128,2048]{1,0:T(8,128)(2,1)S(1)}, u32[]{:S(2)}, u32[]{:S(2)}) collective-permute-start(bf16[128,2048]{1,0:T(8,128)(2,1)} %bitcast.3.saved_ref), channel_id=1, source_target_pairs={{0,24},{1,25},{2,26},{3,27},{4,28},{5,29},{6,30},{7,31},{8,0},{9,1... | collective-permute-start | bytes 1572872 | tf_op jit(solution)/shard_map/ppermute | solution.py:380
  74.2 47.0 %collective-permute-start.13 = (bf16[128,2176]{1,0:T(8,128)(2,1)}, bf16[128,2176]{1,0:T(8,128)(2,1)}, u32[]{:S(2)}, u32[]{:S(2)}) collective-permute-start(bf16[128,2176]{1,0:T(8,128)(2,1)} %collective-permute-done.rows_ref), channel_id=1, source_target_pairs={{0,2},{1,3},{2,0},{3,1},{4,6},{5,7},{6,4},{7,5},{8,10},{9,11},{10,... | collective-permute-start | bytes 1671176 | tf_op jit(solution)/shard_map/ppermute | solution.py:372
  76.0 6.2 %copy-start.20 = (bf16[128,2048]{1,0:T(8,128)(2,1)}, bf16[128,2048]{1,0:T(8,128)(2,1)S(1)}, u32[]{:S(2)}) copy-start(bf16[128,2048]{1,0:T(8,128)(2,1)S(1)} %collective-permute-done.8.refs_6_.refs_0_) | copy-start | bytes 1572868
  76.0 10.9 %copy-start.18 = (f32[2,128,768]{2,1,0:T(8,128)S(1)}, f32[2,128,768]{2,1,0:T(8,128)}, u32[]{:S(2)}) copy-start(f32[2,128,768]{2,1,0:T(8,128)} %copy-done.17) | copy-start | bytes 2359300
  82.2 39.0 %collective-permute-start.9 = (bf16[128,2048]{1,0:T(8,128)(2,1)}, bf16[128,2048]{1,0:T(8,128)(2,1)S(1)}, u32[]{:S(2)}, u32[]{:S(2)}) collective-permute-start(bf16[128,2048]{1,0:T(8,128)(2,1)} %bitcast.upstream_ref), channel_id=1, source_target_pairs={{0,24},{1,25},{2,26},{3,27},{4,28},{5,29},{6,30},{7,31},{8,0},{9,1... | collective-permute-start | bytes 1572872 | tf_op jit(solution)/shard_map/ppermute | solution.py:380
  82.8 44.5 %collective-permute-start.10 = (bf16[128,2048]{1,0:T(8,128)(2,1)S(1)}, bf16[128,2048]{1,0:T(8,128)(2,1)S(1)}, u32[]{:S(2)}, u32[]{:S(2)}) collective-permute-start(bf16[128,2048]{1,0:T(8,128)(2,1)S(1)} %shard_map.90.refs_6_), channel_id=1, source_target_pairs={{0,2},{1,3},{2,30},{3,31},{4,24},{5,25},{6,4},{7,5},{8,10},{9,11},... | collective-permute-start | bytes 1572872 | tf_op jit(solution)/shard_map/ppermute | solution.py:396
  86.9 1.9 %copy-start.6 = (bf16[768,2048]{1,0:T(8,128)(2,1)S(1)}, bf16[768,2048]{1,0:T(8,128)(2,1)}, u32[]{:S(2)}) copy-start(bf16[768,2048]{1,0:T(8,128)(2,1)} %copy-done.5) | copy-start | bytes 9437188
  88.8 1.9 %copy-start.8 = (bf16[768,2048]{1,0:T(8,128)(2,1)S(1)}, bf16[768,2048]{1,0:T(8,128)(2,1)}, u32[]{:S(2)}) copy-start(bf16[768,2048]{1,0:T(8,128)(2,1)} %copy-done.7) | copy-start | bytes 9437188
  90.7 1.9 %copy-start.10 = (bf16[2048,768]{1,0:T(8,128)(2,1)S(1)}, bf16[2048,768]{1,0:T(8,128)(2,1)}, u32[]{:S(2)}) copy-start(bf16[2048,768]{1,0:T(8,128)(2,1)} %copy-done.9) | copy-start | bytes 9437188
  92.6 1.9 %copy-start.12 = (bf16[768,2048]{1,0:T(8,128)(2,1)S(1)}, bf16[768,2048]{1,0:T(8,128)(2,1)}, u32[]{:S(2)}) copy-start(bf16[768,2048]{1,0:T(8,128)(2,1)} %copy-done.11) | copy-start | bytes 9437188
  94.5 1.9 %copy-start.14 = (bf16[768,2048]{1,0:T(8,128)(2,1)S(1)}, bf16[768,2048]{1,0:T(8,128)(2,1)}, u32[]{:S(2)}) copy-start(bf16[768,2048]{1,0:T(8,128)(2,1)} %copy-done.13) | copy-start | bytes 9437188
  96.4 1.9 %copy-start.16 = (bf16[2048,768]{1,0:T(8,128)(2,1)S(1)}, bf16[2048,768]{1,0:T(8,128)(2,1)}, u32[]{:S(2)}) copy-start(bf16[2048,768]{1,0:T(8,128)(2,1)} %copy-done.15) | copy-start | bytes 9437188
  98.3 1.1 copy-start.29
  99.4 21.8 %copy-start.25 = (f32[2,128,768]{2,1,0:T(8,128)S(1)}, f32[2,128,768]{2,1,0:T(8,128)}, u32[]{:S(2)}) copy-start(f32[2,128,768]{2,1,0:T(8,128)} %copy-done.24) | copy-start | bytes 2359300
  99.4 21.8 %copy-start.27 = (f32[2,128,768]{2,1,0:T(8,128)S(1)}, f32[2,128,768]{2,1,0:T(8,128)}, u32[]{:S(2)}) copy-start(f32[2,128,768]{2,1,0:T(8,128)} %copy-done.26) | copy-start | bytes 2359300
  105.5 32.0 %collective-permute-start.12 = (bf16[128,2048]{1,0:T(8,128)(2,1)S(1)}, bf16[128,2048]{1,0:T(8,128)(2,1)S(1)}, u32[]{:S(2)}, u32[]{:S(2)}) collective-permute-start(bf16[128,2048]{1,0:T(8,128)(2,1)S(1)} %shard_map.91.refs_6_), channel_id=1, source_target_pairs={{0,26},{1,27},{2,24},{3,25},{4,30},{5,31},{6,28},{7,29},{8,2},{9,3... | collective-permute-start | bytes 1572872 | tf_op jit(solution)/shard_map/ppermute | solution.py:380
  121.2 16.3 %copy-start.21 = (bf16[128,2048]{1,0:T(8,128)(2,1)S(1)}, bf16[128,2048]{1,0:T(8,128)(2,1)}, u32[]{:S(2)}) copy-start(bf16[128,2048]{1,0:T(8,128)(2,1)} %copy-done.20) | copy-start | bytes 1572868
  127.5 16.5 %collective-permute-start.14 = (bf16[128,2048]{1,0:T(8,128)(2,1)S(1)}, bf16[128,2048]{1,0:T(8,128)(2,1)S(1)}, u32[]{:S(2)}, u32[]{:S(2)}) collective-permute-start(bf16[128,2048]{1,0:T(8,128)(2,1)S(1)} %shard_map.94), channel_id=1, source_target_pairs={{0,30},{1,31},{2,28},{3,29},{4,26},{5,27},{6,24},{7,25},{8,6},{9,7... | collective-permute-start | bytes 1572872 | tf_op jit(solution)/shard_map/ppermute | solution.py:380
  (3 other events, 2.3 us)

commit v5 on v4

--- a/solution.py
+++ b/solution.py
@@ -116,7 +116,6 @@
 
 tile = 256
 in_vmem = pl.BlockSpec(memory_space=pltpu.VMEM)
-in_smem = pl.BlockSpec(memory_space=pltpu.SMEM)
 anywhere = pl.BlockSpec(memory_space=pl.ANY)
 
 
@@ -127,12 +126,15 @@
 def shared_kernel(experts, upstream_ref, ids_ref, share_ref, out_ref):
     size, width = upstream_ref.shape
     lanes = out_ref.shape[1] - width
+    top = ids_ref.shape[0]
     out_ref[:, :width] = upstream_ref[...]
+    both = jnp.concatenate([ids_ref[...].astype(jnp.float32), share_ref[...]], axis=0).T
     lane = lax.broadcasted_iota(jnp.int32, (size, lanes), 1)
+    expert = lax.rem(lane, experts).astype(jnp.float32)
     dense = jnp.zeros((size, lanes), jnp.float32)
-    for k in range(ids_ref.shape[1]):
-        hit = lax.rem(lane, experts) == ids_ref[:, k : k + 1]
-        dense = dense + jnp.where(hit, share_ref[:, k : k + 1], 0.0)
+    for k in range(top):
+        hit = expert == both[:, k : k + 1]
+        dense = dense + jnp.where(hit, both[:, top + k : top + k + 1], 0.0)
     high = dense.astype(jnp.bfloat16).astype(jnp.float32)
     middle = (dense - high).astype(jnp.bfloat16).astype(jnp.float32)
     low = dense - high - middle
@@ -197,20 +199,21 @@
     )(rows, gain_row, *flat, *after)
 
 
-def share_of(rows_ref, width, experts, named):
+def share_of(rows_ref, width, experts, flip):
+    named = lax.axis_index("expert") ^ flip
     parts = rows_ref[:, width:].astype(jnp.float32)
     lane = lax.broadcasted_iota(jnp.int32, parts.shape, 1)
     wanted = (lax.rem(lane, experts) == named) & (lane < 3 * experts)
     return jnp.sum(jnp.where(wanted, parts, 0.0), axis=1, keepdims=True)
 
 
-def turning_kernel(experts, start, named_ref, rows_ref, gain_ref, gate_ref, up_ref, *refs):
+def turning_kernel(experts, start, flip, rows_ref, gain_ref, gate_ref, up_ref, *refs):
     weight_refs, refs = refs[:3], refs[3:]
     base_ref = refs[0] if start else None
     out_ref, gate_turned, up_turned, down_turned, gate_grads, up_grads = refs[-6:]
     width = out_ref.shape[1]
     hidden = gate_ref.shape[2]
-    share = share_of(rows_ref, width, experts, named_ref[0])
+    share = share_of(rows_ref, width, experts, flip)
 
     def grads_of(step, carry):
         cut = tile_cut(step)
@@ -241,15 +244,15 @@
     lax.fori_loop(0, width // tile, pieces_of, 0)
 
 
-def turning_pieces(named, rows, gain_row, factors, weights, experts, kind, base):
+def turning_pieces(flip, rows, gain_row, factors, weights, experts, kind, base):
     _, count, hidden = factors[0].shape
     width = weights[0].shape[0]
     start = [] if base is None else [base]
     turned = jax.ShapeDtypeStruct((hidden, width), jnp.bfloat16)
     down_turned = jax.ShapeDtypeStruct((width, hidden), jnp.bfloat16)
     return pl.pallas_call(
-        functools.partial(turning_kernel, experts, len(start)),
-        in_specs=[in_smem] + [in_vmem] * (7 + len(start)),
+        functools.partial(turning_kernel, experts, len(start), flip),
+        in_specs=[in_vmem] * (7 + len(start)),
         out_specs=[in_vmem] * 4,
         out_shape=[jax.ShapeDtypeStruct((count, width), kind), turned, turned, down_turned],
         scratch_shapes=[pltpu.VMEM((count, hidden), jnp.bfloat16)] * 2,
@@ -259,15 +262,15 @@
             transcendentals=0,
         ),
         compiler_params=pltpu.CompilerParams(vmem_limit_bytes=12 << 20),
-    )(named, rows, gain_row, *factors, *weights, *start)
-
-
-def pieces_kernel(experts, pairs, named_ref, rows_ref, gain_ref, gate_ref, up_ref, *refs):
+    )(rows, gain_row, *factors, *weights, *start)
+
+
+def pieces_kernel(experts, pairs, rows_ref, gain_ref, gate_ref, up_ref, *refs):
     weight_refs = refs[: 3 * pairs]
     out_ref, gate_grads, up_grads = refs[-3:]
     width = out_ref.shape[1]
     hidden = gate_ref.shape[2]
-    shares = [share_of(rows_ref, width, experts, named_ref[w]) for w in range(pairs)]
+    shares = [share_of(rows_ref, width, experts, w) for w in range(pairs)]
 
     def grads_of(step, carry):
         cut = tile_cut(step)
@@ -297,13 +300,13 @@
     lax.fori_loop(0, width // tile, pieces_of, 0)
 
 
-def slot_pieces(named, rows, gain_row, factors, weights, experts, after):
+def slot_pieces(rows, gain_row, factors, weights, experts, after):
     pairs, count, hidden = factors[0].shape
     width = weights[0][0].shape[1]
     flat = [w for group in weights for w in group]
     return pl.pallas_call(
         functools.partial(pieces_kernel, experts, pairs),
-        in_specs=[in_smem] + [in_vmem] * (4 + len(flat)) + [anywhere] * len(after),
+        in_specs=[in_vmem] * (4 + len(flat)) + [anywhere] * len(after),
         out_specs=in_vmem,
         out_shape=jax.ShapeDtypeStruct((count, width), jnp.bfloat16),
         scratch_shapes=[pltpu.VMEM((pairs, count, hidden), jnp.bfloat16)] * 2,
@@ -313,7 +316,7 @@
             transcendentals=0,
         ),
         compiler_params=pltpu.CompilerParams(vmem_limit_bytes=8 << 20),
-    )(named, rows, gain_row, *factors, *flat, *after)
+    )(rows, gain_row, *factors, *flat, *after)
 
 
 def final_kernel(saved_ref, upstream_ref, *refs):
@@ -339,22 +342,24 @@
     )(saved_rows, upstream_rows, *pieces)
 
 
-def joined_kernel(at_ends, is_end_ref, some_ref, *refs):
+def joined_kernel(experts, at_ends, some_ref, *refs):
     out_ref = refs[-1]
-    total = jnp.where(is_end_ref[0] == at_ends, some_ref[...].astype(jnp.float32), 0.0)
+    me = lax.axis_index("expert")
+    is_end = ((me < 2) | (me >= experts - 2)).astype(jnp.int32)
+    total = jnp.where(is_end == at_ends, some_ref[...].astype(jnp.float32), 0.0)
     for ref in refs[:-1]:
         total = total + ref[...].astype(jnp.float32)
     out_ref[...] = total.astype(out_ref.dtype)
 
 
-def joined(is_end, at_ends, some, pieces, kind):
-    return pl.pallas_call(
-        functools.partial(joined_kernel, at_ends),
-        in_specs=[in_smem] + [in_vmem] * (1 + len(pieces)),
+def joined(experts, at_ends, some, pieces, kind):
+    return pl.pallas_call(
+        functools.partial(joined_kernel, experts, at_ends),
+        in_specs=[in_vmem] * (1 + len(pieces)),
         out_specs=in_vmem,
         out_shape=jax.ShapeDtypeStruct(some.shape, kind),
         compiler_params=pltpu.CompilerParams(vmem_limit_bytes=8 << 20),
-    )(is_end, some, *pieces)
+    )(some, *pieces)
 
 
 def line_device(
@@ -364,9 +369,6 @@
     saved_rows, upstream_rows = saved_input[0], upstream[0]
     experts = lax.axis_size("expert")
     sections = lax.axis_size("section")
-    me = lax.axis_index("expert")
-    named = jnp.stack([me, me ^ 1]).astype(jnp.int32)
-    swapped = jnp.stack([me ^ 1, me]).astype(jnp.int32)
 
     def hop(by):
         return lambda value: lax.ppermute(value, "expert", [(i, i ^ by) for i in range(experts)])
@@ -379,13 +381,12 @@
         ]
         return lambda value: lax.ppermute(value, ("section", "expert"), pairs)
 
-    shared = shared_rows(upstream_rows, expert_ids[0], gate_share[0], experts)
+    shared = shared_rows(upstream_rows, expert_ids[0].T, gate_share[0].T, experts)
     x_two, x_one = hop(4)(saved_rows), hop(2)(saved_rows)
     gate_other, up_other = hop(1)(own[0]), hop(1)(own[1])
     u_two = hop(4)(shared)
     gain = norm_gain
     ends = (0, 1, experts - 2, experts - 1)
-    is_end = ((me < 2) | (me >= experts - 2)).astype(jnp.int32).reshape(1)
 
     def second_hop(value):
         pairs = []
@@ -403,10 +404,10 @@
     other_factors = slot_factors(saved_rows, gain, (other,), [gate])
     both = (own, other)
     here, *own_turned = turning_pieces(
-        named, shared, gain, own_factors, own, experts, jnp.float32, None
+        0, shared, gain, own_factors, own, experts, jnp.float32, None
     )
     here, *other_turned = turning_pieces(
-        swapped, shared, gain, other_factors, other, experts, jnp.bfloat16, here
+        1, shared, gain, other_factors, other, experts, jnp.bfloat16, here
     )
     turned = (own_turned, other_turned)
     x_three = hop(2)(x_two)
@@ -420,15 +421,15 @@
     next_saved = handed(0)(saved_later)
     here_next = handed(0)(here)
     u_three = hop(2)(u_two)
-    two = slot_pieces(named, u_two, gain, two_factors, turned, experts, [here_next])
+    two = slot_pieces(u_two, gain, two_factors, turned, experts, [here_next])
     two_next = second_hop(two)
     upstream_later, two = lax.optimization_barrier((upstream_rows, two))
     next_upstream = handed(0)(upstream_later)
-    one = slot_pieces(named, u_one, gain, one_factors, turned, experts, [two, next_saved])
+    one = slot_pieces(u_one, gain, one_factors, turned, experts, [two])
     one_next = handed(2)(one)
-    three = slot_pieces(named, u_three, gain, three_factors, turned, experts, [one, next_upstream])
-    three = joined(is_end, 0, two_next, [three], jnp.bfloat16)
-    summed = joined(is_end, 1, two_next, [here_next, one_next], jnp.float32)
+    three = slot_pieces(u_three, gain, three_factors, turned, experts, [one, next_saved])
+    three = joined(experts, 0, two_next, [three], jnp.bfloat16)
+    summed = joined(experts, 1, two_next, [here_next, one_next], jnp.float32)
     three_next = handed(6)(three)
     return finish(next_saved, next_upstream, [summed, three_next])[None]
 

time: 146 us -> 132 us (0.904)
  the two profiles are of different devices: /device:TPU:8 before, /device:TPU:0 now
where the time goes in v5:
time: 132 us
  waiting for transfers between devices  50.4 us (38%)
  Pallas kernels  38.8 us (29%)
  starting transfers between devices  31.4 us (24%)
  local copies, waits for them, and re-layouts  11 us (8%)
    ppermute x5, waiting for transfers between devices, handed(): return lambda value: lax.ppermute(value, ('section', 'expert'), pairs)  26.6 us
    ppermute x9, waiting for transfers between devices, hop(): lax.ppermute(value, 'expert', [(i, i ^ by) for i in range(experts)])  23.8 us
    ppermute x5, starting transfers between devices, handed(): return lambda value: lax.ppermute(value, ('section', 'expert'), pairs)  19.2 us
    pallas_call x3, Pallas kernels, slot_pieces(): pl.pallas_call(functools.partial(pieces_kernel, experts, pairs), in_specs...  14.7 us
    pallas_call x2, Pallas kernels, turning_pieces(): pl.pallas_call(functools.partial(turning_kernel, experts, len(start), fli...  11.1 us
    unnamed x26, local copies, waits for them, and re-layouts  11 us
    pallas_call x5, Pallas kernels, slot_factors(): pl.pallas_call(functools.partial(factors_kernel, pairs), in_specs=[in_vme...  10.8 us
    ppermute x9, starting transfers between devices, hop(): lax.ppermute(value, 'expert', [(i, i ^ by) for i in range(experts)])  10.3 us
  transfers between devices with their start and end apart: 15, of which 5 were waited for; matrix products, arithmetic and copies ran while one was open for 0% of the time, Pallas kernels for 28%

profile of v5, /device:TPU:0, one launch (start us, length us, event | category | flops | bytes accessed | tf_op | source)
XLA Modules:
  0.0 131.9 jit_solution(16585150965565439349)
XLA Ops:
  0.0 0.5 collective-permute-start.3
  0.5 0.1 collective-permute-start.4
  0.5 0.5 collective-permute-start.6
  1.0 3.6 %collective-permute-start.1 = (bf16[128,2048]{1,0:T(8,128)(2,1)}, bf16[128,2048]{1,0:T(8,128)(2,1)S(1)}, u32[]{:S(2)}, u32[]{:S(2)}) collective-permute-start(bf16[128,2048]{1,0:T(8,128)(2,1)} %bitcast.26), channel_id=1, source_target_pairs={{0,4},{1,5},{2,6},{3,7},{4,0},{5,1},{6,2},{7,3},{8,12},{9,13},{10,... | collective-permute-start | bytes 1572872 | tf_op jit(solution)/shard_map/ppermute | solution.py:374
  4.6 1.6 %collective-permute-start.5 = (bf16[128,2048]{1,0:T(8,128)(2,1)}, bf16[128,2048]{1,0:T(8,128)(2,1)S(1)}, u32[]{:S(2)}, u32[]{:S(2)}) collective-permute-start(bf16[128,2048]{1,0:T(8,128)(2,1)} %bitcast.27), channel_id=1, source_target_pairs={{0,2},{1,3},{2,0},{3,1},{4,6},{5,7},{6,4},{7,5},{8,10},{9,11},{10,... | collective-permute-start | bytes 1572872 | tf_op jit(solution)/shard_map/ppermute | solution.py:374
  6.1 1.0 copy-done.9
  7.2 0.7 copy-done.11
  7.9 0.7 copy-done.12
  8.5 0.3 shard_map.82.rows_ref
  8.9 0.0 copy-start
  8.9 1.9 %copy-done = bf16[1,1,2048,768]{3,2,1,0:T(8,128)(2,1)S(1)} copy-done((bf16[1,1,2048,768]{3,2,1,0:T(8,128)(2,1)S(1)}, bf16[1,1,2048,768]{3,2,1,0:T(8,128)(2,1)}, u32[]{:S(2)}) %copy-start) | copy-done | bytes 3145752
  10.8 1.9 %copy-done.2 = bf16[1,1,2048,768]{3,2,1,0:T(8,128)(2,1)S(1)} copy-done((bf16[1,1,2048,768]{3,2,1,0:T(8,128)(2,1)S(1)}, bf16[1,1,2048,768]{3,2,1,0:T(8,128)(2,1)}, u32[]{:S(2)}) %copy-start.2) | copy-done | bytes 3145752
  12.7 1.0 copy-done.5
  13.7 0.7 copy-done.7
  14.4 1.6 %shard_map.83 = (f32[1,128,768]{2,1,0:T(8,128)S(1)}, f32[1,128,768]{2,1,0:T(8,128)S(1)}) custom-call(bf16[128,2048]{1,0:T(8,128)(2,1)S(1)} %bitcast.28, f32[1,2048]{1,0:T(1,128)S(1)} %copy-done.7, bf16[2048,768]{1,0:T(8,128)(2,1)S(1)} %bitcast.13, bf16[2048,768]{1,0:T(8,128)(2,1)S(1)} %bitcast.19), custom_call_target="tpu_custom_call" | custom-call | flops 1610612736 | bytes 6291456 | tf_op jit(solution)/shard_map/pallas_call | solution.py:187
  16.1 0.2 copy-done.1
  16.3 1.0 copy-done.3
  17.2 1.9 %copy-done.4 = bf16[1,1,768,2048]{3,2,1,0:T(8,128)(2,1)S(1)} copy-done((bf16[1,1,768,2048]{3,2,1,0:T(8,128)(2,1)S(1)}, bf16[1,1,768,2048]{3,2,1,0:T(8,128)(2,1)}, u32[]{:S(2)}) %copy-start.4) | copy-done | bytes 3145752
  19.1 5.5 %shard_map.85 = (f32[128,2048]{1,0:T(8,128)S(1)}, bf16[768,2048]{1,0:T(8,128)(2,1)S(1)}, bf16[768,2048]{1,0:T(8,128)(2,1)S(1)}, bf16[2048,768]{1,0:T(8,128)(2,1)S(1)}) custom-call(bf16[128,2176]{1,0:T(8,128)(2,1)S(1)} %shard_map.82.rows_ref, f32[1,2048]{1,0:T(1,128)S(1)} %copy-done.8, f32[1,128,768]{2,1,0:T(8,128)S(1)} %get-tuple-element.31.refs_2_.gate_ref, ...), custom_call_target="tpu_custom_call" | custom-call | flops 2415919104 | bytes 9437184 | tf_op jit(solution)/shard_map/pallas_call | solution.py:253
  24.7 4.0 %collective-permute-done.1.saved_ref = bf16[128,2048]{1,0:T(8,128)(2,1)S(1)} collective-permute-done((bf16[128,2048]{1,0:T(8,128)(2,1)}, bf16[128,2048]{1,0:T(8,128)(2,1)S(1)}, u32[]{:S(2)}, u32[]{:S(2)}) %collective-permute-start.1) | collective-permute-done | bytes 524320 | tf_op jit(solution)/shard_map/ppermute | solution.py:374
  28.7 0.0 collective-permute-start
  28.7 0.0 collective-permute-done.3.refs_0_.refs_2_
  28.7 4.0 %collective-permute-start.11 = (bf16[128,2176]{1,0:T(8,128)(2,1)S(1)}, bf16[128,2176]{1,0:T(8,128)(2,1)S(1)}, u32[]{:S(2)}, u32[]{:S(2)}) collective-permute-start(bf16[128,2176]{1,0:T(8,128)(2,1)S(1)} %shard_map.82.rows_ref), channel_id=1, source_target_pairs={{0,2},{1,3},{2,0},{3,1},{4,6},{5,7},{6,4},{7,5},{8,10},{9,11},{10,... | collective-permute-start | bytes 1671176 | tf_op jit(solution)/shard_map/ppermute | solution.py:374
  32.7 0.0 collective-permute-done.4.refs_1_.refs_3_
  32.7 0.1 collective-permute-start.2
  32.8 1.6 %shard_map.84 = (f32[1,128,768]{2,1,0:T(8,128)S(1)}, f32[1,128,768]{2,1,0:T(8,128)S(1)}) custom-call(bf16[128,2048]{1,0:T(8,128)(2,1)S(1)} %bitcast.29, f32[1,2048]{1,0:T(1,128)S(1)} %copy-done.8, bf16[2048,768]{1,0:T(8,128)(2,1)S(1)} %collective-permute-done.3.refs_0_.refs_2_, bf16[2048,768]{1,0:T(8,128)(2,1)S(1)} %collective-permute-done.4.refs_1_.refs_3_, ...), custom_call_target="tpu_custom_call" | custom-call | flops 1610612736 | bytes 6291456 | tf_op jit(solution)/shard_map/pallas_call | solution.py:187
  34.4 5.6 %shard_map.86 = (bf16[128,2048]{1,0:T(8,128)(2,1)S(1)}, bf16[768,2048]{1,0:T(8,128)(2,1)S(1)}, bf16[768,2048]{1,0:T(8,128)(2,1)S(1)}, bf16[2048,768]{1,0:T(8,128)(2,1)S(1)}) custom-call(bf16[128,2176]{1,0:T(8,128)(2,1)S(1)} %shard_map.82.rows_ref, f32[1,2048]{1,0:T(1,128)S(1)} %copy-done.8, f32[1,128,768]{2,1,0:T(8,128)S(1)} %get-tuple-element.32.gate_ref, ...), custom_call_target="tpu_custom_call" | custom-call | flops 2415919104 | bytes 9437184 | tf_op jit(solution)/shard_map/pallas_call | solution.py:253
  40.0 2.5 %collective-permute-start.8 = (bf16[128,2048]{1,0:T(8,128)(2,1)S(1)}, bf16[128,2048]{1,0:T(8,128)(2,1)S(1)}, u32[]{:S(2)}, u32[]{:S(2)}) collective-permute-start(bf16[128,2048]{1,0:T(8,128)(2,1)S(1)} %get-tuple-element.36.refs_4_), channel_id=1, source_target_pairs={{0,24},{1,25},{2,26},{3,27},{4,28},{5,29},{6,30},{7,31},{8,0},{9,1... | collective-permute-start | bytes 1572872 | tf_op jit(solution)/shard_map/ppermute | solution.py:382
  42.5 2.5 %shard_map.87 = (f32[2,128,768]{2,1,0:T(8,128)S(1)}, f32[2,128,768]{2,1,0:T(8,128)S(1)}) custom-call(bf16[128,2048]{1,0:T(8,128)(2,1)S(1)} %collective-permute-done.1.saved_ref, f32[1,2048]{1,0:T(1,128)S(1)} %copy-done.8, bf16[2048,768]{1,0:T(8,128)(2,1)S(1)} %bitcast.15, bf16[2048,768]{1,0:T(8,128)(2,1)S(1)} %bitcast.21, ...), custom_call_target="tpu_custom_call" | custom-call | flops 3221225472 | bytes 12582912 | tf_op jit(solution)/shard_map/pallas_call | solution.py:187
  45.0 0.0 collective-permute-done.5.saved_ref
  45.0 2.5 %shard_map.88 = (f32[2,128,768]{2,1,0:T(8,128)S(1)}, f32[2,128,768]{2,1,0:T(8,128)S(1)}) custom-call(bf16[128,2048]{1,0:T(8,128)(2,1)S(1)} %collective-permute-done.5.saved_ref, f32[1,2048]{1,0:T(1,128)S(1)} %copy-done.8, bf16[2048,768]{1,0:T(8,128)(2,1)S(1)} %bitcast.16, bf16[2048,768]{1,0:T(8,128)(2,1)S(1)} %bitcast.22, ...), custom_call_target="tpu_custom_call" | custom-call | flops 3221225472 | bytes 12582912 | tf_op jit(solution)/shard_map/pallas_call | solution.py:187
  47.6 19.8 %collective-permute-done.2.saved_ref = bf16[128,2048]{1,0:T(8,128)(2,1)S(1)} collective-permute-done((bf16[128,2048]{1,0:T(8,128)(2,1)S(1)}, bf16[128,2048]{1,0:T(8,128)(2,1)S(1)}, u32[]{:S(2)}, u32[]{:S(2)}) %collective-permute-start.2) | collective-permute-done | bytes 524320 | tf_op jit(solution)/shard_map/ppermute | solution.py:374
  67.4 2.5 %shard_map.89 = (f32[2,128,768]{2,1,0:T(8,128)S(1)}, f32[2,128,768]{2,1,0:T(8,128)S(1)}) custom-call(bf16[128,2048]{1,0:T(8,128)(2,1)S(1)} %collective-permute-done.2.saved_ref, f32[1,2048]{1,0:T(1,128)S(1)} %copy-done.8, bf16[2048,768]{1,0:T(8,128)(2,1)S(1)} %bitcast.17, bf16[2048,768]{1,0:T(8,128)(2,1)S(1)} %bitcast.23, ...), custom_call_target="tpu_custom_call" | custom-call | flops 3221225472 | bytes 12582912 | tf_op jit(solution)/shard_map/pallas_call | solution.py:187
  69.9 0.1 collective-permute-start.13
  70.0 2.3 %collective-permute-start.7 = (bf16[128,2048]{1,0:T(8,128)(2,1)S(1)}, bf16[128,2048]{1,0:T(8,128)(2,1)S(1)}, u32[]{:S(2)}, u32[]{:S(2)}) collective-permute-start(bf16[128,2048]{1,0:T(8,128)(2,1)S(1)} %bitcast.30), channel_id=1, source_target_pairs={{0,24},{1,25},{2,26},{3,27},{4,28},{5,29},{6,30},{7,31},{8,0},{9,1... | collective-permute-start | bytes 1572872 | tf_op jit(solution)/shard_map/ppermute | solution.py:382
  72.3 4.9 %shard_map.90.refs_6_ = bf16[128,2048]{1,0:T(8,128)(2,1)S(1)} custom-call(bf16[128,2176]{1,0:T(8,128)(2,1)S(1)} %collective-permute-done.rows_ref, f32[1,2048]{1,0:T(1,128)S(1)} %copy-done.8, f32[2,128,768]{2,1,0:T(8,128)S(1)} %get-tuple-element.37.refs_4_.gate_ref, f32[2,128,768]{2,1,0:T(8,128)S(1)} %get-tuple-element.42.up_ref, ...), custom_call_target="tpu_custom_call" | custom-call | flops 4831838208 | bytes 18874368 | tf_op jit(solution)/shard_map/pallas_call | solution.py:307
  77.2 2.0 %collective-permute-start.10 = (bf16[128,2048]{1,0:T(8,128)(2,1)S(1)}, bf16[128,2048]{1,0:T(8,128)(2,1)S(1)}, u32[]{:S(2)}, u32[]{:S(2)}) collective-permute-start(bf16[128,2048]{1,0:T(8,128)(2,1)S(1)} %shard_map.90.refs_6_), channel_id=1, source_target_pairs={{0,2},{1,3},{2,30},{3,31},{4,24},{5,25},{6,4},{7,5},{8,10},{9,11},... | collective-permute-start | bytes 1572872 | tf_op jit(solution)/shard_map/ppermute | solution.py:397
  79.3 4.9 %shard_map.91.refs_6_ = bf16[128,2048]{1,0:T(8,128)(2,1)S(1)} custom-call(bf16[128,2176]{1,0:T(8,128)(2,1)S(1)} %collective-permute-done.11.rows_ref, f32[1,2048]{1,0:T(1,128)S(1)} %copy-done.8, f32[2,128,768]{2,1,0:T(8,128)S(1)} %get-tuple-element.38.refs_4_.gate_ref, f32[2,128,768]{2,1,0:T(8,128)S(1)} %get-tuple-element.51.up_ref, ...), custom_call_target="tpu_custom_call" | custom-call | flops 4831838208 | bytes 18874368 | tf_op jit(solution)/shard_map/pallas_call | solution.py:307
  84.2 2.5 %collective-permute-start.12 = (bf16[128,2048]{1,0:T(8,128)(2,1)S(1)}, bf16[128,2048]{1,0:T(8,128)(2,1)S(1)}, u32[]{:S(2)}, u32[]{:S(2)}) collective-permute-start(bf16[128,2048]{1,0:T(8,128)(2,1)S(1)} %shard_map.91.refs_6_), channel_id=1, source_target_pairs={{0,26},{1,27},{2,24},{3,25},{4,30},{5,31},{6,28},{7,29},{8,2},{9,3... | collective-permute-start | bytes 1572872 | tf_op jit(solution)/shard_map/ppermute | solution.py:382
  86.7 0.5 collective-permute-start.9
  87.2 20.1 %collective-permute-done.7.refs_7_.saved_ref = bf16[128,2048]{1,0:T(8,128)(2,1)S(1)} collective-permute-done((bf16[128,2048]{1,0:T(8,128)(2,1)S(1)}, bf16[128,2048]{1,0:T(8,128)(2,1)S(1)}, u32[]{:S(2)}, u32[]{:S(2)}) %collective-permute-start.7) | collective-permute-done | bytes 524320 | tf_op jit(solution)/shard_map/ppermute | solution.py:382
  107.3 4.9 %shard_map.93.refs_0_ = bf16[128,2048]{1,0:T(8,128)(2,1)S(1)} custom-call(bf16[128,2176]{1,0:T(8,128)(2,1)S(1)} %collective-permute-done.13.rows_ref, f32[1,2048]{1,0:T(1,128)S(1)} %copy-done.8, f32[2,128,768]{2,1,0:T(8,128)S(1)} %get-tuple-element.53.gate_ref, f32[2,128,768]{2,1,0:T(8,128)S(1)} %get-tuple-element.54.up_ref, ...), custom_call_target="tpu_custom_call" | custom-call | flops 4831838208 | bytes 18874368 | tf_op jit(solution)/shard_map/pallas_call | solution.py:307
  112.3 0.2 shard_map.94
  112.4 11.3 %collective-permute-start.14 = (bf16[128,2048]{1,0:T(8,128)(2,1)S(1)}, bf16[128,2048]{1,0:T(8,128)(2,1)S(1)}, u32[]{:S(2)}, u32[]{:S(2)}) collective-permute-start(bf16[128,2048]{1,0:T(8,128)(2,1)S(1)} %shard_map.94), channel_id=1, source_target_pairs={{0,30},{1,31},{2,28},{3,29},{4,26},{5,27},{6,24},{7,25},{8,6},{9,7... | collective-permute-start | bytes 1572872 | tf_op jit(solution)/shard_map/ppermute | solution.py:382
  123.7 0.2 shard_map.92.refs_0_
  123.9 4.1 %collective-permute-done.9.upstream_ref = bf16[128,2048]{1,0:T(8,128)(2,1)S(1)} collective-permute-done((bf16[128,2048]{1,0:T(8,128)(2,1)S(1)}, bf16[128,2048]{1,0:T(8,128)(2,1)S(1)}, u32[]{:S(2)}, u32[]{:S(2)}) %collective-permute-start.9) | collective-permute-done | bytes 524320 | tf_op jit(solution)/shard_map/ppermute | solution.py:382
  128.0 2.4 %collective-permute-done.14.refs_1_ = bf16[128,2048]{1,0:T(8,128)(2,1)S(1)} collective-permute-done((bf16[128,2048]{1,0:T(8,128)(2,1)S(1)}, bf16[128,2048]{1,0:T(8,128)(2,1)S(1)}, u32[]{:S(2)}, u32[]{:S(2)}) %collective-permute-start.14) | collective-permute-done | bytes 524320 | tf_op jit(solution)/shard_map/ppermute | solution.py:382
  130.4 1.5 %shard_map.95 = bf16[128,2048]{1,0:T(8,128)(2,1)} custom-call(bf16[128,2048]{1,0:T(8,128)(2,1)S(1)} %collective-permute-done.7.refs_7_.saved_ref, bf16[128,2048]{1,0:T(8,128)(2,1)S(1)} %collective-permute-done.9.upstream_ref, f32[128,2048]{1,0:T(8,128)S(1)} %shard_map.92.refs_0_, bf16[128,2048]{1,0:T(8,128)(2,1)S(1)} %collective-permute-done.14.refs_1_), custom_call_target="tpu_custom_call" | custom-call | tf_op jit(solution)/shard_map/pallas_call | solution.py:336
  (22 shorter events, 0.0 us)
Async XLA Ops:
  0.0 28.7 %collective-permute-start.3 = (bf16[2048,768]{1,0:T(8,128)(2,1)}, bf16[2048,768]{1,0:T(8,128)(2,1)S(1)}, u32[]{:S(2)}, u32[]{:S(2)}) collective-permute-start(bf16[2048,768]{1,0:T(8,128)(2,1)} %bitcast.12), channel_id=1, source_target_pairs={{0,1},{1,0},{2,3},{3,2},{4,5},{5,4},{6,7},{7,6},{8,9},{9,8},{10,11... | collective-permute-start | bytes 9437192 | tf_op jit(solution)/shard_map/ppermute | solution.py:374
  0.5 32.2 %collective-permute-start.4 = (bf16[2048,768]{1,0:T(8,128)(2,1)}, bf16[2048,768]{1,0:T(8,128)(2,1)S(1)}, u32[]{:S(2)}, u32[]{:S(2)}) collective-permute-start(bf16[2048,768]{1,0:T(8,128)(2,1)} %bitcast.18), channel_id=1, source_target_pairs={{0,1},{1,0},{2,3},{3,2},{4,5},{5,4},{6,7},{7,6},{8,9},{9,8},{10,11... | collective-permute-start | bytes 9437192 | tf_op jit(solution)/shard_map/ppermute | solution.py:374
  0.5 33.9 %collective-permute-start.6 = (bf16[768,2048]{1,0:T(8,128)(2,1)}, bf16[768,2048]{1,0:T(8,128)(2,1)S(1)}, u32[]{:S(2)}, u32[]{:S(2)}) collective-permute-start(bf16[768,2048]{1,0:T(8,128)(2,1)} %bitcast.24), channel_id=1, source_target_pairs={{0,1},{1,0},{2,3},{3,2},{4,5},{5,4},{6,7},{7,6},{8,9},{9,8},{10,11... | collective-permute-start | bytes 9437192 | tf_op jit(solution)/shard_map/ppermute | solution.py:374
  1.0 27.7 %collective-permute-start.1 = (bf16[128,2048]{1,0:T(8,128)(2,1)}, bf16[128,2048]{1,0:T(8,128)(2,1)S(1)}, u32[]{:S(2)}, u32[]{:S(2)}) collective-permute-start(bf16[128,2048]{1,0:T(8,128)(2,1)} %bitcast.26), channel_id=1, source_target_pairs={{0,4},{1,5},{2,6},{3,7},{4,0},{5,1},{6,2},{7,3},{8,12},{9,13},{10,... | collective-permute-start | bytes 1572872 | tf_op jit(solution)/shard_map/ppermute | solution.py:374
  4.6 40.5 %collective-permute-start.5 = (bf16[128,2048]{1,0:T(8,128)(2,1)}, bf16[128,2048]{1,0:T(8,128)(2,1)S(1)}, u32[]{:S(2)}, u32[]{:S(2)}) collective-permute-start(bf16[128,2048]{1,0:T(8,128)(2,1)} %bitcast.27), channel_id=1, source_target_pairs={{0,2},{1,3},{2,0},{3,1},{4,6},{5,7},{6,4},{7,5},{8,10},{9,11},{10,... | collective-permute-start | bytes 1572872 | tf_op jit(solution)/shard_map/ppermute | solution.py:374
  6.1 1.0 copy-start.9
  7.2 0.7 copy-start.11
  7.9 0.7 copy-start.12
  8.9 1.9 %copy-start = (bf16[1,1,2048,768]{3,2,1,0:T(8,128)(2,1)S(1)}, bf16[1,1,2048,768]{3,2,1,0:T(8,128)(2,1)}, u32[]{:S(2)}) copy-start(bf16[1,1,2048,768]{3,2,1,0:T(8,128)(2,1)} %param.11) | copy-start | bytes 9437188
  10.8 1.9 %copy-start.2 = (bf16[1,1,2048,768]{3,2,1,0:T(8,128)(2,1)S(1)}, bf16[1,1,2048,768]{3,2,1,0:T(8,128)(2,1)}, u32[]{:S(2)}) copy-start(bf16[1,1,2048,768]{3,2,1,0:T(8,128)(2,1)} %param.12) | copy-start | bytes 9437188
  12.7 1.0 copy-start.5
  13.7 0.7 copy-start.7
  14.4 1.9 %copy-start.1 = (bf16[1,1,2048,768]{3,2,1,0:T(8,128)(2,1)S(1)}, bf16[1,1,2048,768]{3,2,1,0:T(8,128)(2,1)}, u32[]{:S(2)}) copy-start(bf16[1,1,2048,768]{3,2,1,0:T(8,128)(2,1)} %param.11) | copy-start | bytes 9437188
  14.4 2.8 %copy-start.3 = (bf16[1,1,2048,768]{3,2,1,0:T(8,128)(2,1)S(1)}, bf16[1,1,2048,768]{3,2,1,0:T(8,128)(2,1)}, u32[]{:S(2)}) copy-start(bf16[1,1,2048,768]{3,2,1,0:T(8,128)(2,1)} %param.12) | copy-start | bytes 9437188
  14.4 2.8 %copy-start.8 = (f32[1,2048]{1,0:T(1,128)S(1)}, f32[1,2048]{1,0:T(1,128)}, u32[]{:S(2)}) copy-start(f32[1,2048]{1,0:T(1,128)} %gain_ref.19) | copy-start | bytes 24580
  17.2 1.9 %copy-start.4 = (bf16[1,1,768,2048]{3,2,1,0:T(8,128)(2,1)S(1)}, bf16[1,1,768,2048]{3,2,1,0:T(8,128)(2,1)}, u32[]{:S(2)}) copy-start(bf16[1,1,768,2048]{3,2,1,0:T(8,128)(2,1)} %param.13) | copy-start | bytes 9437188
  19.1 13.6 %copy-start.6 = (bf16[1,128,2048]{2,1,0:T(8,128)(2,1)S(1)}, bf16[1,128,2048]{2,1,0:T(8,128)(2,1)}, u32[]{:S(2)}) copy-start(bf16[1,128,2048]{2,1,0:T(8,128)(2,1)} %param.8) | copy-start | bytes 1572868
  28.7 41.2 %collective-permute-start = (bf16[128,2176]{1,0:T(8,128)(2,1)S(1)}, bf16[128,2176]{1,0:T(8,128)(2,1)S(1)}, u32[]{:S(2)}, u32[]{:S(2)}) collective-permute-start(bf16[128,2176]{1,0:T(8,128)(2,1)S(1)} %shard_map.82.rows_ref), channel_id=1, source_target_pairs={{0,4},{1,5},{2,6},{3,7},{4,0},{5,1},{6,2},{7,3},{8,12},{9,13},{10,... | collective-permute-start | bytes 1671176 | tf_op jit(solution)/shard_map/ppermute | solution.py:374
  28.7 50.6 %collective-permute-start.11 = (bf16[128,2176]{1,0:T(8,128)(2,1)S(1)}, bf16[128,2176]{1,0:T(8,128)(2,1)S(1)}, u32[]{:S(2)}, u32[]{:S(2)}) collective-permute-start(bf16[128,2176]{1,0:T(8,128)(2,1)S(1)} %shard_map.82.rows_ref), channel_id=1, source_target_pairs={{0,2},{1,3},{2,0},{3,1},{4,6},{5,7},{6,4},{7,5},{8,10},{9,11},{10,... | collective-permute-start | bytes 1671176 | tf_op jit(solution)/shard_map/ppermute | solution.py:374
  32.7 34.7 %collective-permute-start.2 = (bf16[128,2048]{1,0:T(8,128)(2,1)S(1)}, bf16[128,2048]{1,0:T(8,128)(2,1)S(1)}, u32[]{:S(2)}, u32[]{:S(2)}) collective-permute-start(bf16[128,2048]{1,0:T(8,128)(2,1)S(1)} %collective-permute-done.1.saved_ref), channel_id=1, source_target_pairs={{0,2},{1,3},{2,0},{3,1},{4,6},{5,7},{6,4},{7,5},{8,10},{9,11},{10,... | collective-permute-start | bytes 1572872 | tf_op jit(solution)/shard_map/ppermute | solution.py:374
  40.0 32.3 %collective-permute-start.8 = (bf16[128,2048]{1,0:T(8,128)(2,1)S(1)}, bf16[128,2048]{1,0:T(8,128)(2,1)S(1)}, u32[]{:S(2)}, u32[]{:S(2)}) collective-permute-start(bf16[128,2048]{1,0:T(8,128)(2,1)S(1)} %get-tuple-element.36.refs_4_), channel_id=1, source_target_pairs={{0,24},{1,25},{2,26},{3,27},{4,28},{5,29},{6,30},{7,31},{8,0},{9,1... | collective-permute-start | bytes 1572872 | tf_op jit(solution)/shard_map/ppermute | solution.py:382
  69.9 37.5 %collective-permute-start.13 = (bf16[128,2176]{1,0:T(8,128)(2,1)S(1)}, bf16[128,2176]{1,0:T(8,128)(2,1)S(1)}, u32[]{:S(2)}, u32[]{:S(2)}) collective-permute-start(bf16[128,2176]{1,0:T(8,128)(2,1)S(1)} %collective-permute-done.rows_ref), channel_id=1, source_target_pairs={{0,2},{1,3},{2,0},{3,1},{4,6},{5,7},{6,4},{7,5},{8,10},{9,11},{10,... | collective-permute-start | bytes 1671176 | tf_op jit(solution)/shard_map/ppermute | solution.py:374
  70.0 37.4 %collective-permute-start.7 = (bf16[128,2048]{1,0:T(8,128)(2,1)S(1)}, bf16[128,2048]{1,0:T(8,128)(2,1)S(1)}, u32[]{:S(2)}, u32[]{:S(2)}) collective-permute-start(bf16[128,2048]{1,0:T(8,128)(2,1)S(1)} %bitcast.30), channel_id=1, source_target_pairs={{0,24},{1,25},{2,26},{3,27},{4,28},{5,29},{6,30},{7,31},{8,0},{9,1... | collective-permute-start | bytes 1572872 | tf_op jit(solution)/shard_map/ppermute | solution.py:382
  77.2 35.0 %collective-permute-start.10 = (bf16[128,2048]{1,0:T(8,128)(2,1)S(1)}, bf16[128,2048]{1,0:T(8,128)(2,1)S(1)}, u32[]{:S(2)}, u32[]{:S(2)}) collective-permute-start(bf16[128,2048]{1,0:T(8,128)(2,1)S(1)} %shard_map.90.refs_6_), channel_id=1, source_target_pairs={{0,2},{1,3},{2,30},{3,31},{4,24},{5,25},{6,4},{7,5},{8,10},{9,11},... | collective-permute-start | bytes 1572872 | tf_op jit(solution)/shard_map/ppermute | solution.py:397
  79.3 7.5 %copy-start.10 = (bf16[1,128,2048]{2,1,0:T(8,128)(2,1)S(1)}, bf16[1,128,2048]{2,1,0:T(8,128)(2,1)}, u32[]{:S(2)}) copy-start(bf16[1,128,2048]{2,1,0:T(8,128)(2,1)} %param.9) | copy-start | bytes 1572868
  84.2 39.5 %collective-permute-start.12 = (bf16[128,2048]{1,0:T(8,128)(2,1)S(1)}, bf16[128,2048]{1,0:T(8,128)(2,1)S(1)}, u32[]{:S(2)}, u32[]{:S(2)}) collective-permute-start(bf16[128,2048]{1,0:T(8,128)(2,1)S(1)} %shard_map.91.refs_6_), channel_id=1, source_target_pairs={{0,26},{1,27},{2,24},{3,25},{4,30},{5,31},{6,28},{7,29},{8,2},{9,3... | collective-permute-start | bytes 1572872 | tf_op jit(solution)/shard_map/ppermute | solution.py:382
  86.7 41.3 %collective-permute-start.9 = (bf16[128,2048]{1,0:T(8,128)(2,1)S(1)}, bf16[128,2048]{1,0:T(8,128)(2,1)S(1)}, u32[]{:S(2)}, u32[]{:S(2)}) collective-permute-start(bf16[128,2048]{1,0:T(8,128)(2,1)S(1)} %bitcast.32), channel_id=1, source_target_pairs={{0,24},{1,25},{2,26},{3,27},{4,28},{5,29},{6,30},{7,31},{8,0},{9,1... | collective-permute-start | bytes 1572872 | tf_op jit(solution)/shard_map/ppermute | solution.py:382
  112.4 18.0 %collective-permute-start.14 = (bf16[128,2048]{1,0:T(8,128)(2,1)S(1)}, bf16[128,2048]{1,0:T(8,128)(2,1)S(1)}, u32[]{:S(2)}, u32[]{:S(2)}) collective-permute-start(bf16[128,2048]{1,0:T(8,128)(2,1)S(1)} %shard_map.94), channel_id=1, source_target_pairs={{0,30},{1,31},{2,28},{3,29},{4,26},{5,27},{6,24},{7,25},{8,6},{9,7... | collective-permute-start | bytes 1572872 | tf_op jit(solution)/shard_map/ppermute | solution.py:382

commit v6 on v5

--- a/solution.py
+++ b/solution.py
@@ -402,6 +402,11 @@
     other = (gate_other, up_other, hop(1)(own[2]))
     u_one = hop(2)(later)
     other_factors = slot_factors(saved_rows, gain, (other,), [gate])
+    saved_later, upstream_later, gate = lax.optimization_barrier(
+        (saved_rows, upstream_rows, other_factors[0])
+    )
+    other_factors = (gate, other_factors[1])
+    next_saved, next_upstream = handed(0)(saved_later), handed(0)(upstream_later)
     both = (own, other)
     here, *own_turned = turning_pieces(
         0, shared, gain, own_factors, own, experts, jnp.float32, None
@@ -413,21 +418,16 @@
     x_three = hop(2)(x_two)
     two_factors = slot_factors(x_two, gain, both, [here])
     one_factors = slot_factors(x_one, gain, both, [two_factors[0]])
-    three_factors = slot_factors(x_three, gain, both, [one_factors[0]])
-    u_two, saved_later, three_gate = lax.optimization_barrier(
-        (u_two, saved_rows, three_factors[0])
-    )
-    three_factors = (three_gate, three_factors[1])
-    next_saved = handed(0)(saved_later)
+    u_two, one_gate = lax.optimization_barrier((u_two, one_factors[0]))
+    one_factors = (one_gate, one_factors[1])
     here_next = handed(0)(here)
     u_three = hop(2)(u_two)
-    two = slot_pieces(u_two, gain, two_factors, turned, experts, [here_next])
+    two = slot_pieces(u_two, gain, two_factors, turned, experts, [next_saved, next_upstream])
     two_next = second_hop(two)
-    upstream_later, two = lax.optimization_barrier((upstream_rows, two))
-    next_upstream = handed(0)(upstream_later)
-    one = slot_pieces(u_one, gain, one_factors, turned, experts, [two])
+    three_factors = slot_factors(x_three, gain, both, [two])
+    one = slot_pieces(u_one, gain, one_factors, turned, experts, [three_factors[0]])
     one_next = handed(2)(one)
-    three = slot_pieces(u_three, gain, three_factors, turned, experts, [one, next_saved])
+    three = slot_pieces(u_three, gain, three_factors, turned, experts, [one])
     three = joined(experts, 0, two_next, [three], jnp.bfloat16)
     summed = joined(experts, 1, two_next, [here_next, one_next], jnp.float32)
     three_next = handed(6)(three)

time: 132 us -> 121 us (0.917)
  the two profiles are of different devices: /device:TPU:0 before, /device:TPU:8 now
where the time goes in v6:
time: 121 us; the launch traced here: 120 us
  Pallas kernels  38.8 us (32%)
  waiting for transfers between devices  36.8 us (30%)
  starting transfers between devices  32.9 us (27%)
  local copies, waits for them, and re-layouts  11 us (9%)
    ppermute x5, waiting for transfers between devices, handed(): return lambda value: lax.ppermute(value, ('section', 'expert'), pairs)  24.8 us
    ppermute x5, starting transfers between devices, handed(): return lambda value: lax.ppermute(value, ('section', 'expert'), pairs)  23.4 us
    pallas_call x3, Pallas kernels, slot_pieces(): pl.pallas_call(functools.partial(pieces_kernel, experts, pairs), in_specs...  14.7 us
    ppermute x9, waiting for transfers between devices, hop(): lax.ppermute(value, 'expert', [(i, i ^ by) for i in range(experts)])  12.1 us
    pallas_call x2, Pallas kernels, turning_pieces(): pl.pallas_call(functools.partial(turning_kernel, experts, len(start), fli...  11.1 us
    unnamed x26, local copies, waits for them, and re-layouts  11 us
    pallas_call x5, Pallas kernels, slot_factors(): pl.pallas_call(functools.partial(factors_kernel, pairs), in_specs=[in_vme...  10.8 us
    ppermute x9, starting transfers between devices, hop(): lax.ppermute(value, 'expert', [(i, i ^ by) for i in range(experts)])  7.43 us
  transfers between devices with their start and end apart: 15, of which 4 were waited for; matrix products, arithmetic and copies ran while one was open for 0% of the time, Pallas kernels for 31%

profile of v6, /device:TPU:8, one launch (start us, length us, event | category | flops | bytes accessed | tf_op | source)
XLA Modules:
  0.0 119.7 jit_solution(9100723857995159048)
XLA Ops:
  0.0 0.5 collective-permute-start.1
  0.5 0.0 collective-permute-start.7
  0.5 2.6 %collective-permute-start.6 = (bf16[128,2048]{1,0:T(8,128)(2,1)}, bf16[128,2048]{1,0:T(8,128)(2,1)S(1)}, u32[]{:S(2)}, u32[]{:S(2)}) collective-permute-start(bf16[128,2048]{1,0:T(8,128)(2,1)} %bitcast.26), channel_id=1, source_target_pairs={{0,4},{1,5},{2,6},{3,7},{4,0},{5,1},{6,2},{7,3},{8,12},{9,13},{10,... | collective-permute-start | bytes 1572872 | tf_op jit(solution)/shard_map/ppermute | solution.py:374
  3.1 0.4 collective-permute-start.5
  3.6 1.0 copy-done.9
  4.6 0.7 copy-done.11
  5.3 0.7 copy-done.12
  6.0 0.3 shard_map.82.rows_ref
  6.3 0.0 copy-start
  6.3 1.9 %copy-done = bf16[1,1,2048,768]{3,2,1,0:T(8,128)(2,1)S(1)} copy-done((bf16[1,1,2048,768]{3,2,1,0:T(8,128)(2,1)S(1)}, bf16[1,1,2048,768]{3,2,1,0:T(8,128)(2,1)}, u32[]{:S(2)}) %copy-start) | copy-done | bytes 3145752
  8.2 1.9 %copy-done.2 = bf16[1,1,2048,768]{3,2,1,0:T(8,128)(2,1)S(1)} copy-done((bf16[1,1,2048,768]{3,2,1,0:T(8,128)(2,1)S(1)}, bf16[1,1,2048,768]{3,2,1,0:T(8,128)(2,1)}, u32[]{:S(2)}) %copy-start.2) | copy-done | bytes 3145752
  10.1 1.0 copy-done.5
  11.1 0.7 copy-done.7
  11.8 1.6 %shard_map.83 = (f32[1,128,768]{2,1,0:T(8,128)S(1)}, f32[1,128,768]{2,1,0:T(8,128)S(1)}) custom-call(bf16[128,2048]{1,0:T(8,128)(2,1)S(1)} %bitcast.28, f32[1,2048]{1,0:T(1,128)S(1)} %copy-done.7, bf16[2048,768]{1,0:T(8,128)(2,1)S(1)} %bitcast.13, bf16[2048,768]{1,0:T(8,128)(2,1)S(1)} %bitcast.19), custom_call_target="tpu_custom_call" | custom-call | flops 1610612736 | bytes 6291456 | tf_op jit(solution)/shard_map/pallas_call | solution.py:187
  13.5 0.2 copy-done.1
  13.7 1.0 copy-done.3
  14.7 1.9 %copy-done.4 = bf16[1,1,768,2048]{3,2,1,0:T(8,128)(2,1)S(1)} copy-done((bf16[1,1,768,2048]{3,2,1,0:T(8,128)(2,1)S(1)}, bf16[1,1,768,2048]{3,2,1,0:T(8,128)(2,1)}, u32[]{:S(2)}) %copy-start.4) | copy-done | bytes 3145752
  16.6 5.5 %shard_map.85 = (f32[128,2048]{1,0:T(8,128)S(1)}, bf16[768,2048]{1,0:T(8,128)(2,1)S(1)}, bf16[768,2048]{1,0:T(8,128)(2,1)S(1)}, bf16[2048,768]{1,0:T(8,128)(2,1)S(1)}) custom-call(bf16[128,2176]{1,0:T(8,128)(2,1)S(1)} %shard_map.82.rows_ref, f32[1,2048]{1,0:T(1,128)S(1)} %copy-done.8, f32[1,128,768]{2,1,0:T(8,128)S(1)} %get-tuple-element.31.refs_2_.gate_ref, ...), custom_call_target="tpu_custom_call" | custom-call | flops 2415919104 | bytes 9437184 | tf_op jit(solution)/shard_map/pallas_call | solution.py:253
  22.1 0.0 collective-permute-done.refs_0_.refs_2_
  22.1 0.1 collective-permute-start.4
  22.2 0.0 collective-permute-done.1.refs_1_.refs_3_
  22.2 1.9 %collective-permute-start.10 = (bf16[128,2176]{1,0:T(8,128)(2,1)S(1)}, bf16[128,2176]{1,0:T(8,128)(2,1)S(1)}, u32[]{:S(2)}, u32[]{:S(2)}) collective-permute-start(bf16[128,2176]{1,0:T(8,128)(2,1)S(1)} %shard_map.82.rows_ref), channel_id=1, source_target_pairs={{0,2},{1,3},{2,0},{3,1},{4,6},{5,7},{6,4},{7,5},{8,10},{9,11},{10,... | collective-permute-start | bytes 1671176 | tf_op jit(solution)/shard_map/ppermute | solution.py:374
  24.1 1.6 %shard_map.84 = (f32[1,128,768]{2,1,0:T(8,128)S(1)}, f32[1,128,768]{2,1,0:T(8,128)S(1)}) custom-call(bf16[128,2048]{1,0:T(8,128)(2,1)S(1)} %bitcast.29, f32[1,2048]{1,0:T(1,128)S(1)} %copy-done.8, bf16[2048,768]{1,0:T(8,128)(2,1)S(1)} %collective-permute-done.refs_0_.refs_2_, bf16[2048,768]{1,0:T(8,128)(2,1)S(1)} %collective-permute-done.1.refs_1_.refs_3_, ...), custom_call_target="tpu_custom_call" | custom-call | flops 1610612736 | bytes 6291456 | tf_op jit(solution)/shard_map/pallas_call | solution.py:187
  25.8 2.5 %collective-permute-start.2 = (bf16[128,2048]{1,0:T(8,128)(2,1)S(1)}, bf16[128,2048]{1,0:T(8,128)(2,1)S(1)}, u32[]{:S(2)}, u32[]{:S(2)}) collective-permute-start(bf16[128,2048]{1,0:T(8,128)(2,1)S(1)} %bitcast.30), channel_id=1, source_target_pairs={{0,24},{1,25},{2,26},{3,27},{4,28},{5,29},{6,30},{7,31},{8,0},{9,1... | collective-permute-start | bytes 1572872 | tf_op jit(solution)/shard_map/ppermute | solution.py:382
  28.3 5.6 %shard_map.86 = (bf16[128,2048]{1,0:T(8,128)(2,1)S(1)}, bf16[768,2048]{1,0:T(8,128)(2,1)S(1)}, bf16[768,2048]{1,0:T(8,128)(2,1)S(1)}, bf16[2048,768]{1,0:T(8,128)(2,1)S(1)}) custom-call(bf16[128,2176]{1,0:T(8,128)(2,1)S(1)} %shard_map.82.rows_ref, f32[1,2048]{1,0:T(1,128)S(1)} %copy-done.8, f32[1,128,768]{2,1,0:T(8,128)S(1)} %get-tuple-element.35.gate_ref, ...), custom_call_target="tpu_custom_call" | custom-call | flops 2415919104 | bytes 9437184 | tf_op jit(solution)/shard_map/pallas_call | solution.py:253
  33.9 0.6 collective-permute-start.3
  34.5 2.5 %shard_map.87 = (f32[2,128,768]{2,1,0:T(8,128)S(1)}, f32[2,128,768]{2,1,0:T(8,128)S(1)}) custom-call(bf16[128,2048]{1,0:T(8,128)(2,1)S(1)} %collective-permute-done.6.saved_ref, f32[1,2048]{1,0:T(1,128)S(1)} %copy-done.8, bf16[2048,768]{1,0:T(8,128)(2,1)S(1)} %bitcast.15, bf16[2048,768]{1,0:T(8,128)(2,1)S(1)} %bitcast.21, ...), custom_call_target="tpu_custom_call" | custom-call | flops 3221225472 | bytes 12582912 | tf_op jit(solution)/shard_map/pallas_call | solution.py:187
  37.0 0.0 collective-permute-done.5.saved_ref
  37.0 0.5 collective-permute-start.11
  37.5 2.5 %shard_map.88 = (f32[2,128,768]{2,1,0:T(8,128)S(1)}, f32[2,128,768]{2,1,0:T(8,128)S(1)}) custom-call(bf16[128,2048]{1,0:T(8,128)(2,1)S(1)} %collective-permute-done.5.saved_ref, f32[1,2048]{1,0:T(1,128)S(1)} %copy-done.8, bf16[2048,768]{1,0:T(8,128)(2,1)S(1)} %bitcast.16, bf16[2048,768]{1,0:T(8,128)(2,1)S(1)} %bitcast.22, ...), custom_call_target="tpu_custom_call" | custom-call | flops 3221225472 | bytes 12582912 | tf_op jit(solution)/shard_map/pallas_call | solution.py:187
  40.0 10.3 %collective-permute-done.4.rows_ref = bf16[128,2176]{1,0:T(8,128)(2,1)S(1)} collective-permute-done((bf16[128,2176]{1,0:T(8,128)(2,1)S(1)}, bf16[128,2176]{1,0:T(8,128)(2,1)S(1)}, u32[]{:S(2)}, u32[]{:S(2)}) %collective-permute-start.4) | collective-permute-done | bytes 557088 | tf_op jit(solution)/shard_map/ppermute | solution.py:374
  50.3 2.4 %collective-permute-start.9 = (bf16[128,2048]{1,0:T(8,128)(2,1)S(1)}, bf16[128,2048]{1,0:T(8,128)(2,1)S(1)}, u32[]{:S(2)}, u32[]{:S(2)}) collective-permute-start(bf16[128,2048]{1,0:T(8,128)(2,1)S(1)} %get-tuple-element.39.refs_4_), channel_id=1, source_target_pairs={{0,24},{1,25},{2,26},{3,27},{4,28},{5,29},{6,30},{7,31},{8,0},{9,1... | collective-permute-start | bytes 1572872 | tf_op jit(solution)/shard_map/ppermute | solution.py:382
  52.7 1.4 %collective-permute-start.13 = (bf16[128,2176]{1,0:T(8,128)(2,1)S(1)}, bf16[128,2176]{1,0:T(8,128)(2,1)S(1)}, u32[]{:S(2)}, u32[]{:S(2)}) collective-permute-start(bf16[128,2176]{1,0:T(8,128)(2,1)S(1)} %collective-permute-done.4.rows_ref), channel_id=1, source_target_pairs={{0,2},{1,3},{2,0},{3,1},{4,6},{5,7},{6,4},{7,5},{8,10},{9,11},{10,... | collective-permute-start | bytes 1671176 | tf_op jit(solution)/shard_map/ppermute | solution.py:374
  54.1 0.0 collective-permute-done.3.refs_7_.upstream_ref
  54.1 4.9 %shard_map.89.refs_4_ = bf16[128,2048]{1,0:T(8,128)(2,1)S(1)} custom-call(bf16[128,2176]{1,0:T(8,128)(2,1)S(1)} %collective-permute-done.4.rows_ref, f32[1,2048]{1,0:T(1,128)S(1)} %copy-done.8, f32[2,128,768]{2,1,0:T(8,128)S(1)} %get-tuple-element.40.refs_4_.gate_ref, f32[2,128,768]{2,1,0:T(8,128)S(1)} %get-tuple-element.43.up_ref, ...), custom_call_target="tpu_custom_call" | custom-call | flops 4831838208 | bytes 18874368 | tf_op jit(solution)/shard_map/pallas_call | solution.py:307
  59.0 2.1 %collective-permute-start.8 = (bf16[128,2048]{1,0:T(8,128)(2,1)S(1)}, bf16[128,2048]{1,0:T(8,128)(2,1)S(1)}, u32[]{:S(2)}, u32[]{:S(2)}) collective-permute-start(bf16[128,2048]{1,0:T(8,128)(2,1)S(1)} %shard_map.89.refs_4_), channel_id=1, source_target_pairs={{0,2},{1,3},{2,30},{3,31},{4,24},{5,25},{6,4},{7,5},{8,10},{9,11},... | collective-permute-start | bytes 1572872 | tf_op jit(solution)/shard_map/ppermute | solution.py:397
  61.1 1.8 %collective-permute-done.11.saved_ref = bf16[128,2048]{1,0:T(8,128)(2,1)S(1)} collective-permute-done((bf16[128,2048]{1,0:T(8,128)(2,1)S(1)}, bf16[128,2048]{1,0:T(8,128)(2,1)S(1)}, u32[]{:S(2)}, u32[]{:S(2)}) %collective-permute-start.11) | collective-permute-done | bytes 524320 | tf_op jit(solution)/shard_map/ppermute | solution.py:374
  62.9 2.5 %shard_map.90 = (f32[2,128,768]{2,1,0:T(8,128)S(1)}, f32[2,128,768]{2,1,0:T(8,128)S(1)}) custom-call(bf16[128,2048]{1,0:T(8,128)(2,1)S(1)} %collective-permute-done.11.saved_ref, f32[1,2048]{1,0:T(1,128)S(1)} %copy-done.8, bf16[2048,768]{1,0:T(8,128)(2,1)S(1)} %bitcast.17, bf16[2048,768]{1,0:T(8,128)(2,1)S(1)} %bitcast.23, ...), custom_call_target="tpu_custom_call" | custom-call | flops 3221225472 | bytes 12582912 | tf_op jit(solution)/shard_map/pallas_call | solution.py:187
  65.4 0.0 collective-permute-done.10.rows_ref
  65.4 4.9 %shard_map.91.refs_6_ = bf16[128,2048]{1,0:T(8,128)(2,1)S(1)} custom-call(bf16[128,2176]{1,0:T(8,128)(2,1)S(1)} %collective-permute-done.10.rows_ref, f32[1,2048]{1,0:T(1,128)S(1)} %copy-done.8, f32[2,128,768]{2,1,0:T(8,128)S(1)} %get-tuple-element.51.gate_ref, f32[2,128,768]{2,1,0:T(8,128)S(1)} %get-tuple-element.52.up_ref, ...), custom_call_target="tpu_custom_call" | custom-call | flops 4831838208 | bytes 18874368 | tf_op jit(solution)/shard_map/pallas_call | solution.py:307
  70.3 13.5 %collective-permute-start.12 = (bf16[128,2048]{1,0:T(8,128)(2,1)S(1)}, bf16[128,2048]{1,0:T(8,128)(2,1)S(1)}, u32[]{:S(2)}, u32[]{:S(2)}) collective-permute-start(bf16[128,2048]{1,0:T(8,128)(2,1)S(1)} %shard_map.91.refs_6_), channel_id=1, source_target_pairs={{0,26},{1,27},{2,24},{3,25},{4,30},{5,31},{6,28},{7,29},{8,2},{9,3... | collective-permute-start | bytes 1572872 | tf_op jit(solution)/shard_map/ppermute | solution.py:382
  83.8 4.9 %shard_map.93.refs_0_ = bf16[128,2048]{1,0:T(8,128)(2,1)S(1)} custom-call(bf16[128,2176]{1,0:T(8,128)(2,1)S(1)} %collective-permute-done.13.rows_ref, f32[1,2048]{1,0:T(1,128)S(1)} %copy-done.8, f32[2,128,768]{2,1,0:T(8,128)S(1)} %get-tuple-element.53.refs_6_.gate_ref, f32[2,128,768]{2,1,0:T(8,128)S(1)} %get-tuple-element.54.up_ref, ...), custom_call_target="tpu_custom_call" | custom-call | flops 4831838208 | bytes 18874368 | tf_op jit(solution)/shard_map/pallas_call | solution.py:307
  88.7 0.2 shard_map.94
  88.9 4.4 %collective-permute-start.14 = (bf16[128,2048]{1,0:T(8,128)(2,1)S(1)}, bf16[128,2048]{1,0:T(8,128)(2,1)S(1)}, u32[]{:S(2)}, u32[]{:S(2)}) collective-permute-start(bf16[128,2048]{1,0:T(8,128)(2,1)S(1)} %shard_map.94), channel_id=1, source_target_pairs={{0,30},{1,31},{2,28},{3,29},{4,26},{5,27},{6,24},{7,25},{8,6},{9,7... | collective-permute-start | bytes 1572872 | tf_op jit(solution)/shard_map/ppermute | solution.py:382
  93.3 9.0 %collective-permute-done.12.refs_1_ = bf16[128,2048]{1,0:T(8,128)(2,1)S(1)} collective-permute-done((bf16[128,2048]{1,0:T(8,128)(2,1)S(1)}, bf16[128,2048]{1,0:T(8,128)(2,1)S(1)}, u32[]{:S(2)}, u32[]{:S(2)}) %collective-permute-start.12) | collective-permute-done | bytes 524320 | tf_op jit(solution)/shard_map/ppermute | solution.py:382
  102.2 0.2 shard_map.92.refs_0_
  102.5 15.8 %collective-permute-done.14.refs_1_ = bf16[128,2048]{1,0:T(8,128)(2,1)S(1)} collective-permute-done((bf16[128,2048]{1,0:T(8,128)(2,1)S(1)}, bf16[128,2048]{1,0:T(8,128)(2,1)S(1)}, u32[]{:S(2)}, u32[]{:S(2)}) %collective-permute-start.14) | collective-permute-done | bytes 524320 | tf_op jit(solution)/shard_map/ppermute | solution.py:382
  118.2 1.5 %shard_map.95 = bf16[128,2048]{1,0:T(8,128)(2,1)} custom-call(bf16[128,2048]{1,0:T(8,128)(2,1)S(1)} %collective-permute-done.2.refs_6_.saved_ref, bf16[128,2048]{1,0:T(8,128)(2,1)S(1)} %collective-permute-done.3.refs_7_.upstream_ref, f32[128,2048]{1,0:T(8,128)S(1)} %shard_map.92.refs_0_, bf16[128,2048]{1,0:T(8,128)(2,1)S(1)} %collective-permute-done.14.refs_1_), custom_call_target="tpu_custom_call" | custom-call | tf_op jit(solution)/shard_map/pallas_call | solution.py:336
  (22 shorter events, 0.0 us)
Async XLA Ops:
  0.0 22.1 %collective-permute-start = (bf16[2048,768]{1,0:T(8,128)(2,1)}, bf16[2048,768]{1,0:T(8,128)(2,1)S(1)}, u32[]{:S(2)}, u32[]{:S(2)}) collective-permute-start(bf16[2048,768]{1,0:T(8,128)(2,1)} %bitcast.12), channel_id=1, source_target_pairs={{0,1},{1,0},{2,3},{3,2},{4,5},{5,4},{6,7},{7,6},{8,9},{9,8},{10,11... | collective-permute-start | bytes 9437192 | tf_op jit(solution)/shard_map/ppermute | solution.py:374
  0.0 22.2 %collective-permute-start.1 = (bf16[2048,768]{1,0:T(8,128)(2,1)}, bf16[2048,768]{1,0:T(8,128)(2,1)S(1)}, u32[]{:S(2)}, u32[]{:S(2)}) collective-permute-start(bf16[2048,768]{1,0:T(8,128)(2,1)} %bitcast.18), channel_id=1, source_target_pairs={{0,1},{1,0},{2,3},{3,2},{4,5},{5,4},{6,7},{7,6},{8,9},{9,8},{10,11... | collective-permute-start | bytes 9437192 | tf_op jit(solution)/shard_map/ppermute | solution.py:374
  0.5 25.3 %collective-permute-start.7 = (bf16[768,2048]{1,0:T(8,128)(2,1)}, bf16[768,2048]{1,0:T(8,128)(2,1)S(1)}, u32[]{:S(2)}, u32[]{:S(2)}) collective-permute-start(bf16[768,2048]{1,0:T(8,128)(2,1)} %bitcast.24), channel_id=1, source_target_pairs={{0,1},{1,0},{2,3},{3,2},{4,5},{5,4},{6,7},{7,6},{8,9},{9,8},{10,11... | collective-permute-start | bytes 9437192 | tf_op jit(solution)/shard_map/ppermute | solution.py:374
  0.5 33.3 %collective-permute-start.6 = (bf16[128,2048]{1,0:T(8,128)(2,1)}, bf16[128,2048]{1,0:T(8,128)(2,1)S(1)}, u32[]{:S(2)}, u32[]{:S(2)}) collective-permute-start(bf16[128,2048]{1,0:T(8,128)(2,1)} %bitcast.26), channel_id=1, source_target_pairs={{0,4},{1,5},{2,6},{3,7},{4,0},{5,1},{6,2},{7,3},{8,12},{9,13},{10,... | collective-permute-start | bytes 1572872 | tf_op jit(solution)/shard_map/ppermute | solution.py:374
  3.1 33.9 %collective-permute-start.5 = (bf16[128,2048]{1,0:T(8,128)(2,1)}, bf16[128,2048]{1,0:T(8,128)(2,1)S(1)}, u32[]{:S(2)}, u32[]{:S(2)}) collective-permute-start(bf16[128,2048]{1,0:T(8,128)(2,1)} %bitcast.27), channel_id=1, source_target_pairs={{0,2},{1,3},{2,0},{3,1},{4,6},{5,7},{6,4},{7,5},{8,10},{9,11},{10,... | collective-permute-start | bytes 1572872 | tf_op jit(solution)/shard_map/ppermute | solution.py:374
  3.6 1.0 copy-start.9
  4.6 0.7 copy-start.11
  5.3 0.7 copy-start.12
  6.3 1.9 %copy-start = (bf16[1,1,2048,768]{3,2,1,0:T(8,128)(2,1)S(1)}, bf16[1,1,2048,768]{3,2,1,0:T(8,128)(2,1)}, u32[]{:S(2)}) copy-start(bf16[1,1,2048,768]{3,2,1,0:T(8,128)(2,1)} %param.11) | copy-start | bytes 9437188
  8.2 1.9 %copy-start.2 = (bf16[1,1,2048,768]{3,2,1,0:T(8,128)(2,1)S(1)}, bf16[1,1,2048,768]{3,2,1,0:T(8,128)(2,1)}, u32[]{:S(2)}) copy-start(bf16[1,1,2048,768]{3,2,1,0:T(8,128)(2,1)} %param.12) | copy-start | bytes 9437188
  10.1 1.0 copy-start.5
  11.1 0.7 copy-start.7
  11.8 1.9 %copy-start.1 = (bf16[1,1,2048,768]{3,2,1,0:T(8,128)(2,1)S(1)}, bf16[1,1,2048,768]{3,2,1,0:T(8,128)(2,1)}, u32[]{:S(2)}) copy-start(bf16[1,1,2048,768]{3,2,1,0:T(8,128)(2,1)} %param.11) | copy-start | bytes 9437188
  11.8 2.8 %copy-start.3 = (bf16[1,1,2048,768]{3,2,1,0:T(8,128)(2,1)S(1)}, bf16[1,1,2048,768]{3,2,1,0:T(8,128)(2,1)}, u32[]{:S(2)}) copy-start(bf16[1,1,2048,768]{3,2,1,0:T(8,128)(2,1)} %param.12) | copy-start | bytes 9437188
  11.8 2.8 %copy-start.8 = (f32[1,2048]{1,0:T(1,128)S(1)}, f32[1,2048]{1,0:T(1,128)}, u32[]{:S(2)}) copy-start(f32[1,2048]{1,0:T(1,128)} %gain_ref.19) | copy-start | bytes 24580
  14.7 1.9 %copy-start.4 = (bf16[1,1,768,2048]{3,2,1,0:T(8,128)(2,1)S(1)}, bf16[1,1,768,2048]{3,2,1,0:T(8,128)(2,1)}, u32[]{:S(2)}) copy-start(bf16[1,1,768,2048]{3,2,1,0:T(8,128)(2,1)} %param.13) | copy-start | bytes 9437188
  16.6 7.6 %copy-start.6 = (bf16[1,128,2048]{2,1,0:T(8,128)(2,1)S(1)}, bf16[1,128,2048]{2,1,0:T(8,128)(2,1)}, u32[]{:S(2)}) copy-start(bf16[1,128,2048]{2,1,0:T(8,128)(2,1)} %param.8) | copy-start | bytes 1572868
  22.1 28.1 %collective-permute-start.4 = (bf16[128,2176]{1,0:T(8,128)(2,1)S(1)}, bf16[128,2176]{1,0:T(8,128)(2,1)S(1)}, u32[]{:S(2)}, u32[]{:S(2)}) collective-permute-start(bf16[128,2176]{1,0:T(8,128)(2,1)S(1)} %shard_map.82.rows_ref), channel_id=1, source_target_pairs={{0,4},{1,5},{2,6},{3,7},{4,0},{5,1},{6,2},{7,3},{8,12},{9,13},{10,... | collective-permute-start | bytes 1671176 | tf_op jit(solution)/shard_map/ppermute | solution.py:374
  22.2 43.2 %collective-permute-start.10 = (bf16[128,2176]{1,0:T(8,128)(2,1)S(1)}, bf16[128,2176]{1,0:T(8,128)(2,1)S(1)}, u32[]{:S(2)}, u32[]{:S(2)}) collective-permute-start(bf16[128,2176]{1,0:T(8,128)(2,1)S(1)} %shard_map.82.rows_ref), channel_id=1, source_target_pairs={{0,2},{1,3},{2,0},{3,1},{4,6},{5,7},{6,4},{7,5},{8,10},{9,11},{10,... | collective-permute-start | bytes 1671176 | tf_op jit(solution)/shard_map/ppermute | solution.py:374
  25.8 27.0 %collective-permute-start.2 = (bf16[128,2048]{1,0:T(8,128)(2,1)S(1)}, bf16[128,2048]{1,0:T(8,128)(2,1)S(1)}, u32[]{:S(2)}, u32[]{:S(2)}) collective-permute-start(bf16[128,2048]{1,0:T(8,128)(2,1)S(1)} %bitcast.30), channel_id=1, source_target_pairs={{0,24},{1,25},{2,26},{3,27},{4,28},{5,29},{6,30},{7,31},{8,0},{9,1... | collective-permute-start | bytes 1572872 | tf_op jit(solution)/shard_map/ppermute | solution.py:382
  28.3 5.6 %copy-start.10 = (bf16[1,128,2048]{2,1,0:T(8,128)(2,1)S(1)}, bf16[1,128,2048]{2,1,0:T(8,128)(2,1)}, u32[]{:S(2)}) copy-start(bf16[1,128,2048]{2,1,0:T(8,128)(2,1)} %param.9) | copy-start | bytes 1572868
  33.9 20.3 %collective-permute-start.3 = (bf16[128,2048]{1,0:T(8,128)(2,1)S(1)}, bf16[128,2048]{1,0:T(8,128)(2,1)S(1)}, u32[]{:S(2)}, u32[]{:S(2)}) collective-permute-start(bf16[128,2048]{1,0:T(8,128)(2,1)S(1)} %bitcast.32), channel_id=1, source_target_pairs={{0,24},{1,25},{2,26},{3,27},{4,28},{5,29},{6,30},{7,31},{8,0},{9,1... | collective-permute-start | bytes 1572872 | tf_op jit(solution)/shard_map/ppermute | solution.py:382
  37.0 25.9 %collective-permute-start.11 = (bf16[128,2048]{1,0:T(8,128)(2,1)S(1)}, bf16[128,2048]{1,0:T(8,128)(2,1)S(1)}, u32[]{:S(2)}, u32[]{:S(2)}) collective-permute-start(bf16[128,2048]{1,0:T(8,128)(2,1)S(1)} %collective-permute-done.6.saved_ref), channel_id=1, source_target_pairs={{0,2},{1,3},{2,0},{3,1},{4,6},{5,7},{6,4},{7,5},{8,10},{9,11},{10,... | collective-permute-start | bytes 1572872 | tf_op jit(solution)/shard_map/ppermute | solution.py:374
  50.3 43.0 %collective-permute-start.9 = (bf16[128,2048]{1,0:T(8,128)(2,1)S(1)}, bf16[128,2048]{1,0:T(8,128)(2,1)S(1)}, u32[]{:S(2)}, u32[]{:S(2)}) collective-permute-start(bf16[128,2048]{1,0:T(8,128)(2,1)S(1)} %get-tuple-element.39.refs_4_), channel_id=1, source_target_pairs={{0,24},{1,25},{2,26},{3,27},{4,28},{5,29},{6,30},{7,31},{8,0},{9,1... | collective-permute-start | bytes 1572872 | tf_op jit(solution)/shard_map/ppermute | solution.py:382
  52.7 31.1 %collective-permute-start.13 = (bf16[128,2176]{1,0:T(8,128)(2,1)S(1)}, bf16[128,2176]{1,0:T(8,128)(2,1)S(1)}, u32[]{:S(2)}, u32[]{:S(2)}) collective-permute-start(bf16[128,2176]{1,0:T(8,128)(2,1)S(1)} %collective-permute-done.4.rows_ref), channel_id=1, source_target_pairs={{0,2},{1,3},{2,0},{3,1},{4,6},{5,7},{6,4},{7,5},{8,10},{9,11},{10,... | collective-permute-start | bytes 1671176 | tf_op jit(solution)/shard_map/ppermute | solution.py:374
  59.0 29.7 %collective-permute-start.8 = (bf16[128,2048]{1,0:T(8,128)(2,1)S(1)}, bf16[128,2048]{1,0:T(8,128)(2,1)S(1)}, u32[]{:S(2)}, u32[]{:S(2)}) collective-permute-start(bf16[128,2048]{1,0:T(8,128)(2,1)S(1)} %shard_map.89.refs_4_), channel_id=1, source_target_pairs={{0,2},{1,3},{2,30},{3,31},{4,24},{5,25},{6,4},{7,5},{8,10},{9,11},... | collective-permute-start | bytes 1572872 | tf_op jit(solution)/shard_map/ppermute | solution.py:397
  70.3 31.9 %collective-permute-start.12 = (bf16[128,2048]{1,0:T(8,128)(2,1)S(1)}, bf16[128,2048]{1,0:T(8,128)(2,1)S(1)}, u32[]{:S(2)}, u32[]{:S(2)}) collective-permute-start(bf16[128,2048]{1,0:T(8,128)(2,1)S(1)} %shard_map.91.refs_6_), channel_id=1, source_target_pairs={{0,26},{1,27},{2,24},{3,25},{4,30},{5,31},{6,28},{7,29},{8,2},{9,3... | collective-permute-start | bytes 1572872 | tf_op jit(solution)/shard_map/ppermute | solution.py:382
  88.9 29.3 %collective-permute-start.14 = (bf16[128,2048]{1,0:T(8,128)(2,1)S(1)}, bf16[128,2048]{1,0:T(8,128)(2,1)S(1)}, u32[]{:S(2)}, u32[]{:S(2)}) collective-permute-start(bf16[128,2048]{1,0:T(8,128)(2,1)S(1)} %shard_map.94), channel_id=1, source_target_pairs={{0,30},{1,31},{2,28},{3,29},{4,26},{5,27},{6,24},{7,25},{8,6},{9,7... | collective-permute-start | bytes 1572872 | tf_op jit(solution)/shard_map/ppermute | solution.py:382

commit v7 on v6

--- a/solution.py
+++ b/solution.py
@@ -426,12 +426,13 @@
     two_next = second_hop(two)
     three_factors = slot_factors(x_three, gain, both, [two])
     one = slot_pieces(u_one, gain, one_factors, turned, experts, [three_factors[0]])
-    one_next = handed(2)(one)
     three = slot_pieces(u_three, gain, three_factors, turned, experts, [one])
     three = joined(experts, 0, two_next, [three], jnp.bfloat16)
-    summed = joined(experts, 1, two_next, [here_next, one_next], jnp.float32)
+    three, one = lax.optimization_barrier((three, one))
     three_next = handed(6)(three)
-    return finish(next_saved, next_upstream, [summed, three_next])[None]
+    one_next = handed(2)(one)
+    summed = joined(experts, 1, two_next, [here_next, three_next], jnp.float32)
+    return finish(next_saved, next_upstream, [summed, one_next])[None]
 
 
 def solution(mesh):

time: 121 us -> 129 us (1.066)
  waiting for transfers between devices: 36.8 us -> 54.8 us
  starting transfers between devices: 32.9 us -> 22.7 us
    ppermute x9, waiting for transfers between devices: 12.1 us -> 25.4 us  [hop(): lax.ppermute(value, 'expert', [(i, i ^ by) for i in range(experts)])]
    ppermute x5, starting transfers between devices: 23.4 us -> 13.2 us  [handed(): return lambda value: lax.ppermute(value, ('section', 'expert'), pairs)]
    ppermute x5, waiting for transfers between devices: 24.8 us -> 29.3 us  [handed(): return lambda value: lax.ppermute(value, ('section', 'expert'), pairs)]
  transfers between devices with their start and end apart: 15 -> 15, of which waited for: 4 -> 5; matrix products, arithmetic and copies ran while one was open for 0% -> 0% of each run, Pallas kernels for 31% -> 29%
where the time goes in v7:
time: 129 us; the launch traced here: 127 us
  waiting for transfers between devices  54.8 us (42%)
  Pallas kernels  38.8 us (30%)
  starting transfers between devices  22.7 us (18%)
  local copies, waits for them, and re-layouts  11 us (9%)
    ppermute x5, waiting for transfers between devices, handed(): return lambda value: lax.ppermute(value, ('section', 'expert'), pairs)  29.3 us
    ppermute x9, waiting for transfers between devices, hop(): lax.ppermute(value, 'expert', [(i, i ^ by) for i in range(experts)])  25.4 us
    pallas_call x3, Pallas kernels, slot_pieces(): pl.pallas_call(functools.partial(pieces_kernel, experts, pairs), in_specs...  14.7 us
    ppermute x5, starting transfers between devices, handed(): return lambda value: lax.ppermute(value, ('section', 'expert'), pairs)  13.2 us
    pallas_call x2, Pallas kernels, turning_pieces(): pl.pallas_call(functools.partial(turning_kernel, experts, len(start), fli...  11.1 us
    unnamed x26, local copies, waits for them, and re-layouts  11 us
    pallas_call x5, Pallas kernels, slot_factors(): pl.pallas_call(functools.partial(factors_kernel, pairs), in_specs=[in_vme...  10.8 us
    ppermute x9, starting transfers between devices, hop(): lax.ppermute(value, 'expert', [(i, i ^ by) for i in range(experts)])  7.43 us
  transfers between devices with their start and end apart: 15, of which 5 were waited for; matrix products, arithmetic and copies ran while one was open for 0% of the time, Pallas kernels for 29%

profile of v7, /device:TPU:8, one launch (start us, length us, event | category | flops | bytes accessed | tf_op | source)
XLA Modules:
  0.0 127.4 jit_solution(18043582974832826756)
XLA Ops:
  0.0 0.0 collective-permute-start
  0.0 0.5 collective-permute-start.1
  0.5 2.6 %collective-permute-start.6 = (bf16[128,2048]{1,0:T(8,128)(2,1)}, bf16[128,2048]{1,0:T(8,128)(2,1)S(1)}, u32[]{:S(2)}, u32[]{:S(2)}) collective-permute-start(bf16[128,2048]{1,0:T(8,128)(2,1)} %bitcast.26), channel_id=1, source_target_pairs={{0,4},{1,5},{2,6},{3,7},{4,0},{5,1},{6,2},{7,3},{8,12},{9,13},{10,... | collective-permute-start | bytes 1572872 | tf_op jit(solution)/shard_map/ppermute | solution.py:374
  3.1 0.4 collective-permute-start.5
  3.6 1.0 copy-done.9
  4.6 0.7 copy-done.11
  5.3 0.7 copy-done.12
  6.0 0.3 shard_map.82.rows_ref
  6.3 0.0 copy-start
  6.3 1.9 %copy-done = bf16[1,1,2048,768]{3,2,1,0:T(8,128)(2,1)S(1)} copy-done((bf16[1,1,2048,768]{3,2,1,0:T(8,128)(2,1)S(1)}, bf16[1,1,2048,768]{3,2,1,0:T(8,128)(2,1)}, u32[]{:S(2)}) %copy-start) | copy-done | bytes 3145752
  8.2 1.9 %copy-done.2 = bf16[1,1,2048,768]{3,2,1,0:T(8,128)(2,1)S(1)} copy-done((bf16[1,1,2048,768]{3,2,1,0:T(8,128)(2,1)S(1)}, bf16[1,1,2048,768]{3,2,1,0:T(8,128)(2,1)}, u32[]{:S(2)}) %copy-start.2) | copy-done | bytes 3145752
  10.1 1.0 copy-done.5
  11.1 0.7 copy-done.7
  11.8 1.6 %shard_map.83 = (f32[1,128,768]{2,1,0:T(8,128)S(1)}, f32[1,128,768]{2,1,0:T(8,128)S(1)}) custom-call(bf16[128,2048]{1,0:T(8,128)(2,1)S(1)} %bitcast.28, f32[1,2048]{1,0:T(1,128)S(1)} %copy-done.7, bf16[2048,768]{1,0:T(8,128)(2,1)S(1)} %bitcast.13, bf16[2048,768]{1,0:T(8,128)(2,1)S(1)} %bitcast.19), custom_call_target="tpu_custom_call" | custom-call | flops 1610612736 | bytes 6291456 | tf_op jit(solution)/shard_map/pallas_call | solution.py:187
  13.5 0.2 copy-done.1
  13.7 1.0 copy-done.3
  14.7 1.9 %copy-done.4 = bf16[1,1,768,2048]{3,2,1,0:T(8,128)(2,1)S(1)} copy-done((bf16[1,1,768,2048]{3,2,1,0:T(8,128)(2,1)S(1)}, bf16[1,1,768,2048]{3,2,1,0:T(8,128)(2,1)}, u32[]{:S(2)}) %copy-start.4) | copy-done | bytes 3145752
  16.6 5.5 %shard_map.85 = (f32[128,2048]{1,0:T(8,128)S(1)}, bf16[768,2048]{1,0:T(8,128)(2,1)S(1)}, bf16[768,2048]{1,0:T(8,128)(2,1)S(1)}, bf16[2048,768]{1,0:T(8,128)(2,1)S(1)}) custom-call(bf16[128,2176]{1,0:T(8,128)(2,1)S(1)} %shard_map.82.rows_ref, f32[1,2048]{1,0:T(1,128)S(1)} %copy-done.8, f32[1,128,768]{2,1,0:T(8,128)S(1)} %get-tuple-element.33.refs_2_.gate_ref, ...), custom_call_target="tpu_custom_call" | custom-call | flops 2415919104 | bytes 9437184 | tf_op jit(solution)/shard_map/pallas_call | solution.py:253
  22.1 0.1 collective-permute-start.4
  22.2 0.0 collective-permute-done.1.refs_1_.refs_3_
  22.2 1.9 %collective-permute-start.12 = (bf16[128,2176]{1,0:T(8,128)(2,1)S(1)}, bf16[128,2176]{1,0:T(8,128)(2,1)S(1)}, u32[]{:S(2)}, u32[]{:S(2)}) collective-permute-start(bf16[128,2176]{1,0:T(8,128)(2,1)S(1)} %shard_map.82.rows_ref), channel_id=1, source_target_pairs={{0,2},{1,3},{2,0},{3,1},{4,6},{5,7},{6,4},{7,5},{8,10},{9,11},{10,... | collective-permute-start | bytes 1671176 | tf_op jit(solution)/shard_map/ppermute | solution.py:374
  24.1 1.6 %shard_map.84 = (f32[1,128,768]{2,1,0:T(8,128)S(1)}, f32[1,128,768]{2,1,0:T(8,128)S(1)}) custom-call(bf16[128,2048]{1,0:T(8,128)(2,1)S(1)} %bitcast.29, f32[1,2048]{1,0:T(1,128)S(1)} %copy-done.8, bf16[2048,768]{1,0:T(8,128)(2,1)S(1)} %collective-permute-done.refs_0_.refs_2_, bf16[2048,768]{1,0:T(8,128)(2,1)S(1)} %collective-permute-done.1.refs_1_.refs_3_, ...), custom_call_target="tpu_custom_call" | custom-call | flops 1610612736 | bytes 6291456 | tf_op jit(solution)/shard_map/pallas_call | solution.py:187
  25.8 0.0 collective-permute-done.7.refs_2_
  25.8 2.5 %collective-permute-start.2 = (bf16[128,2048]{1,0:T(8,128)(2,1)S(1)}, bf16[128,2048]{1,0:T(8,128)(2,1)S(1)}, u32[]{:S(2)}, u32[]{:S(2)}) collective-permute-start(bf16[128,2048]{1,0:T(8,128)(2,1)S(1)} %bitcast.30), channel_id=1, source_target_pairs={{0,24},{1,25},{2,26},{3,27},{4,28},{5,29},{6,30},{7,31},{8,0},{9,1... | collective-permute-start | bytes 1572872 | tf_op jit(solution)/shard_map/ppermute | solution.py:382
  28.3 5.6 %shard_map.86 = (bf16[128,2048]{1,0:T(8,128)(2,1)S(1)}, bf16[768,2048]{1,0:T(8,128)(2,1)S(1)}, bf16[768,2048]{1,0:T(8,128)(2,1)S(1)}, bf16[2048,768]{1,0:T(8,128)(2,1)S(1)}) custom-call(bf16[128,2176]{1,0:T(8,128)(2,1)S(1)} %shard_map.82.rows_ref, f32[1,2048]{1,0:T(1,128)S(1)} %copy-done.8, f32[1,128,768]{2,1,0:T(8,128)S(1)} %get-tuple-element.37.gate_ref, ...), custom_call_target="tpu_custom_call" | custom-call | flops 2415919104 | bytes 9437184 | tf_op jit(solution)/shard_map/pallas_call | solution.py:253
  33.9 0.0 collective-permute-done.6.saved_ref
  33.9 0.6 collective-permute-start.3
  34.5 2.5 %shard_map.87 = (f32[2,128,768]{2,1,0:T(8,128)S(1)}, f32[2,128,768]{2,1,0:T(8,128)S(1)}) custom-call(bf16[128,2048]{1,0:T(8,128)(2,1)S(1)} %collective-permute-done.6.saved_ref, f32[1,2048]{1,0:T(1,128)S(1)} %copy-done.8, bf16[2048,768]{1,0:T(8,128)(2,1)S(1)} %bitcast.15, bf16[2048,768]{1,0:T(8,128)(2,1)S(1)} %bitcast.21, ...), custom_call_target="tpu_custom_call" | custom-call | flops 3221225472 | bytes 12582912 | tf_op jit(solution)/shard_map/pallas_call | solution.py:187
  37.0 0.0 collective-permute-done.5.saved_ref
  37.0 0.5 collective-permute-start.11
  37.5 2.5 %shard_map.88 = (f32[2,128,768]{2,1,0:T(8,128)S(1)}, f32[2,128,768]{2,1,0:T(8,128)S(1)}) custom-call(bf16[128,2048]{1,0:T(8,128)(2,1)S(1)} %collective-permute-done.5.saved_ref, f32[1,2048]{1,0:T(1,128)S(1)} %copy-done.8, bf16[2048,768]{1,0:T(8,128)(2,1)S(1)} %bitcast.16, bf16[2048,768]{1,0:T(8,128)(2,1)S(1)} %bitcast.22, ...), custom_call_target="tpu_custom_call" | custom-call | flops 3221225472 | bytes 12582912 | tf_op jit(solution)/shard_map/pallas_call | solution.py:187
  40.0 10.3 %collective-permute-done.4.rows_ref = bf16[128,2176]{1,0:T(8,128)(2,1)S(1)} collective-permute-done((bf16[128,2176]{1,0:T(8,128)(2,1)S(1)}, bf16[128,2176]{1,0:T(8,128)(2,1)S(1)}, u32[]{:S(2)}, u32[]{:S(2)}) %collective-permute-start.4) | collective-permute-done | bytes 557088 | tf_op jit(solution)/shard_map/ppermute | solution.py:374
  50.3 2.4 %collective-permute-start.9 = (bf16[128,2048]{1,0:T(8,128)(2,1)S(1)}, bf16[128,2048]{1,0:T(8,128)(2,1)S(1)}, u32[]{:S(2)}, u32[]{:S(2)}) collective-permute-start(bf16[128,2048]{1,0:T(8,128)(2,1)S(1)} %get-tuple-element.41.refs_4_), channel_id=1, source_target_pairs={{0,24},{1,25},{2,26},{3,27},{4,28},{5,29},{6,30},{7,31},{8,0},{9,1... | collective-permute-start | bytes 1572872 | tf_op jit(solution)/shard_map/ppermute | solution.py:382
  52.7 1.4 %collective-permute-start.10 = (bf16[128,2176]{1,0:T(8,128)(2,1)S(1)}, bf16[128,2176]{1,0:T(8,128)(2,1)S(1)}, u32[]{:S(2)}, u32[]{:S(2)}) collective-permute-start(bf16[128,2176]{1,0:T(8,128)(2,1)S(1)} %collective-permute-done.4.rows_ref), channel_id=1, source_target_pairs={{0,2},{1,3},{2,0},{3,1},{4,6},{5,7},{6,4},{7,5},{8,10},{9,11},{10,... | collective-permute-start | bytes 1671176 | tf_op jit(solution)/shard_map/ppermute | solution.py:374
  54.1 4.9 %shard_map.89.refs_4_ = bf16[128,2048]{1,0:T(8,128)(2,1)S(1)} custom-call(bf16[128,2176]{1,0:T(8,128)(2,1)S(1)} %collective-permute-done.4.rows_ref, f32[1,2048]{1,0:T(1,128)S(1)} %copy-done.8, f32[2,128,768]{2,1,0:T(8,128)S(1)} %get-tuple-element.42.refs_4_.gate_ref, f32[2,128,768]{2,1,0:T(8,128)S(1)} %get-tuple-element.45.up_ref, ...), custom_call_target="tpu_custom_call" | custom-call | flops 4831838208 | bytes 18874368 | tf_op jit(solution)/shard_map/pallas_call | solution.py:307
  59.0 2.1 %collective-permute-start.8 = (bf16[128,2048]{1,0:T(8,128)(2,1)S(1)}, bf16[128,2048]{1,0:T(8,128)(2,1)S(1)}, u32[]{:S(2)}, u32[]{:S(2)}) collective-permute-start(bf16[128,2048]{1,0:T(8,128)(2,1)S(1)} %shard_map.89.refs_4_), channel_id=1, source_target_pairs={{0,2},{1,3},{2,30},{3,31},{4,24},{5,25},{6,4},{7,5},{8,10},{9,11},... | collective-permute-start | bytes 1572872 | tf_op jit(solution)/shard_map/ppermute | solution.py:397
  61.1 1.8 %collective-permute-done.11.saved_ref = bf16[128,2048]{1,0:T(8,128)(2,1)S(1)} collective-permute-done((bf16[128,2048]{1,0:T(8,128)(2,1)S(1)}, bf16[128,2048]{1,0:T(8,128)(2,1)S(1)}, u32[]{:S(2)}, u32[]{:S(2)}) %collective-permute-start.11) | collective-permute-done | bytes 524320 | tf_op jit(solution)/shard_map/ppermute | solution.py:374
  62.9 2.5 %shard_map.90 = (f32[2,128,768]{2,1,0:T(8,128)S(1)}, f32[2,128,768]{2,1,0:T(8,128)S(1)}) custom-call(bf16[128,2048]{1,0:T(8,128)(2,1)S(1)} %collective-permute-done.11.saved_ref, f32[1,2048]{1,0:T(1,128)S(1)} %copy-done.8, bf16[2048,768]{1,0:T(8,128)(2,1)S(1)} %bitcast.17, bf16[2048,768]{1,0:T(8,128)(2,1)S(1)} %bitcast.23, ...), custom_call_target="tpu_custom_call" | custom-call | flops 3221225472 | bytes 12582912 | tf_op jit(solution)/shard_map/pallas_call | solution.py:187
  65.4 4.9 %shard_map.91.refs_6_ = bf16[128,2048]{1,0:T(8,128)(2,1)S(1)} custom-call(bf16[128,2176]{1,0:T(8,128)(2,1)S(1)} %collective-permute-done.12.rows_ref, f32[1,2048]{1,0:T(1,128)S(1)} %copy-done.8, f32[2,128,768]{2,1,0:T(8,128)S(1)} %get-tuple-element.55.gate_ref, f32[2,128,768]{2,1,0:T(8,128)S(1)} %get-tuple-element.56.up_ref, ...), custom_call_target="tpu_custom_call" | custom-call | flops 4831838208 | bytes 18874368 | tf_op jit(solution)/shard_map/pallas_call | solution.py:307
  70.3 13.4 %collective-permute-done.10.rows_ref = bf16[128,2176]{1,0:T(8,128)(2,1)S(1)} collective-permute-done((bf16[128,2176]{1,0:T(8,128)(2,1)S(1)}, bf16[128,2176]{1,0:T(8,128)(2,1)S(1)}, u32[]{:S(2)}, u32[]{:S(2)}) %collective-permute-start.10) | collective-permute-done | bytes 557088 | tf_op jit(solution)/shard_map/ppermute | solution.py:374
  83.7 4.9 %shard_map.92.refs_0_ = bf16[128,2048]{1,0:T(8,128)(2,1)S(1)} custom-call(bf16[128,2176]{1,0:T(8,128)(2,1)S(1)} %collective-permute-done.10.rows_ref, f32[1,2048]{1,0:T(1,128)S(1)} %copy-done.8, f32[2,128,768]{2,1,0:T(8,128)S(1)} %get-tuple-element.52.refs_6_.gate_ref, f32[2,128,768]{2,1,0:T(8,128)S(1)} %get-tuple-element.53.up_ref, ...), custom_call_target="tpu_custom_call" | custom-call | flops 4831838208 | bytes 18874368 | tf_op jit(solution)/shard_map/pallas_call | solution.py:307
  88.6 0.2 shard_map.93
  88.8 4.3 %collective-permute-start.13 = (bf16[128,2048]{1,0:T(8,128)(2,1)S(1)}, bf16[128,2048]{1,0:T(8,128)(2,1)S(1)}, u32[]{:S(2)}, u32[]{:S(2)}) collective-permute-start(bf16[128,2048]{1,0:T(8,128)(2,1)S(1)} %shard_map.93), channel_id=1, source_target_pairs={{0,30},{1,31},{2,28},{3,29},{4,26},{5,27},{6,24},{7,25},{8,6},{9,7... | collective-permute-start | bytes 1572872 | tf_op jit(solution)/shard_map/ppermute | solution.py:382
  93.1 3.4 %collective-permute-start.14 = (bf16[128,2048]{1,0:T(8,128)(2,1)S(1)}, bf16[128,2048]{1,0:T(8,128)(2,1)S(1)}, u32[]{:S(2)}, u32[]{:S(2)}) collective-permute-start(bf16[128,2048]{1,0:T(8,128)(2,1)S(1)} %shard_map.91.refs_6_), channel_id=1, source_target_pairs={{0,26},{1,27},{2,24},{3,25},{4,30},{5,31},{6,28},{7,29},{8,2},{9,3... | collective-permute-start | bytes 1572872 | tf_op jit(solution)/shard_map/ppermute | solution.py:382
  96.4 26.5 %collective-permute-done.13.refs_1_ = bf16[128,2048]{1,0:T(8,128)(2,1)S(1)} collective-permute-done((bf16[128,2048]{1,0:T(8,128)(2,1)S(1)}, bf16[128,2048]{1,0:T(8,128)(2,1)S(1)}, u32[]{:S(2)}, u32[]{:S(2)}) %collective-permute-start.13) | collective-permute-done | bytes 524320 | tf_op jit(solution)/shard_map/ppermute | solution.py:382
  122.9 0.2 shard_map.94.refs_0_
  123.1 2.9 %collective-permute-done.14.refs_1_ = bf16[128,2048]{1,0:T(8,128)(2,1)S(1)} collective-permute-done((bf16[128,2048]{1,0:T(8,128)(2,1)S(1)}, bf16[128,2048]{1,0:T(8,128)(2,1)S(1)}, u32[]{:S(2)}, u32[]{:S(2)}) %collective-permute-start.14) | collective-permute-done | bytes 524320 | tf_op jit(solution)/shard_map/ppermute | solution.py:382
  126.0 1.5 %shard_map.95 = bf16[128,2048]{1,0:T(8,128)(2,1)} custom-call(bf16[128,2048]{1,0:T(8,128)(2,1)S(1)} %collective-permute-done.2.refs_6_.saved_ref, bf16[128,2048]{1,0:T(8,128)(2,1)S(1)} %collective-permute-done.3.refs_7_.upstream_ref, f32[128,2048]{1,0:T(8,128)S(1)} %shard_map.94.refs_0_, bf16[128,2048]{1,0:T(8,128)(2,1)S(1)} %collective-permute-done.14.refs_1_), custom_call_target="tpu_custom_call" | custom-call | tf_op jit(solution)/shard_map/pallas_call | solution.py:336
  (22 shorter events, 0.0 us)
Async XLA Ops:
  0.0 22.1 %collective-permute-start = (bf16[2048,768]{1,0:T(8,128)(2,1)}, bf16[2048,768]{1,0:T(8,128)(2,1)S(1)}, u32[]{:S(2)}, u32[]{:S(2)}) collective-permute-start(bf16[2048,768]{1,0:T(8,128)(2,1)} %bitcast.12), channel_id=1, source_target_pairs={{0,1},{1,0},{2,3},{3,2},{4,5},{5,4},{6,7},{7,6},{8,9},{9,8},{10,11... | collective-permute-start | bytes 9437192 | tf_op jit(solution)/shard_map/ppermute | solution.py:374
  0.0 22.2 %collective-permute-start.1 = (bf16[2048,768]{1,0:T(8,128)(2,1)}, bf16[2048,768]{1,0:T(8,128)(2,1)S(1)}, u32[]{:S(2)}, u32[]{:S(2)}) collective-permute-start(bf16[2048,768]{1,0:T(8,128)(2,1)} %bitcast.18), channel_id=1, source_target_pairs={{0,1},{1,0},{2,3},{3,2},{4,5},{5,4},{6,7},{7,6},{8,9},{9,8},{10,11... | collective-permute-start | bytes 9437192 | tf_op jit(solution)/shard_map/ppermute | solution.py:374
  0.5 25.3 %collective-permute-start.7 = (bf16[768,2048]{1,0:T(8,128)(2,1)}, bf16[768,2048]{1,0:T(8,128)(2,1)S(1)}, u32[]{:S(2)}, u32[]{:S(2)}) collective-permute-start(bf16[768,2048]{1,0:T(8,128)(2,1)} %bitcast.24), channel_id=1, source_target_pairs={{0,1},{1,0},{2,3},{3,2},{4,5},{5,4},{6,7},{7,6},{8,9},{9,8},{10,11... | collective-permute-start | bytes 9437192 | tf_op jit(solution)/shard_map/ppermute | solution.py:374
  0.5 33.3 %collective-permute-start.6 = (bf16[128,2048]{1,0:T(8,128)(2,1)}, bf16[128,2048]{1,0:T(8,128)(2,1)S(1)}, u32[]{:S(2)}, u32[]{:S(2)}) collective-permute-start(bf16[128,2048]{1,0:T(8,128)(2,1)} %bitcast.26), channel_id=1, source_target_pairs={{0,4},{1,5},{2,6},{3,7},{4,0},{5,1},{6,2},{7,3},{8,12},{9,13},{10,... | collective-permute-start | bytes 1572872 | tf_op jit(solution)/shard_map/ppermute | solution.py:374
  3.1 33.9 %collective-permute-start.5 = (bf16[128,2048]{1,0:T(8,128)(2,1)}, bf16[128,2048]{1,0:T(8,128)(2,1)S(1)}, u32[]{:S(2)}, u32[]{:S(2)}) collective-permute-start(bf16[128,2048]{1,0:T(8,128)(2,1)} %bitcast.27), channel_id=1, source_target_pairs={{0,2},{1,3},{2,0},{3,1},{4,6},{5,7},{6,4},{7,5},{8,10},{9,11},{10,... | collective-permute-start | bytes 1572872 | tf_op jit(solution)/shard_map/ppermute | solution.py:374
  3.6 1.0 copy-start.9
  4.6 0.7 copy-start.11
  5.3 0.7 copy-start.12
  6.3 1.9 %copy-start = (bf16[1,1,2048,768]{3,2,1,0:T(8,128)(2,1)S(1)}, bf16[1,1,2048,768]{3,2,1,0:T(8,128)(2,1)}, u32[]{:S(2)}) copy-start(bf16[1,1,2048,768]{3,2,1,0:T(8,128)(2,1)} %param.11) | copy-start | bytes 9437188
  8.2 1.9 %copy-start.2 = (bf16[1,1,2048,768]{3,2,1,0:T(8,128)(2,1)S(1)}, bf16[1,1,2048,768]{3,2,1,0:T(8,128)(2,1)}, u32[]{:S(2)}) copy-start(bf16[1,1,2048,768]{3,2,1,0:T(8,128)(2,1)} %param.12) | copy-start | bytes 9437188
  10.1 1.0 copy-start.5
  11.1 0.7 copy-start.7
  11.8 1.9 %copy-start.1 = (bf16[1,1,2048,768]{3,2,1,0:T(8,128)(2,1)S(1)}, bf16[1,1,2048,768]{3,2,1,0:T(8,128)(2,1)}, u32[]{:S(2)}) copy-start(bf16[1,1,2048,768]{3,2,1,0:T(8,128)(2,1)} %param.11) | copy-start | bytes 9437188
  11.8 2.8 %copy-start.3 = (bf16[1,1,2048,768]{3,2,1,0:T(8,128)(2,1)S(1)}, bf16[1,1,2048,768]{3,2,1,0:T(8,128)(2,1)}, u32[]{:S(2)}) copy-start(bf16[1,1,2048,768]{3,2,1,0:T(8,128)(2,1)} %param.12) | copy-start | bytes 9437188
  11.8 2.8 %copy-start.8 = (f32[1,2048]{1,0:T(1,128)S(1)}, f32[1,2048]{1,0:T(1,128)}, u32[]{:S(2)}) copy-start(f32[1,2048]{1,0:T(1,128)} %gain_ref.19) | copy-start | bytes 24580
  14.7 1.9 %copy-start.4 = (bf16[1,1,768,2048]{3,2,1,0:T(8,128)(2,1)S(1)}, bf16[1,1,768,2048]{3,2,1,0:T(8,128)(2,1)}, u32[]{:S(2)}) copy-start(bf16[1,1,768,2048]{3,2,1,0:T(8,128)(2,1)} %param.13) | copy-start | bytes 9437188
  16.6 7.6 %copy-start.6 = (bf16[1,128,2048]{2,1,0:T(8,128)(2,1)S(1)}, bf16[1,128,2048]{2,1,0:T(8,128)(2,1)}, u32[]{:S(2)}) copy-start(bf16[1,128,2048]{2,1,0:T(8,128)(2,1)} %param.8) | copy-start | bytes 1572868
  22.1 28.1 %collective-permute-start.4 = (bf16[128,2176]{1,0:T(8,128)(2,1)S(1)}, bf16[128,2176]{1,0:T(8,128)(2,1)S(1)}, u32[]{:S(2)}, u32[]{:S(2)}) collective-permute-start(bf16[128,2176]{1,0:T(8,128)(2,1)S(1)} %shard_map.82.rows_ref), channel_id=1, source_target_pairs={{0,4},{1,5},{2,6},{3,7},{4,0},{5,1},{6,2},{7,3},{8,12},{9,13},{10,... | collective-permute-start | bytes 1671176 | tf_op jit(solution)/shard_map/ppermute | solution.py:374
  22.2 43.2 %collective-permute-start.12 = (bf16[128,2176]{1,0:T(8,128)(2,1)S(1)}, bf16[128,2176]{1,0:T(8,128)(2,1)S(1)}, u32[]{:S(2)}, u32[]{:S(2)}) collective-permute-start(bf16[128,2176]{1,0:T(8,128)(2,1)S(1)} %shard_map.82.rows_ref), channel_id=1, source_target_pairs={{0,2},{1,3},{2,0},{3,1},{4,6},{5,7},{6,4},{7,5},{8,10},{9,11},{10,... | collective-permute-start | bytes 1671176 | tf_op jit(solution)/shard_map/ppermute | solution.py:374
  25.8 27.0 %collective-permute-start.2 = (bf16[128,2048]{1,0:T(8,128)(2,1)S(1)}, bf16[128,2048]{1,0:T(8,128)(2,1)S(1)}, u32[]{:S(2)}, u32[]{:S(2)}) collective-permute-start(bf16[128,2048]{1,0:T(8,128)(2,1)S(1)} %bitcast.30), channel_id=1, source_target_pairs={{0,24},{1,25},{2,26},{3,27},{4,28},{5,29},{6,30},{7,31},{8,0},{9,1... | collective-permute-start | bytes 1572872 | tf_op jit(solution)/shard_map/ppermute | solution.py:382
  28.3 5.6 %copy-start.10 = (bf16[1,128,2048]{2,1,0:T(8,128)(2,1)S(1)}, bf16[1,128,2048]{2,1,0:T(8,128)(2,1)}, u32[]{:S(2)}) copy-start(bf16[1,128,2048]{2,1,0:T(8,128)(2,1)} %param.9) | copy-start | bytes 1572868
  33.9 20.3 %collective-permute-start.3 = (bf16[128,2048]{1,0:T(8,128)(2,1)S(1)}, bf16[128,2048]{1,0:T(8,128)(2,1)S(1)}, u32[]{:S(2)}, u32[]{:S(2)}) collective-permute-start(bf16[128,2048]{1,0:T(8,128)(2,1)S(1)} %bitcast.32), channel_id=1, source_target_pairs={{0,24},{1,25},{2,26},{3,27},{4,28},{5,29},{6,30},{7,31},{8,0},{9,1... | collective-permute-start | bytes 1572872 | tf_op jit(solution)/shard_map/ppermute | solution.py:382
  37.0 25.9 %collective-permute-start.11 = (bf16[128,2048]{1,0:T(8,128)(2,1)S(1)}, bf16[128,2048]{1,0:T(8,128)(2,1)S(1)}, u32[]{:S(2)}, u32[]{:S(2)}) collective-permute-start(bf16[128,2048]{1,0:T(8,128)(2,1)S(1)} %collective-permute-done.6.saved_ref), channel_id=1, source_target_pairs={{0,2},{1,3},{2,0},{3,1},{4,6},{5,7},{6,4},{7,5},{8,10},{9,11},{10,... | collective-permute-start | bytes 1572872 | tf_op jit(solution)/shard_map/ppermute | solution.py:374
  50.3 46.1 %collective-permute-start.9 = (bf16[128,2048]{1,0:T(8,128)(2,1)S(1)}, bf16[128,2048]{1,0:T(8,128)(2,1)S(1)}, u32[]{:S(2)}, u32[]{:S(2)}) collective-permute-start(bf16[128,2048]{1,0:T(8,128)(2,1)S(1)} %get-tuple-element.41.refs_4_), channel_id=1, source_target_pairs={{0,24},{1,25},{2,26},{3,27},{4,28},{5,29},{6,30},{7,31},{8,0},{9,1... | collective-permute-start | bytes 1572872 | tf_op jit(solution)/shard_map/ppermute | solution.py:382
  52.7 31.0 %collective-permute-start.10 = (bf16[128,2176]{1,0:T(8,128)(2,1)S(1)}, bf16[128,2176]{1,0:T(8,128)(2,1)S(1)}, u32[]{:S(2)}, u32[]{:S(2)}) collective-permute-start(bf16[128,2176]{1,0:T(8,128)(2,1)S(1)} %collective-permute-done.4.rows_ref), channel_id=1, source_target_pairs={{0,2},{1,3},{2,0},{3,1},{4,6},{5,7},{6,4},{7,5},{8,10},{9,11},{10,... | collective-permute-start | bytes 1671176 | tf_op jit(solution)/shard_map/ppermute | solution.py:374
  59.0 29.6 %collective-permute-start.8 = (bf16[128,2048]{1,0:T(8,128)(2,1)S(1)}, bf16[128,2048]{1,0:T(8,128)(2,1)S(1)}, u32[]{:S(2)}, u32[]{:S(2)}) collective-permute-start(bf16[128,2048]{1,0:T(8,128)(2,1)S(1)} %shard_map.89.refs_4_), channel_id=1, source_target_pairs={{0,2},{1,3},{2,30},{3,31},{4,24},{5,25},{6,4},{7,5},{8,10},{9,11},... | collective-permute-start | bytes 1572872 | tf_op jit(solution)/shard_map/ppermute | solution.py:397
  88.8 34.1 %collective-permute-start.13 = (bf16[128,2048]{1,0:T(8,128)(2,1)S(1)}, bf16[128,2048]{1,0:T(8,128)(2,1)S(1)}, u32[]{:S(2)}, u32[]{:S(2)}) collective-permute-start(bf16[128,2048]{1,0:T(8,128)(2,1)S(1)} %shard_map.93), channel_id=1, source_target_pairs={{0,30},{1,31},{2,28},{3,29},{4,26},{5,27},{6,24},{7,25},{8,6},{9,7... | collective-permute-start | bytes 1572872 | tf_op jit(solution)/shard_map/ppermute | solution.py:382
  93.1 32.9 %collective-permute-start.14 = (bf16[128,2048]{1,0:T(8,128)(2,1)S(1)}, bf16[128,2048]{1,0:T(8,128)(2,1)S(1)}, u32[]{:S(2)}, u32[]{:S(2)}) collective-permute-start(bf16[128,2048]{1,0:T(8,128)(2,1)S(1)} %shard_map.91.refs_6_), channel_id=1, source_target_pairs={{0,26},{1,27},{2,24},{3,25},{4,30},{5,31},{6,28},{7,29},{8,2},{9,3... | collective-permute-start | bytes 1572872 | tf_op jit(solution)/shard_map/ppermute | solution.py:382

commit v8 on v6

--- a/solution.py
+++ b/solution.py
@@ -420,14 +420,16 @@
     one_factors = slot_factors(x_one, gain, both, [two_factors[0]])
     u_two, one_gate = lax.optimization_barrier((u_two, one_factors[0]))
     one_factors = (one_gate, one_factors[1])
-    here_next = handed(0)(here)
     u_three = hop(2)(u_two)
     two = slot_pieces(u_two, gain, two_factors, turned, experts, [next_saved, next_upstream])
     two_next = second_hop(two)
     three_factors = slot_factors(x_three, gain, both, [two])
+    here_later, three_gate = lax.optimization_barrier((here, three_factors[0]))
+    three_factors = (three_gate, three_factors[1])
+    here_next = handed(0)(here_later)
     one = slot_pieces(u_one, gain, one_factors, turned, experts, [three_factors[0]])
     one_next = handed(2)(one)
-    three = slot_pieces(u_three, gain, three_factors, turned, experts, [one])
+    three = slot_pieces(u_three, gain, three_factors, turned, experts, [one, here_next])
     three = joined(experts, 0, two_next, [three], jnp.bfloat16)
     summed = joined(experts, 1, two_next, [here_next, one_next], jnp.float32)
     three_next = handed(6)(three)

time: 121 us -> 126 us (1.041)
  the two profiles are of different devices: /device:TPU:8 before, /device:TPU:0 now
where the time goes in v8:
time: 126 us
  waiting for transfers between devices  50 us (40%)
  Pallas kernels  38.8 us (31%)
  starting transfers between devices  25.7 us (20%)
  local copies, waits for them, and re-layouts  11 us (9%)
    ppermute x5, waiting for transfers between devices, handed(): return lambda value: lax.ppermute(value, ('section', 'expert'), pairs)  25.5 us
    ppermute x9, waiting for transfers between devices, hop(): lax.ppermute(value, 'expert', [(i, i ^ by) for i in range(experts)])  24.4 us
    ppermute x5, starting transfers between devices, handed(): return lambda value: lax.ppermute(value, ('section', 'expert'), pairs)  14.9 us
    pallas_call x3, Pallas kernels, slot_pieces(): pl.pallas_call(functools.partial(pieces_kernel, experts, pairs), in_specs...  14.7 us
    pallas_call x2, Pallas kernels, turning_pieces(): pl.pallas_call(functools.partial(turning_kernel, experts, len(start), fli...  11.1 us
    unnamed x26, local copies, waits for them, and re-layouts  11 us
    pallas_call x5, Pallas kernels, slot_factors(): pl.pallas_call(functools.partial(factors_kernel, pairs), in_specs=[in_vme...  10.8 us
    ppermute x9, starting transfers between devices, hop(): lax.ppermute(value, 'expert', [(i, i ^ by) for i in range(experts)])  9.04 us
  transfers between devices with their start and end apart: 15, of which 5 were waited for; matrix products, arithmetic and copies ran while one was open for 0% of the time, Pallas kernels for 30%

profile of v8, /device:TPU:0, one launch (start us, length us, event | category | flops | bytes accessed | tf_op | source)
XLA Modules:
  0.0 125.6 jit_solution(18435099205751922636)
XLA Ops:
  0.0 0.5 collective-permute-start
  0.5 0.1 collective-permute-start.1
  0.5 0.5 collective-permute-start.7
  1.0 3.6 %collective-permute-start.6 = (bf16[128,2048]{1,0:T(8,128)(2,1)}, bf16[128,2048]{1,0:T(8,128)(2,1)S(1)}, u32[]{:S(2)}, u32[]{:S(2)}) collective-permute-start(bf16[128,2048]{1,0:T(8,128)(2,1)} %bitcast.26), channel_id=1, source_target_pairs={{0,4},{1,5},{2,6},{3,7},{4,0},{5,1},{6,2},{7,3},{8,12},{9,13},{10,... | collective-permute-start | bytes 1572872 | tf_op jit(solution)/shard_map/ppermute | solution.py:374
  4.6 1.6 %collective-permute-start.5 = (bf16[128,2048]{1,0:T(8,128)(2,1)}, bf16[128,2048]{1,0:T(8,128)(2,1)S(1)}, u32[]{:S(2)}, u32[]{:S(2)}) collective-permute-start(bf16[128,2048]{1,0:T(8,128)(2,1)} %bitcast.27), channel_id=1, source_target_pairs={{0,2},{1,3},{2,0},{3,1},{4,6},{5,7},{6,4},{7,5},{8,10},{9,11},{10,... | collective-permute-start | bytes 1572872 | tf_op jit(solution)/shard_map/ppermute | solution.py:374
  6.1 1.0 copy-done.9
  7.2 0.7 copy-done.11
  7.9 0.7 copy-done.12
  8.5 0.3 shard_map.82.rows_ref
  8.9 0.0 copy-start
  8.9 1.9 %copy-done = bf16[1,1,2048,768]{3,2,1,0:T(8,128)(2,1)S(1)} copy-done((bf16[1,1,2048,768]{3,2,1,0:T(8,128)(2,1)S(1)}, bf16[1,1,2048,768]{3,2,1,0:T(8,128)(2,1)}, u32[]{:S(2)}) %copy-start) | copy-done | bytes 3145752
  10.8 1.9 %copy-done.2 = bf16[1,1,2048,768]{3,2,1,0:T(8,128)(2,1)S(1)} copy-done((bf16[1,1,2048,768]{3,2,1,0:T(8,128)(2,1)S(1)}, bf16[1,1,2048,768]{3,2,1,0:T(8,128)(2,1)}, u32[]{:S(2)}) %copy-start.2) | copy-done | bytes 3145752
  12.7 1.0 copy-done.5
  13.7 0.7 copy-done.7
  14.4 1.6 %shard_map.83 = (f32[1,128,768]{2,1,0:T(8,128)S(1)}, f32[1,128,768]{2,1,0:T(8,128)S(1)}) custom-call(bf16[128,2048]{1,0:T(8,128)(2,1)S(1)} %bitcast.28, f32[1,2048]{1,0:T(1,128)S(1)} %copy-done.7, bf16[2048,768]{1,0:T(8,128)(2,1)S(1)} %bitcast.13, bf16[2048,768]{1,0:T(8,128)(2,1)S(1)} %bitcast.19), custom_call_target="tpu_custom_call" | custom-call | flops 1610612736 | bytes 6291456 | tf_op jit(solution)/shard_map/pallas_call | solution.py:187
  16.1 0.2 copy-done.1
  16.3 1.0 copy-done.3
  17.2 1.9 %copy-done.4 = bf16[1,1,768,2048]{3,2,1,0:T(8,128)(2,1)S(1)} copy-done((bf16[1,1,768,2048]{3,2,1,0:T(8,128)(2,1)S(1)}, bf16[1,1,768,2048]{3,2,1,0:T(8,128)(2,1)}, u32[]{:S(2)}) %copy-start.4) | copy-done | bytes 3145752
  19.1 5.5 %shard_map.85 = (f32[128,2048]{1,0:T(8,128)S(1)}, bf16[768,2048]{1,0:T(8,128)(2,1)S(1)}, bf16[768,2048]{1,0:T(8,128)(2,1)S(1)}, bf16[2048,768]{1,0:T(8,128)(2,1)S(1)}) custom-call(bf16[128,2176]{1,0:T(8,128)(2,1)S(1)} %shard_map.82.rows_ref, f32[1,2048]{1,0:T(1,128)S(1)} %copy-done.8, f32[1,128,768]{2,1,0:T(8,128)S(1)} %get-tuple-element.33.refs_2_.gate_ref, ...), custom_call_target="tpu_custom_call" | custom-call | flops 2415919104 | bytes 9437184 | tf_op jit(solution)/shard_map/pallas_call | solution.py:253
  24.7 0.4 collective-permute-start.4
  25.1 0.0 collective-permute-done.1.refs_1_.refs_3_
  25.1 0.2 collective-permute-start.11
  25.3 1.6 %shard_map.84 = (f32[1,128,768]{2,1,0:T(8,128)S(1)}, f32[1,128,768]{2,1,0:T(8,128)S(1)}) custom-call(bf16[128,2048]{1,0:T(8,128)(2,1)S(1)} %bitcast.29, f32[1,2048]{1,0:T(1,128)S(1)} %copy-done.8, bf16[2048,768]{1,0:T(8,128)(2,1)S(1)} %collective-permute-done.refs_0_.refs_2_, bf16[2048,768]{1,0:T(8,128)(2,1)S(1)} %collective-permute-done.1.refs_1_.refs_3_, ...), custom_call_target="tpu_custom_call" | custom-call | flops 1610612736 | bytes 6291456 | tf_op jit(solution)/shard_map/pallas_call | solution.py:187
  27.0 0.0 collective-permute-done.7.refs_2_
  27.0 2.8 %collective-permute-start.2 = (bf16[128,2048]{1,0:T(8,128)(2,1)S(1)}, bf16[128,2048]{1,0:T(8,128)(2,1)S(1)}, u32[]{:S(2)}, u32[]{:S(2)}) collective-permute-start(bf16[128,2048]{1,0:T(8,128)(2,1)S(1)} %bitcast.30), channel_id=1, source_target_pairs={{0,24},{1,25},{2,26},{3,27},{4,28},{5,29},{6,30},{7,31},{8,0},{9,1... | collective-permute-start | bytes 1572872 | tf_op jit(solution)/shard_map/ppermute | solution.py:382
  29.7 5.6 %shard_map.86 = (bf16[128,2048]{1,0:T(8,128)(2,1)S(1)}, bf16[768,2048]{1,0:T(8,128)(2,1)S(1)}, bf16[768,2048]{1,0:T(8,128)(2,1)S(1)}, bf16[2048,768]{1,0:T(8,128)(2,1)S(1)}) custom-call(bf16[128,2176]{1,0:T(8,128)(2,1)S(1)} %shard_map.82.rows_ref, f32[1,2048]{1,0:T(1,128)S(1)} %copy-done.8, f32[1,128,768]{2,1,0:T(8,128)S(1)} %get-tuple-element.37.gate_ref, ...), custom_call_target="tpu_custom_call" | custom-call | flops 2415919104 | bytes 9437184 | tf_op jit(solution)/shard_map/pallas_call | solution.py:253
  35.3 0.0 collective-permute-done.6.saved_ref
  35.3 0.6 collective-permute-start.3
  35.9 2.5 %shard_map.87 = (f32[2,128,768]{2,1,0:T(8,128)S(1)}, f32[2,128,768]{2,1,0:T(8,128)S(1)}) custom-call(bf16[128,2048]{1,0:T(8,128)(2,1)S(1)} %collective-permute-done.6.saved_ref, f32[1,2048]{1,0:T(1,128)S(1)} %copy-done.8, bf16[2048,768]{1,0:T(8,128)(2,1)S(1)} %bitcast.15, bf16[2048,768]{1,0:T(8,128)(2,1)S(1)} %bitcast.21, ...), custom_call_target="tpu_custom_call" | custom-call | flops 3221225472 | bytes 12582912 | tf_op jit(solution)/shard_map/pallas_call | solution.py:187
  38.4 1.6 %collective-permute-start.9 = (bf16[128,2048]{1,0:T(8,128)(2,1)S(1)}, bf16[128,2048]{1,0:T(8,128)(2,1)S(1)}, u32[]{:S(2)}, u32[]{:S(2)}) collective-permute-start(bf16[128,2048]{1,0:T(8,128)(2,1)S(1)} %collective-permute-done.6.saved_ref), channel_id=1, source_target_pairs={{0,2},{1,3},{2,0},{3,1},{4,6},{5,7},{6,4},{7,5},{8,10},{9,11},{10,... | collective-permute-start | bytes 1572872 | tf_op jit(solution)/shard_map/ppermute | solution.py:374
  40.1 2.5 %shard_map.88 = (f32[2,128,768]{2,1,0:T(8,128)S(1)}, f32[2,128,768]{2,1,0:T(8,128)S(1)}) custom-call(bf16[128,2048]{1,0:T(8,128)(2,1)S(1)} %collective-permute-done.5.saved_ref, f32[1,2048]{1,0:T(1,128)S(1)} %copy-done.8, bf16[2048,768]{1,0:T(8,128)(2,1)S(1)} %bitcast.16, bf16[2048,768]{1,0:T(8,128)(2,1)S(1)} %bitcast.22, ...), custom_call_target="tpu_custom_call" | custom-call | flops 3221225472 | bytes 12582912 | tf_op jit(solution)/shard_map/pallas_call | solution.py:187
  42.6 10.0 %collective-permute-done.4.rows_ref = bf16[128,2176]{1,0:T(8,128)(2,1)S(1)} collective-permute-done((bf16[128,2176]{1,0:T(8,128)(2,1)S(1)}, bf16[128,2176]{1,0:T(8,128)(2,1)S(1)}, u32[]{:S(2)}, u32[]{:S(2)}) %collective-permute-start.4) | collective-permute-done | bytes 557088 | tf_op jit(solution)/shard_map/ppermute | solution.py:374
  52.6 0.7 collective-permute-start.13
  53.3 4.9 %shard_map.89.refs_4_ = bf16[128,2048]{1,0:T(8,128)(2,1)S(1)} custom-call(bf16[128,2176]{1,0:T(8,128)(2,1)S(1)} %collective-permute-done.4.rows_ref, f32[1,2048]{1,0:T(1,128)S(1)} %copy-done.8, f32[2,128,768]{2,1,0:T(8,128)S(1)} %get-tuple-element.42.refs_4_.gate_ref, f32[2,128,768]{2,1,0:T(8,128)S(1)} %get-tuple-element.45.up_ref, ...), custom_call_target="tpu_custom_call" | custom-call | flops 4831838208 | bytes 18874368 | tf_op jit(solution)/shard_map/pallas_call | solution.py:307
  58.2 5.9 %collective-permute-done.9.saved_ref = bf16[128,2048]{1,0:T(8,128)(2,1)S(1)} collective-permute-done((bf16[128,2048]{1,0:T(8,128)(2,1)S(1)}, bf16[128,2048]{1,0:T(8,128)(2,1)S(1)}, u32[]{:S(2)}, u32[]{:S(2)}) %collective-permute-start.9) | collective-permute-done | bytes 524320 | tf_op jit(solution)/shard_map/ppermute | solution.py:374
  64.1 2.5 %shard_map.90 = (f32[2,128,768]{2,1,0:T(8,128)S(1)}, f32[2,128,768]{2,1,0:T(8,128)S(1)}) custom-call(bf16[128,2048]{1,0:T(8,128)(2,1)S(1)} %collective-permute-done.9.saved_ref, f32[1,2048]{1,0:T(1,128)S(1)} %copy-done.8, bf16[2048,768]{1,0:T(8,128)(2,1)S(1)} %bitcast.17, bf16[2048,768]{1,0:T(8,128)(2,1)S(1)} %bitcast.23, ...), custom_call_target="tpu_custom_call" | custom-call | flops 3221225472 | bytes 12582912 | tf_op jit(solution)/shard_map/pallas_call | solution.py:187
  66.6 2.6 %collective-permute-start.10 = (bf16[128,2048]{1,0:T(8,128)(2,1)S(1)}, bf16[128,2048]{1,0:T(8,128)(2,1)S(1)}, u32[]{:S(2)}, u32[]{:S(2)}) collective-permute-start(bf16[128,2048]{1,0:T(8,128)(2,1)S(1)} %get-tuple-element.53.refs_4_), channel_id=1, source_target_pairs={{0,24},{1,25},{2,26},{3,27},{4,28},{5,29},{6,30},{7,31},{8,0},{9,1... | collective-permute-start | bytes 1572872 | tf_op jit(solution)/shard_map/ppermute | solution.py:382
  69.2 1.7 %collective-permute-start.8 = (bf16[128,2048]{1,0:T(8,128)(2,1)S(1)}, bf16[128,2048]{1,0:T(8,128)(2,1)S(1)}, u32[]{:S(2)}, u32[]{:S(2)}) collective-permute-start(bf16[128,2048]{1,0:T(8,128)(2,1)S(1)} %shard_map.89.refs_4_), channel_id=1, source_target_pairs={{0,2},{1,3},{2,30},{3,31},{4,24},{5,25},{6,4},{7,5},{8,10},{9,11},... | collective-permute-start | bytes 1572872 | tf_op jit(solution)/shard_map/ppermute | solution.py:397
  70.9 4.9 %shard_map.91.refs_6_ = bf16[128,2048]{1,0:T(8,128)(2,1)S(1)} custom-call(bf16[128,2176]{1,0:T(8,128)(2,1)S(1)} %collective-permute-done.11.rows_ref, f32[1,2048]{1,0:T(1,128)S(1)} %copy-done.8, f32[2,128,768]{2,1,0:T(8,128)S(1)} %get-tuple-element.55.gate_ref, f32[2,128,768]{2,1,0:T(8,128)S(1)} %get-tuple-element.56.up_ref, ...), custom_call_target="tpu_custom_call" | custom-call | flops 4831838208 | bytes 18874368 | tf_op jit(solution)/shard_map/pallas_call | solution.py:307
  75.8 3.0 %collective-permute-start.12 = (bf16[128,2048]{1,0:T(8,128)(2,1)S(1)}, bf16[128,2048]{1,0:T(8,128)(2,1)S(1)}, u32[]{:S(2)}, u32[]{:S(2)}) collective-permute-start(bf16[128,2048]{1,0:T(8,128)(2,1)S(1)} %shard_map.91.refs_6_), channel_id=1, source_target_pairs={{0,26},{1,27},{2,24},{3,25},{4,30},{5,31},{6,28},{7,29},{8,2},{9,3... | collective-permute-start | bytes 1572872 | tf_op jit(solution)/shard_map/ppermute | solution.py:382
  78.8 8.5 %collective-permute-done.13.rows_ref = bf16[128,2176]{1,0:T(8,128)(2,1)S(1)} collective-permute-done((bf16[128,2176]{1,0:T(8,128)(2,1)S(1)}, bf16[128,2176]{1,0:T(8,128)(2,1)S(1)}, u32[]{:S(2)}, u32[]{:S(2)}) %collective-permute-start.13) | collective-permute-done | bytes 557088 | tf_op jit(solution)/shard_map/ppermute | solution.py:374
  87.3 15.6 %collective-permute-done.10.refs_0_.refs_7_ = bf16[128,2048]{1,0:T(8,128)(2,1)S(1)} collective-permute-done((bf16[128,2048]{1,0:T(8,128)(2,1)S(1)}, bf16[128,2048]{1,0:T(8,128)(2,1)S(1)}, u32[]{:S(2)}, u32[]{:S(2)}) %collective-permute-start.10) | collective-permute-done | bytes 524320 | tf_op jit(solution)/shard_map/ppermute | solution.py:382
  102.9 4.9 %shard_map.93.refs_0_ = bf16[128,2048]{1,0:T(8,128)(2,1)S(1)} custom-call(bf16[128,2176]{1,0:T(8,128)(2,1)S(1)} %collective-permute-done.13.rows_ref, f32[1,2048]{1,0:T(1,128)S(1)} %copy-done.8, f32[2,128,768]{2,1,0:T(8,128)S(1)} %get-tuple-element.57.refs_6_.gate_ref, f32[2,128,768]{2,1,0:T(8,128)S(1)} %get-tuple-element.58.up_ref, ...), custom_call_target="tpu_custom_call" | custom-call | flops 4831838208 | bytes 18874368 | tf_op jit(solution)/shard_map/pallas_call | solution.py:307
  107.8 0.2 shard_map.94
  108.0 6.0 %collective-permute-start.14 = (bf16[128,2048]{1,0:T(8,128)(2,1)S(1)}, bf16[128,2048]{1,0:T(8,128)(2,1)S(1)}, u32[]{:S(2)}, u32[]{:S(2)}) collective-permute-start(bf16[128,2048]{1,0:T(8,128)(2,1)S(1)} %shard_map.94), channel_id=1, source_target_pairs={{0,30},{1,31},{2,28},{3,29},{4,26},{5,27},{6,24},{7,25},{8,6},{9,7... | collective-permute-start | bytes 1572872 | tf_op jit(solution)/shard_map/ppermute | solution.py:382
  113.9 0.2 shard_map.92.refs_0_
  114.2 10.0 %collective-permute-done.14.refs_1_ = bf16[128,2048]{1,0:T(8,128)(2,1)S(1)} collective-permute-done((bf16[128,2048]{1,0:T(8,128)(2,1)S(1)}, bf16[128,2048]{1,0:T(8,128)(2,1)S(1)}, u32[]{:S(2)}, u32[]{:S(2)}) %collective-permute-start.14) | collective-permute-done | bytes 524320 | tf_op jit(solution)/shard_map/ppermute | solution.py:382
  124.1 1.5 %shard_map.95 = bf16[128,2048]{1,0:T(8,128)(2,1)} custom-call(bf16[128,2048]{1,0:T(8,128)(2,1)S(1)} %collective-permute-done.2.refs_6_.saved_ref, bf16[128,2048]{1,0:T(8,128)(2,1)S(1)} %collective-permute-done.3.refs_7_.upstream_ref, f32[128,2048]{1,0:T(8,128)S(1)} %shard_map.92.refs_0_, bf16[128,2048]{1,0:T(8,128)(2,1)S(1)} %collective-permute-done.14.refs_1_), custom_call_target="tpu_custom_call" | custom-call | tf_op jit(solution)/shard_map/pallas_call | solution.py:336
  (22 shorter events, 0.0 us)
Async XLA Ops:
  0.0 24.7 %collective-permute-start = (bf16[2048,768]{1,0:T(8,128)(2,1)}, bf16[2048,768]{1,0:T(8,128)(2,1)S(1)}, u32[]{:S(2)}, u32[]{:S(2)}) collective-permute-start(bf16[2048,768]{1,0:T(8,128)(2,1)} %bitcast.12), channel_id=1, source_target_pairs={{0,1},{1,0},{2,3},{3,2},{4,5},{5,4},{6,7},{7,6},{8,9},{9,8},{10,11... | collective-permute-start | bytes 9437192 | tf_op jit(solution)/shard_map/ppermute | solution.py:374
  0.5 24.7 %collective-permute-start.1 = (bf16[2048,768]{1,0:T(8,128)(2,1)}, bf16[2048,768]{1,0:T(8,128)(2,1)S(1)}, u32[]{:S(2)}, u32[]{:S(2)}) collective-permute-start(bf16[2048,768]{1,0:T(8,128)(2,1)} %bitcast.18), channel_id=1, source_target_pairs={{0,1},{1,0},{2,3},{3,2},{4,5},{5,4},{6,7},{7,6},{8,9},{9,8},{10,11... | collective-permute-start | bytes 9437192 | tf_op jit(solution)/shard_map/ppermute | solution.py:374
  0.5 26.5 %collective-permute-start.7 = (bf16[768,2048]{1,0:T(8,128)(2,1)}, bf16[768,2048]{1,0:T(8,128)(2,1)S(1)}, u32[]{:S(2)}, u32[]{:S(2)}) collective-permute-start(bf16[768,2048]{1,0:T(8,128)(2,1)} %bitcast.24), channel_id=1, source_target_pairs={{0,1},{1,0},{2,3},{3,2},{4,5},{5,4},{6,7},{7,6},{8,9},{9,8},{10,11... | collective-permute-start | bytes 9437192 | tf_op jit(solution)/shard_map/ppermute | solution.py:374
  1.0 34.3 %collective-permute-start.6 = (bf16[128,2048]{1,0:T(8,128)(2,1)}, bf16[128,2048]{1,0:T(8,128)(2,1)S(1)}, u32[]{:S(2)}, u32[]{:S(2)}) collective-permute-start(bf16[128,2048]{1,0:T(8,128)(2,1)} %bitcast.26), channel_id=1, source_target_pairs={{0,4},{1,5},{2,6},{3,7},{4,0},{5,1},{6,2},{7,3},{8,12},{9,13},{10,... | collective-permute-start | bytes 1572872 | tf_op jit(solution)/shard_map/ppermute | solution.py:374
  4.6 33.9 %collective-permute-start.5 = (bf16[128,2048]{1,0:T(8,128)(2,1)}, bf16[128,2048]{1,0:T(8,128)(2,1)S(1)}, u32[]{:S(2)}, u32[]{:S(2)}) collective-permute-start(bf16[128,2048]{1,0:T(8,128)(2,1)} %bitcast.27), channel_id=1, source_target_pairs={{0,2},{1,3},{2,0},{3,1},{4,6},{5,7},{6,4},{7,5},{8,10},{9,11},{10,... | collective-permute-start | bytes 1572872 | tf_op jit(solution)/shard_map/ppermute | solution.py:374
  6.1 1.0 copy-start.9
  7.2 0.7 copy-start.11
  7.9 0.7 copy-start.12
  8.9 1.9 %copy-start = (bf16[1,1,2048,768]{3,2,1,0:T(8,128)(2,1)S(1)}, bf16[1,1,2048,768]{3,2,1,0:T(8,128)(2,1)}, u32[]{:S(2)}) copy-start(bf16[1,1,2048,768]{3,2,1,0:T(8,128)(2,1)} %param.11) | copy-start | bytes 9437188
  10.8 1.9 %copy-start.2 = (bf16[1,1,2048,768]{3,2,1,0:T(8,128)(2,1)S(1)}, bf16[1,1,2048,768]{3,2,1,0:T(8,128)(2,1)}, u32[]{:S(2)}) copy-start(bf16[1,1,2048,768]{3,2,1,0:T(8,128)(2,1)} %param.12) | copy-start | bytes 9437188
  12.7 1.0 copy-start.5
  13.7 0.7 copy-start.7
  14.4 1.9 %copy-start.1 = (bf16[1,1,2048,768]{3,2,1,0:T(8,128)(2,1)S(1)}, bf16[1,1,2048,768]{3,2,1,0:T(8,128)(2,1)}, u32[]{:S(2)}) copy-start(bf16[1,1,2048,768]{3,2,1,0:T(8,128)(2,1)} %param.11) | copy-start | bytes 9437188
  14.4 2.8 %copy-start.3 = (bf16[1,1,2048,768]{3,2,1,0:T(8,128)(2,1)S(1)}, bf16[1,1,2048,768]{3,2,1,0:T(8,128)(2,1)}, u32[]{:S(2)}) copy-start(bf16[1,1,2048,768]{3,2,1,0:T(8,128)(2,1)} %param.12) | copy-start | bytes 9437188
  14.4 2.8 %copy-start.8 = (f32[1,2048]{1,0:T(1,128)S(1)}, f32[1,2048]{1,0:T(1,128)}, u32[]{:S(2)}) copy-start(f32[1,2048]{1,0:T(1,128)} %gain_ref.19) | copy-start | bytes 24580
  17.2 1.9 %copy-start.4 = (bf16[1,1,768,2048]{3,2,1,0:T(8,128)(2,1)S(1)}, bf16[1,1,768,2048]{3,2,1,0:T(8,128)(2,1)}, u32[]{:S(2)}) copy-start(bf16[1,1,768,2048]{3,2,1,0:T(8,128)(2,1)} %param.13) | copy-start | bytes 9437188
  19.1 6.2 %copy-start.6 = (bf16[1,128,2048]{2,1,0:T(8,128)(2,1)S(1)}, bf16[1,128,2048]{2,1,0:T(8,128)(2,1)}, u32[]{:S(2)}) copy-start(bf16[1,128,2048]{2,1,0:T(8,128)(2,1)} %param.8) | copy-start | bytes 1572868
  24.7 27.9 %collective-permute-start.4 = (bf16[128,2176]{1,0:T(8,128)(2,1)S(1)}, bf16[128,2176]{1,0:T(8,128)(2,1)S(1)}, u32[]{:S(2)}, u32[]{:S(2)}) collective-permute-start(bf16[128,2176]{1,0:T(8,128)(2,1)S(1)} %shard_map.82.rows_ref), channel_id=1, source_target_pairs={{0,4},{1,5},{2,6},{3,7},{4,0},{5,1},{6,2},{7,3},{8,12},{9,13},{10,... | collective-permute-start | bytes 1671176 | tf_op jit(solution)/shard_map/ppermute | solution.py:374
  25.1 45.8 %collective-permute-start.11 = (bf16[128,2176]{1,0:T(8,128)(2,1)S(1)}, bf16[128,2176]{1,0:T(8,128)(2,1)S(1)}, u32[]{:S(2)}, u32[]{:S(2)}) collective-permute-start(bf16[128,2176]{1,0:T(8,128)(2,1)S(1)} %shard_map.82.rows_ref), channel_id=1, source_target_pairs={{0,2},{1,3},{2,0},{3,1},{4,6},{5,7},{6,4},{7,5},{8,10},{9,11},{10,... | collective-permute-start | bytes 1671176 | tf_op jit(solution)/shard_map/ppermute | solution.py:374
  27.0 26.3 %collective-permute-start.2 = (bf16[128,2048]{1,0:T(8,128)(2,1)S(1)}, bf16[128,2048]{1,0:T(8,128)(2,1)S(1)}, u32[]{:S(2)}, u32[]{:S(2)}) collective-permute-start(bf16[128,2048]{1,0:T(8,128)(2,1)S(1)} %bitcast.30), channel_id=1, source_target_pairs={{0,24},{1,25},{2,26},{3,27},{4,28},{5,29},{6,30},{7,31},{8,0},{9,1... | collective-permute-start | bytes 1572872 | tf_op jit(solution)/shard_map/ppermute | solution.py:382
  29.7 5.6 %copy-start.10 = (bf16[1,128,2048]{2,1,0:T(8,128)(2,1)S(1)}, bf16[1,128,2048]{2,1,0:T(8,128)(2,1)}, u32[]{:S(2)}) copy-start(bf16[1,128,2048]{2,1,0:T(8,128)(2,1)} %param.9) | copy-start | bytes 1572868
  35.3 18.0 %collective-permute-start.3 = (bf16[128,2048]{1,0:T(8,128)(2,1)S(1)}, bf16[128,2048]{1,0:T(8,128)(2,1)S(1)}, u32[]{:S(2)}, u32[]{:S(2)}) collective-permute-start(bf16[128,2048]{1,0:T(8,128)(2,1)S(1)} %bitcast.32), channel_id=1, source_target_pairs={{0,24},{1,25},{2,26},{3,27},{4,28},{5,29},{6,30},{7,31},{8,0},{9,1... | collective-permute-start | bytes 1572872 | tf_op jit(solution)/shard_map/ppermute | solution.py:382
  38.4 25.7 %collective-permute-start.9 = (bf16[128,2048]{1,0:T(8,128)(2,1)S(1)}, bf16[128,2048]{1,0:T(8,128)(2,1)S(1)}, u32[]{:S(2)}, u32[]{:S(2)}) collective-permute-start(bf16[128,2048]{1,0:T(8,128)(2,1)S(1)} %collective-permute-done.6.saved_ref), channel_id=1, source_target_pairs={{0,2},{1,3},{2,0},{3,1},{4,6},{5,7},{6,4},{7,5},{8,10},{9,11},{10,... | collective-permute-start | bytes 1572872 | tf_op jit(solution)/shard_map/ppermute | solution.py:374
  52.6 34.7 %collective-permute-start.13 = (bf16[128,2176]{1,0:T(8,128)(2,1)S(1)}, bf16[128,2176]{1,0:T(8,128)(2,1)S(1)}, u32[]{:S(2)}, u32[]{:S(2)}) collective-permute-start(bf16[128,2176]{1,0:T(8,128)(2,1)S(1)} %collective-permute-done.4.rows_ref), channel_id=1, source_target_pairs={{0,2},{1,3},{2,0},{3,1},{4,6},{5,7},{6,4},{7,5},{8,10},{9,11},{10,... | collective-permute-start | bytes 1671176 | tf_op jit(solution)/shard_map/ppermute | solution.py:374
  66.6 36.2 %collective-permute-start.10 = (bf16[128,2048]{1,0:T(8,128)(2,1)S(1)}, bf16[128,2048]{1,0:T(8,128)(2,1)S(1)}, u32[]{:S(2)}, u32[]{:S(2)}) collective-permute-start(bf16[128,2048]{1,0:T(8,128)(2,1)S(1)} %get-tuple-element.53.refs_4_), channel_id=1, source_target_pairs={{0,24},{1,25},{2,26},{3,27},{4,28},{5,29},{6,30},{7,31},{8,0},{9,1... | collective-permute-start | bytes 1572872 | tf_op jit(solution)/shard_map/ppermute | solution.py:382
  69.2 38.6 %collective-permute-start.8 = (bf16[128,2048]{1,0:T(8,128)(2,1)S(1)}, bf16[128,2048]{1,0:T(8,128)(2,1)S(1)}, u32[]{:S(2)}, u32[]{:S(2)}) collective-permute-start(bf16[128,2048]{1,0:T(8,128)(2,1)S(1)} %shard_map.89.refs_4_), channel_id=1, source_target_pairs={{0,2},{1,3},{2,30},{3,31},{4,24},{5,25},{6,4},{7,5},{8,10},{9,11},... | collective-permute-start | bytes 1572872 | tf_op jit(solution)/shard_map/ppermute | solution.py:397
  75.8 38.1 %collective-permute-start.12 = (bf16[128,2048]{1,0:T(8,128)(2,1)S(1)}, bf16[128,2048]{1,0:T(8,128)(2,1)S(1)}, u32[]{:S(2)}, u32[]{:S(2)}) collective-permute-start(bf16[128,2048]{1,0:T(8,128)(2,1)S(1)} %shard_map.91.refs_6_), channel_id=1, source_target_pairs={{0,26},{1,27},{2,24},{3,25},{4,30},{5,31},{6,28},{7,29},{8,2},{9,3... | collective-permute-start | bytes 1572872 | tf_op jit(solution)/shard_map/ppermute | solution.py:382
  108.0 16.2 %collective-permute-start.14 = (bf16[128,2048]{1,0:T(8,128)(2,1)S(1)}, bf16[128,2048]{1,0:T(8,128)(2,1)S(1)}, u32[]{:S(2)}, u32[]{:S(2)}) collective-permute-start(bf16[128,2048]{1,0:T(8,128)(2,1)S(1)} %shard_map.94), channel_id=1, source_target_pairs={{0,30},{1,31},{2,28},{3,29},{4,26},{5,27},{6,24},{7,25},{8,6},{9,7... | collective-permute-start | bytes 1572872 | tf_op jit(solution)/shard_map/ppermute | solution.py:382

commit v9 on v6

--- a/solution.py
+++ b/solution.py
@@ -418,14 +418,14 @@
     x_three = hop(2)(x_two)
     two_factors = slot_factors(x_two, gain, both, [here])
     one_factors = slot_factors(x_one, gain, both, [two_factors[0]])
-    u_two, one_gate = lax.optimization_barrier((u_two, one_factors[0]))
-    one_factors = (one_gate, one_factors[1])
+    three_factors = slot_factors(x_three, gain, both, [one_factors[0]])
+    u_two, three_gate = lax.optimization_barrier((u_two, three_factors[0]))
+    three_factors = (three_gate, three_factors[1])
     here_next = handed(0)(here)
     u_three = hop(2)(u_two)
     two = slot_pieces(u_two, gain, two_factors, turned, experts, [next_saved, next_upstream])
     two_next = second_hop(two)
-    three_factors = slot_factors(x_three, gain, both, [two])
-    one = slot_pieces(u_one, gain, one_factors, turned, experts, [three_factors[0]])
+    one = slot_pieces(u_one, gain, one_factors, turned, experts, [two])
     one_next = handed(2)(one)
     three = slot_pieces(u_three, gain, three_factors, turned, experts, [one])
     three = joined(experts, 0, two_next, [three], jnp.bfloat16)

time: 121 us -> 128 us (1.058)
  waiting for transfers between devices: 36.8 us -> 55.9 us
  starting transfers between devices: 32.9 us -> 20.7 us
    ppermute x9, waiting for transfers between devices: 12.1 us -> 33.4 us  [hop(): lax.ppermute(value, 'expert', [(i, i ^ by) for i in range(experts)])]
    ppermute x5, starting transfers between devices: 23.4 us -> 7.69 us  [handed(): return lambda value: lax.ppermute(value, ('section', 'expert'), pairs)]
    ppermute x9, starting transfers between devices: 7.43 us -> 11.4 us  [hop(): lax.ppermute(value, 'expert', [(i, i ^ by) for i in range(experts)])]
    ppermute x5, waiting for transfers between devices: 24.8 us -> 22.4 us  [handed(): return lambda value: lax.ppermute(value, ('section', 'expert'), pairs)]
  transfers between devices with their start and end apart: 15 -> 15, of which waited for: 4 -> 5; matrix products, arithmetic and copies ran while one was open for 0% -> 0% of each run, Pallas kernels for 31% -> 30%
where the time goes in v9:
time: 128 us; the launch traced here: 127 us
  waiting for transfers between devices  55.9 us (44%)
  Pallas kernels  38.9 us (30%)
  starting transfers between devices  20.7 us (16%)
  local copies, waits for them, and re-layouts  11 us (9%)
    ppermute x9, waiting for transfers between devices, hop(): lax.ppermute(value, 'expert', [(i, i ^ by) for i in range(experts)])  33.4 us
    ppermute x5, waiting for transfers between devices, handed(): return lambda value: lax.ppermute(value, ('section', 'expert'), pairs)  22.4 us
    pallas_call x3, Pallas kernels, slot_pieces(): pl.pallas_call(functools.partial(pieces_kernel, experts, pairs), in_specs...  14.8 us
    ppermute x9, starting transfers between devices, hop(): lax.ppermute(value, 'expert', [(i, i ^ by) for i in range(experts)])  11.4 us
    pallas_call x2, Pallas kernels, turning_pieces(): pl.pallas_call(functools.partial(turning_kernel, experts, len(start), fli...  11.1 us
    unnamed x26, local copies, waits for them, and re-layouts  11 us
    pallas_call x5, Pallas kernels, slot_factors(): pl.pallas_call(functools.partial(factors_kernel, pairs), in_specs=[in_vme...  10.8 us
    ppermute x5, starting transfers between devices, handed(): return lambda value: lax.ppermute(value, ('section', 'expert'), pairs)  7.69 us
  transfers between devices with their start and end apart: 15, of which 5 were waited for; matrix products, arithmetic and copies ran while one was open for 0% of the time, Pallas kernels for 30%

profile of v9, /device:TPU:8, one launch (start us, length us, event | category | flops | bytes accessed | tf_op | source)
XLA Modules:
  0.0 126.6 jit_solution(5539031706126322371)
XLA Ops:
  0.0 0.5 collective-permute-start.1
  0.5 0.0 collective-permute-start.8
  0.5 2.6 %collective-permute-start.5 = (bf16[128,2048]{1,0:T(8,128)(2,1)}, bf16[128,2048]{1,0:T(8,128)(2,1)S(1)}, u32[]{:S(2)}, u32[]{:S(2)}) collective-permute-start(bf16[128,2048]{1,0:T(8,128)(2,1)} %bitcast.26), channel_id=1, source_target_pairs={{0,4},{1,5},{2,6},{3,7},{4,0},{5,1},{6,2},{7,3},{8,12},{9,13},{10,... | collective-permute-start | bytes 1572872 | tf_op jit(solution)/shard_map/ppermute | solution.py:374
  3.1 0.4 collective-permute-start.7
  3.6 1.0 copy-done.9
  4.6 0.7 copy-done.11
  5.3 0.7 copy-done.12
  6.0 0.3 shard_map.82.rows_ref
  6.3 0.0 copy-start
  6.3 1.9 %copy-done = bf16[1,1,2048,768]{3,2,1,0:T(8,128)(2,1)S(1)} copy-done((bf16[1,1,2048,768]{3,2,1,0:T(8,128)(2,1)S(1)}, bf16[1,1,2048,768]{3,2,1,0:T(8,128)(2,1)}, u32[]{:S(2)}) %copy-start) | copy-done | bytes 3145752
  8.2 1.9 %copy-done.2 = bf16[1,1,2048,768]{3,2,1,0:T(8,128)(2,1)S(1)} copy-done((bf16[1,1,2048,768]{3,2,1,0:T(8,128)(2,1)S(1)}, bf16[1,1,2048,768]{3,2,1,0:T(8,128)(2,1)}, u32[]{:S(2)}) %copy-start.2) | copy-done | bytes 3145752
  10.1 1.0 copy-done.5
  11.1 0.7 copy-done.7
  11.8 1.6 %shard_map.83 = (f32[1,128,768]{2,1,0:T(8,128)S(1)}, f32[1,128,768]{2,1,0:T(8,128)S(1)}) custom-call(bf16[128,2048]{1,0:T(8,128)(2,1)S(1)} %bitcast.28, f32[1,2048]{1,0:T(1,128)S(1)} %copy-done.7, bf16[2048,768]{1,0:T(8,128)(2,1)S(1)} %bitcast.13, bf16[2048,768]{1,0:T(8,128)(2,1)S(1)} %bitcast.19), custom_call_target="tpu_custom_call" | custom-call | flops 1610612736 | bytes 6291456 | tf_op jit(solution)/shard_map/pallas_call | solution.py:187
  13.5 0.2 copy-done.1
  13.7 1.0 copy-done.3
  14.7 1.9 %copy-done.4 = bf16[1,1,768,2048]{3,2,1,0:T(8,128)(2,1)S(1)} copy-done((bf16[1,1,768,2048]{3,2,1,0:T(8,128)(2,1)S(1)}, bf16[1,1,768,2048]{3,2,1,0:T(8,128)(2,1)}, u32[]{:S(2)}) %copy-start.4) | copy-done | bytes 3145752
  16.6 5.5 %shard_map.85 = (f32[128,2048]{1,0:T(8,128)S(1)}, bf16[768,2048]{1,0:T(8,128)(2,1)S(1)}, bf16[768,2048]{1,0:T(8,128)(2,1)S(1)}, bf16[2048,768]{1,0:T(8,128)(2,1)S(1)}) custom-call(bf16[128,2176]{1,0:T(8,128)(2,1)S(1)} %shard_map.82.rows_ref, f32[1,2048]{1,0:T(1,128)S(1)} %copy-done.8, f32[1,128,768]{2,1,0:T(8,128)S(1)} %get-tuple-element.31.refs_2_.gate_ref, ...), custom_call_target="tpu_custom_call" | custom-call | flops 2415919104 | bytes 9437184 | tf_op jit(solution)/shard_map/pallas_call | solution.py:253
  22.1 4.3 %collective-permute-done.5.saved_ref = bf16[128,2048]{1,0:T(8,128)(2,1)S(1)} collective-permute-done((bf16[128,2048]{1,0:T(8,128)(2,1)}, bf16[128,2048]{1,0:T(8,128)(2,1)S(1)}, u32[]{:S(2)}, u32[]{:S(2)}) %collective-permute-start.5) | collective-permute-done | bytes 524320 | tf_op jit(solution)/shard_map/ppermute | solution.py:374
  26.4 3.3 %collective-permute-start.4 = (bf16[128,2176]{1,0:T(8,128)(2,1)S(1)}, bf16[128,2176]{1,0:T(8,128)(2,1)S(1)}, u32[]{:S(2)}, u32[]{:S(2)}) collective-permute-start(bf16[128,2176]{1,0:T(8,128)(2,1)S(1)} %shard_map.82.rows_ref), channel_id=1, source_target_pairs={{0,4},{1,5},{2,6},{3,7},{4,0},{5,1},{6,2},{7,3},{8,12},{9,13},{10,... | collective-permute-start | bytes 1671176 | tf_op jit(solution)/shard_map/ppermute | solution.py:374
  29.7 0.0 collective-permute-start.11
  29.7 0.0 collective-permute-done.1.refs_1_.refs_3_
  29.7 2.0 %collective-permute-start.6 = (bf16[128,2048]{1,0:T(8,128)(2,1)S(1)}, bf16[128,2048]{1,0:T(8,128)(2,1)S(1)}, u32[]{:S(2)}, u32[]{:S(2)}) collective-permute-start(bf16[128,2048]{1,0:T(8,128)(2,1)S(1)} %collective-permute-done.5.saved_ref), channel_id=1, source_target_pairs={{0,2},{1,3},{2,0},{3,1},{4,6},{5,7},{6,4},{7,5},{8,10},{9,11},{10,... | collective-permute-start | bytes 1572872 | tf_op jit(solution)/shard_map/ppermute | solution.py:374
  31.7 1.6 %shard_map.84 = (f32[1,128,768]{2,1,0:T(8,128)S(1)}, f32[1,128,768]{2,1,0:T(8,128)S(1)}) custom-call(bf16[128,2048]{1,0:T(8,128)(2,1)S(1)} %bitcast.29, f32[1,2048]{1,0:T(1,128)S(1)} %copy-done.8, bf16[2048,768]{1,0:T(8,128)(2,1)S(1)} %collective-permute-done.refs_0_.refs_2_, bf16[2048,768]{1,0:T(8,128)(2,1)S(1)} %collective-permute-done.1.refs_1_.refs_3_, ...), custom_call_target="tpu_custom_call" | custom-call | flops 1610612736 | bytes 6291456 | tf_op jit(solution)/shard_map/pallas_call | solution.py:187
  33.4 0.0 collective-permute-done.8.refs_2_
  33.4 2.5 %collective-permute-start.2 = (bf16[128,2048]{1,0:T(8,128)(2,1)S(1)}, bf16[128,2048]{1,0:T(8,128)(2,1)S(1)}, u32[]{:S(2)}, u32[]{:S(2)}) collective-permute-start(bf16[128,2048]{1,0:T(8,128)(2,1)S(1)} %bitcast.30), channel_id=1, source_target_pairs={{0,24},{1,25},{2,26},{3,27},{4,28},{5,29},{6,30},{7,31},{8,0},{9,1... | collective-permute-start | bytes 1572872 | tf_op jit(solution)/shard_map/ppermute | solution.py:382
  35.9 5.6 %shard_map.86 = (bf16[128,2048]{1,0:T(8,128)(2,1)S(1)}, bf16[768,2048]{1,0:T(8,128)(2,1)S(1)}, bf16[768,2048]{1,0:T(8,128)(2,1)S(1)}, bf16[2048,768]{1,0:T(8,128)(2,1)S(1)}) custom-call(bf16[128,2176]{1,0:T(8,128)(2,1)S(1)} %shard_map.82.rows_ref, f32[1,2048]{1,0:T(1,128)S(1)} %copy-done.8, f32[1,128,768]{2,1,0:T(8,128)S(1)} %get-tuple-element.35.gate_ref, ...), custom_call_target="tpu_custom_call" | custom-call | flops 2415919104 | bytes 9437184 | tf_op jit(solution)/shard_map/pallas_call | solution.py:253
  41.4 0.0 copy-start.10
  41.5 2.5 %shard_map.87 = (f32[2,128,768]{2,1,0:T(8,128)S(1)}, f32[2,128,768]{2,1,0:T(8,128)S(1)}) custom-call(bf16[128,2048]{1,0:T(8,128)(2,1)S(1)} %collective-permute-done.5.saved_ref, f32[1,2048]{1,0:T(1,128)S(1)} %copy-done.8, bf16[2048,768]{1,0:T(8,128)(2,1)S(1)} %bitcast.15, bf16[2048,768]{1,0:T(8,128)(2,1)S(1)} %bitcast.21, ...), custom_call_target="tpu_custom_call" | custom-call | flops 3221225472 | bytes 12582912 | tf_op jit(solution)/shard_map/pallas_call | solution.py:187
  44.0 0.6 collective-permute-start.3
  44.6 2.5 %shard_map.88 = (f32[2,128,768]{2,1,0:T(8,128)S(1)}, f32[2,128,768]{2,1,0:T(8,128)S(1)}) custom-call(bf16[128,2048]{1,0:T(8,128)(2,1)S(1)} %collective-permute-done.7.saved_ref, f32[1,2048]{1,0:T(1,128)S(1)} %copy-done.8, bf16[2048,768]{1,0:T(8,128)(2,1)S(1)} %bitcast.16, bf16[2048,768]{1,0:T(8,128)(2,1)S(1)} %bitcast.22, ...), custom_call_target="tpu_custom_call" | custom-call | flops 3221225472 | bytes 12582912 | tf_op jit(solution)/shard_map/pallas_call | solution.py:187
  47.1 16.8 %collective-permute-done.6.saved_ref = bf16[128,2048]{1,0:T(8,128)(2,1)S(1)} collective-permute-done((bf16[128,2048]{1,0:T(8,128)(2,1)S(1)}, bf16[128,2048]{1,0:T(8,128)(2,1)S(1)}, u32[]{:S(2)}, u32[]{:S(2)}) %collective-permute-start.6) | collective-permute-done | bytes 524320 | tf_op jit(solution)/shard_map/ppermute | solution.py:374
  63.9 2.3 %collective-permute-start.10 = (bf16[128,2048]{1,0:T(8,128)(2,1)S(1)}, bf16[128,2048]{1,0:T(8,128)(2,1)S(1)}, u32[]{:S(2)}, u32[]{:S(2)}) collective-permute-start(bf16[128,2048]{1,0:T(8,128)(2,1)S(1)} %get-tuple-element.39.refs_4_), channel_id=1, source_target_pairs={{0,24},{1,25},{2,26},{3,27},{4,28},{5,29},{6,30},{7,31},{8,0},{9,1... | collective-permute-start | bytes 1572872 | tf_op jit(solution)/shard_map/ppermute | solution.py:382
  66.2 2.5 %shard_map.89 = (f32[2,128,768]{2,1,0:T(8,128)S(1)}, f32[2,128,768]{2,1,0:T(8,128)S(1)}) custom-call(bf16[128,2048]{1,0:T(8,128)(2,1)S(1)} %collective-permute-done.6.saved_ref, f32[1,2048]{1,0:T(1,128)S(1)} %copy-done.8, bf16[2048,768]{1,0:T(8,128)(2,1)S(1)} %bitcast.17, bf16[2048,768]{1,0:T(8,128)(2,1)S(1)} %bitcast.23, ...), custom_call_target="tpu_custom_call" | custom-call | flops 3221225472 | bytes 12582912 | tf_op jit(solution)/shard_map/pallas_call | solution.py:187
  68.7 0.0 collective-permute-done.4.rows_ref
  68.7 2.5 %collective-permute-start.13 = (bf16[128,2176]{1,0:T(8,128)(2,1)S(1)}, bf16[128,2176]{1,0:T(8,128)(2,1)S(1)}, u32[]{:S(2)}, u32[]{:S(2)}) collective-permute-start(bf16[128,2176]{1,0:T(8,128)(2,1)S(1)} %collective-permute-done.4.rows_ref), channel_id=1, source_target_pairs={{0,2},{1,3},{2,0},{3,1},{4,6},{5,7},{6,4},{7,5},{8,10},{9,11},{10,... | collective-permute-start | bytes 1671176 | tf_op jit(solution)/shard_map/ppermute | solution.py:374
  71.2 4.9 %shard_map.90.refs_6_ = bf16[128,2048]{1,0:T(8,128)(2,1)S(1)} custom-call(bf16[128,2176]{1,0:T(8,128)(2,1)S(1)} %collective-permute-done.4.rows_ref, f32[1,2048]{1,0:T(1,128)S(1)} %copy-done.8, f32[2,128,768]{2,1,0:T(8,128)S(1)} %get-tuple-element.40.refs_4_.gate_ref, f32[2,128,768]{2,1,0:T(8,128)S(1)} %get-tuple-element.44.up_ref, ...), custom_call_target="tpu_custom_call" | custom-call | flops 4831838208 | bytes 18874368 | tf_op jit(solution)/shard_map/pallas_call | solution.py:307
  76.2 1.6 %collective-permute-start.9 = (bf16[128,2048]{1,0:T(8,128)(2,1)S(1)}, bf16[128,2048]{1,0:T(8,128)(2,1)S(1)}, u32[]{:S(2)}, u32[]{:S(2)}) collective-permute-start(bf16[128,2048]{1,0:T(8,128)(2,1)S(1)} %shard_map.90.refs_6_), channel_id=1, source_target_pairs={{0,2},{1,3},{2,30},{3,31},{4,24},{5,25},{6,4},{7,5},{8,10},{9,11},... | collective-permute-start | bytes 1572872 | tf_op jit(solution)/shard_map/ppermute | solution.py:397
  77.8 4.9 %shard_map.91.refs_6_ = bf16[128,2048]{1,0:T(8,128)(2,1)S(1)} custom-call(bf16[128,2176]{1,0:T(8,128)(2,1)S(1)} %collective-permute-done.11.rows_ref, f32[1,2048]{1,0:T(1,128)S(1)} %copy-done.8, f32[2,128,768]{2,1,0:T(8,128)S(1)} %get-tuple-element.41.refs_4_.gate_ref, f32[2,128,768]{2,1,0:T(8,128)S(1)} %get-tuple-element.52.up_ref, ...), custom_call_target="tpu_custom_call" | custom-call | flops 4831838208 | bytes 18874368 | tf_op jit(solution)/shard_map/pallas_call | solution.py:307
  82.7 0.4 collective-permute-start.12
  83.2 12.4 %collective-permute-done.13.rows_ref = bf16[128,2176]{1,0:T(8,128)(2,1)S(1)} collective-permute-done((bf16[128,2176]{1,0:T(8,128)(2,1)S(1)}, bf16[128,2176]{1,0:T(8,128)(2,1)S(1)}, u32[]{:S(2)}, u32[]{:S(2)}) %collective-permute-start.13) | collective-permute-done | bytes 557088 | tf_op jit(solution)/shard_map/ppermute | solution.py:374
  95.6 4.9 %shard_map.93.refs_0_ = bf16[128,2048]{1,0:T(8,128)(2,1)S(1)} custom-call(bf16[128,2176]{1,0:T(8,128)(2,1)S(1)} %collective-permute-done.13.rows_ref, f32[1,2048]{1,0:T(1,128)S(1)} %copy-done.8, f32[2,128,768]{2,1,0:T(8,128)S(1)} %get-tuple-element.53.gate_ref, f32[2,128,768]{2,1,0:T(8,128)S(1)} %get-tuple-element.54.up_ref, ...), custom_call_target="tpu_custom_call" | custom-call | flops 4831838208 | bytes 18874368 | tf_op jit(solution)/shard_map/pallas_call | solution.py:307
  100.5 0.2 shard_map.94
  100.6 1.9 %collective-permute-start.14 = (bf16[128,2048]{1,0:T(8,128)(2,1)S(1)}, bf16[128,2048]{1,0:T(8,128)(2,1)S(1)}, u32[]{:S(2)}, u32[]{:S(2)}) collective-permute-start(bf16[128,2048]{1,0:T(8,128)(2,1)S(1)} %shard_map.94), channel_id=1, source_target_pairs={{0,30},{1,31},{2,28},{3,29},{4,26},{5,27},{6,24},{7,25},{8,6},{9,7... | collective-permute-start | bytes 1572872 | tf_op jit(solution)/shard_map/ppermute | solution.py:382
  102.5 6.6 %collective-permute-done.12.refs_1_ = bf16[128,2048]{1,0:T(8,128)(2,1)S(1)} collective-permute-done((bf16[128,2048]{1,0:T(8,128)(2,1)S(1)}, bf16[128,2048]{1,0:T(8,128)(2,1)S(1)}, u32[]{:S(2)}, u32[]{:S(2)}) %collective-permute-start.12) | collective-permute-done | bytes 524320 | tf_op jit(solution)/shard_map/ppermute | solution.py:382
  109.1 0.2 shard_map.92.refs_0_
  109.3 15.8 %collective-permute-done.14.refs_1_ = bf16[128,2048]{1,0:T(8,128)(2,1)S(1)} collective-permute-done((bf16[128,2048]{1,0:T(8,128)(2,1)S(1)}, bf16[128,2048]{1,0:T(8,128)(2,1)S(1)}, u32[]{:S(2)}, u32[]{:S(2)}) %collective-permute-start.14) | collective-permute-done | bytes 524320 | tf_op jit(solution)/shard_map/ppermute | solution.py:382
  125.1 1.5 %shard_map.95 = bf16[128,2048]{1,0:T(8,128)(2,1)} custom-call(bf16[128,2048]{1,0:T(8,128)(2,1)S(1)} %collective-permute-done.2.refs_6_.saved_ref, bf16[128,2048]{1,0:T(8,128)(2,1)S(1)} %collective-permute-done.3.refs_7_.upstream_ref, f32[128,2048]{1,0:T(8,128)S(1)} %shard_map.92.refs_0_, bf16[128,2048]{1,0:T(8,128)(2,1)S(1)} %collective-permute-done.14.refs_1_), custom_call_target="tpu_custom_call" | custom-call | tf_op jit(solution)/shard_map/pallas_call | solution.py:336
  (22 shorter events, 0.0 us)
Async XLA Ops:
  0.0 29.7 %collective-permute-start = (bf16[2048,768]{1,0:T(8,128)(2,1)}, bf16[2048,768]{1,0:T(8,128)(2,1)S(1)}, u32[]{:S(2)}, u32[]{:S(2)}) collective-permute-start(bf16[2048,768]{1,0:T(8,128)(2,1)} %bitcast.12), channel_id=1, source_target_pairs={{0,1},{1,0},{2,3},{3,2},{4,5},{5,4},{6,7},{7,6},{8,9},{9,8},{10,11... | collective-permute-start | bytes 9437192 | tf_op jit(solution)/shard_map/ppermute | solution.py:374
  0.0 29.7 %collective-permute-start.1 = (bf16[2048,768]{1,0:T(8,128)(2,1)}, bf16[2048,768]{1,0:T(8,128)(2,1)S(1)}, u32[]{:S(2)}, u32[]{:S(2)}) collective-permute-start(bf16[2048,768]{1,0:T(8,128)(2,1)} %bitcast.18), channel_id=1, source_target_pairs={{0,1},{1,0},{2,3},{3,2},{4,5},{5,4},{6,7},{7,6},{8,9},{9,8},{10,11... | collective-permute-start | bytes 9437192 | tf_op jit(solution)/shard_map/ppermute | solution.py:374
  0.5 32.8 %collective-permute-start.8 = (bf16[768,2048]{1,0:T(8,128)(2,1)}, bf16[768,2048]{1,0:T(8,128)(2,1)S(1)}, u32[]{:S(2)}, u32[]{:S(2)}) collective-permute-start(bf16[768,2048]{1,0:T(8,128)(2,1)} %bitcast.24), channel_id=1, source_target_pairs={{0,1},{1,0},{2,3},{3,2},{4,5},{5,4},{6,7},{7,6},{8,9},{9,8},{10,11... | collective-permute-start | bytes 9437192 | tf_op jit(solution)/shard_map/ppermute | solution.py:374
  0.5 25.9 %collective-permute-start.5 = (bf16[128,2048]{1,0:T(8,128)(2,1)}, bf16[128,2048]{1,0:T(8,128)(2,1)S(1)}, u32[]{:S(2)}, u32[]{:S(2)}) collective-permute-start(bf16[128,2048]{1,0:T(8,128)(2,1)} %bitcast.26), channel_id=1, source_target_pairs={{0,4},{1,5},{2,6},{3,7},{4,0},{5,1},{6,2},{7,3},{8,12},{9,13},{10,... | collective-permute-start | bytes 1572872 | tf_op jit(solution)/shard_map/ppermute | solution.py:374
  3.1 40.9 %collective-permute-start.7 = (bf16[128,2048]{1,0:T(8,128)(2,1)}, bf16[128,2048]{1,0:T(8,128)(2,1)S(1)}, u32[]{:S(2)}, u32[]{:S(2)}) collective-permute-start(bf16[128,2048]{1,0:T(8,128)(2,1)} %bitcast.27), channel_id=1, source_target_pairs={{0,2},{1,3},{2,0},{3,1},{4,6},{5,7},{6,4},{7,5},{8,10},{9,11},{10,... | collective-permute-start | bytes 1572872 | tf_op jit(solution)/shard_map/ppermute | solution.py:374
  3.6 1.0 copy-start.9
  4.6 0.7 copy-start.11
  5.3 0.7 copy-start.12
  6.3 1.9 %copy-start = (bf16[1,1,2048,768]{3,2,1,0:T(8,128)(2,1)S(1)}, bf16[1,1,2048,768]{3,2,1,0:T(8,128)(2,1)}, u32[]{:S(2)}) copy-start(bf16[1,1,2048,768]{3,2,1,0:T(8,128)(2,1)} %param.11) | copy-start | bytes 9437188
  8.2 1.9 %copy-start.2 = (bf16[1,1,2048,768]{3,2,1,0:T(8,128)(2,1)S(1)}, bf16[1,1,2048,768]{3,2,1,0:T(8,128)(2,1)}, u32[]{:S(2)}) copy-start(bf16[1,1,2048,768]{3,2,1,0:T(8,128)(2,1)} %param.12) | copy-start | bytes 9437188
  10.1 1.0 copy-start.5
  11.1 0.7 copy-start.7
  11.8 1.9 %copy-start.1 = (bf16[1,1,2048,768]{3,2,1,0:T(8,128)(2,1)S(1)}, bf16[1,1,2048,768]{3,2,1,0:T(8,128)(2,1)}, u32[]{:S(2)}) copy-start(bf16[1,1,2048,768]{3,2,1,0:T(8,128)(2,1)} %param.11) | copy-start | bytes 9437188
  11.8 2.8 %copy-start.3 = (bf16[1,1,2048,768]{3,2,1,0:T(8,128)(2,1)S(1)}, bf16[1,1,2048,768]{3,2,1,0:T(8,128)(2,1)}, u32[]{:S(2)}) copy-start(bf16[1,1,2048,768]{3,2,1,0:T(8,128)(2,1)} %param.12) | copy-start | bytes 9437188
  11.8 2.8 %copy-start.8 = (f32[1,2048]{1,0:T(1,128)S(1)}, f32[1,2048]{1,0:T(1,128)}, u32[]{:S(2)}) copy-start(f32[1,2048]{1,0:T(1,128)} %gain_ref.19) | copy-start | bytes 24580
  14.7 1.9 %copy-start.4 = (bf16[1,1,768,2048]{3,2,1,0:T(8,128)(2,1)S(1)}, bf16[1,1,768,2048]{3,2,1,0:T(8,128)(2,1)}, u32[]{:S(2)}) copy-start(bf16[1,1,768,2048]{3,2,1,0:T(8,128)(2,1)} %param.13) | copy-start | bytes 9437188
  16.6 15.1 %copy-start.6 = (bf16[1,128,2048]{2,1,0:T(8,128)(2,1)S(1)}, bf16[1,128,2048]{2,1,0:T(8,128)(2,1)}, u32[]{:S(2)}) copy-start(bf16[1,128,2048]{2,1,0:T(8,128)(2,1)} %param.8) | copy-start | bytes 1572868
  26.4 42.3 %collective-permute-start.4 = (bf16[128,2176]{1,0:T(8,128)(2,1)S(1)}, bf16[128,2176]{1,0:T(8,128)(2,1)S(1)}, u32[]{:S(2)}, u32[]{:S(2)}) collective-permute-start(bf16[128,2176]{1,0:T(8,128)(2,1)S(1)} %shard_map.82.rows_ref), channel_id=1, source_target_pairs={{0,4},{1,5},{2,6},{3,7},{4,0},{5,1},{6,2},{7,3},{8,12},{9,13},{10,... | collective-permute-start | bytes 1671176 | tf_op jit(solution)/shard_map/ppermute | solution.py:374
  29.7 48.1 %collective-permute-start.11 = (bf16[128,2176]{1,0:T(8,128)(2,1)S(1)}, bf16[128,2176]{1,0:T(8,128)(2,1)S(1)}, u32[]{:S(2)}, u32[]{:S(2)}) collective-permute-start(bf16[128,2176]{1,0:T(8,128)(2,1)S(1)} %shard_map.82.rows_ref), channel_id=1, source_target_pairs={{0,2},{1,3},{2,0},{3,1},{4,6},{5,7},{6,4},{7,5},{8,10},{9,11},{10,... | collective-permute-start | bytes 1671176 | tf_op jit(solution)/shard_map/ppermute | solution.py:374
  29.7 34.2 %collective-permute-start.6 = (bf16[128,2048]{1,0:T(8,128)(2,1)S(1)}, bf16[128,2048]{1,0:T(8,128)(2,1)S(1)}, u32[]{:S(2)}, u32[]{:S(2)}) collective-permute-start(bf16[128,2048]{1,0:T(8,128)(2,1)S(1)} %collective-permute-done.5.saved_ref), channel_id=1, source_target_pairs={{0,2},{1,3},{2,0},{3,1},{4,6},{5,7},{6,4},{7,5},{8,10},{9,11},{10,... | collective-permute-start | bytes 1572872 | tf_op jit(solution)/shard_map/ppermute | solution.py:374
  33.4 37.9 %collective-permute-start.2 = (bf16[128,2048]{1,0:T(8,128)(2,1)S(1)}, bf16[128,2048]{1,0:T(8,128)(2,1)S(1)}, u32[]{:S(2)}, u32[]{:S(2)}) collective-permute-start(bf16[128,2048]{1,0:T(8,128)(2,1)S(1)} %bitcast.30), channel_id=1, source_target_pairs={{0,24},{1,25},{2,26},{3,27},{4,28},{5,29},{6,30},{7,31},{8,0},{9,1... | collective-permute-start | bytes 1572872 | tf_op jit(solution)/shard_map/ppermute | solution.py:382
  41.4 2.5 %copy-start.10 = (bf16[1,128,2048]{2,1,0:T(8,128)(2,1)S(1)}, bf16[1,128,2048]{2,1,0:T(8,128)(2,1)}, u32[]{:S(2)}) copy-start(bf16[1,128,2048]{2,1,0:T(8,128)(2,1)} %param.9) | copy-start | bytes 1572868
  44.0 27.2 %collective-permute-start.3 = (bf16[128,2048]{1,0:T(8,128)(2,1)S(1)}, bf16[128,2048]{1,0:T(8,128)(2,1)S(1)}, u32[]{:S(2)}, u32[]{:S(2)}) collective-permute-start(bf16[128,2048]{1,0:T(8,128)(2,1)S(1)} %bitcast.32), channel_id=1, source_target_pairs={{0,24},{1,25},{2,26},{3,27},{4,28},{5,29},{6,30},{7,31},{8,0},{9,1... | collective-permute-start | bytes 1572872 | tf_op jit(solution)/shard_map/ppermute | solution.py:382
  63.9 38.6 %collective-permute-start.10 = (bf16[128,2048]{1,0:T(8,128)(2,1)S(1)}, bf16[128,2048]{1,0:T(8,128)(2,1)S(1)}, u32[]{:S(2)}, u32[]{:S(2)}) collective-permute-start(bf16[128,2048]{1,0:T(8,128)(2,1)S(1)} %get-tuple-element.39.refs_4_), channel_id=1, source_target_pairs={{0,24},{1,25},{2,26},{3,27},{4,28},{5,29},{6,30},{7,31},{8,0},{9,1... | collective-permute-start | bytes 1572872 | tf_op jit(solution)/shard_map/ppermute | solution.py:382
  68.7 26.9 %collective-permute-start.13 = (bf16[128,2176]{1,0:T(8,128)(2,1)S(1)}, bf16[128,2176]{1,0:T(8,128)(2,1)S(1)}, u32[]{:S(2)}, u32[]{:S(2)}) collective-permute-start(bf16[128,2176]{1,0:T(8,128)(2,1)S(1)} %collective-permute-done.4.rows_ref), channel_id=1, source_target_pairs={{0,2},{1,3},{2,0},{3,1},{4,6},{5,7},{6,4},{7,5},{8,10},{9,11},{10,... | collective-permute-start | bytes 1671176 | tf_op jit(solution)/shard_map/ppermute | solution.py:374
  76.2 24.3 %collective-permute-start.9 = (bf16[128,2048]{1,0:T(8,128)(2,1)S(1)}, bf16[128,2048]{1,0:T(8,128)(2,1)S(1)}, u32[]{:S(2)}, u32[]{:S(2)}) collective-permute-start(bf16[128,2048]{1,0:T(8,128)(2,1)S(1)} %shard_map.90.refs_6_), channel_id=1, source_target_pairs={{0,2},{1,3},{2,30},{3,31},{4,24},{5,25},{6,4},{7,5},{8,10},{9,11},... | collective-permute-start | bytes 1572872 | tf_op jit(solution)/shard_map/ppermute | solution.py:397
  82.7 26.4 %collective-permute-start.12 = (bf16[128,2048]{1,0:T(8,128)(2,1)S(1)}, bf16[128,2048]{1,0:T(8,128)(2,1)S(1)}, u32[]{:S(2)}, u32[]{:S(2)}) collective-permute-start(bf16[128,2048]{1,0:T(8,128)(2,1)S(1)} %shard_map.91.refs_6_), channel_id=1, source_target_pairs={{0,26},{1,27},{2,24},{3,25},{4,30},{5,31},{6,28},{7,29},{8,2},{9,3... | collective-permute-start | bytes 1572872 | tf_op jit(solution)/shard_map/ppermute | solution.py:382
  100.6 24.5 %collective-permute-start.14 = (bf16[128,2048]{1,0:T(8,128)(2,1)S(1)}, bf16[128,2048]{1,0:T(8,128)(2,1)S(1)}, u32[]{:S(2)}, u32[]{:S(2)}) collective-permute-start(bf16[128,2048]{1,0:T(8,128)(2,1)S(1)} %shard_map.94), channel_id=1, source_target_pairs={{0,30},{1,31},{2,28},{3,29},{4,26},{5,27},{6,24},{7,25},{8,6},{9,7... | collective-permute-start | bytes 1572872 | tf_op jit(solution)/shard_map/ppermute | solution.py:382
